TPU v7x, 32 devices: a whole 2x2x4 slice. The times are simulated.
32 devices in a mesh: dp: 8 (over z, x), seq: 4 (over y, core).
Axes of the slice: x: 2, y: 2, z: 4, core: 2. Of those that a mesh axis runs over, the one named last changes fastest.
Arguments:
- tokens: float32 [8192, 384], P(('dp', 'seq')), may hold values from -6 to 6
- class_tokens: float32 [32, 384], P('dp'), may hold values from -6 to 6
- cot_patch: float32 [8192, 384], P(('dp', 'seq')), may hold values from -6 to 6
- cot_class: float32 [32, 384], P('dp'), may hold values from -6 to 6
- lengths: int32 [8, 4], P('dp'), may hold values from 64 to 832, as said below
- matrices: float32 [2, 3, 384, 1536], replicated, may hold values from -0.3125 to 0.3125
- matrices_moment1: float32 [2, 3, 384, 1536], P(None, None, 'dp'), may hold values from -0.00035029993 to 0.00035029993
- matrices_moment2: float32 [2, 3, 384, 1536], P(None, None, 'dp'), may hold values from 2.8170347e-10 to 1.1268139e-09
- matrices_ema: float32 [2, 3, 384, 1536], P(None, None, 'dp'), may hold values from -0.3125 to 0.3125
- vectors: float32 [28, 384], replicated, may hold values from -1 to 3
- vectors_moment1: float32 [28, 384], P(None, 'dp'), may hold values from -0.0014011997 to 0.0014011997
- vectors_moment2: float32 [28, 384], P(None, 'dp'), may hold values from 4.5072555e-09 to 1.8029022e-08
- vectors_ema: float32 [28, 384], P(None, 'dp'), may hold values from 0.5 to 1.5
- talking: float32 [8, 17], replicated, may hold values from -1 to 2
- talking_moment1: float32 [8, 17], replicated, may hold values from -0.0035029992 to 0.0035029992
- talking_moment2: float32 [8, 17], replicated, may hold values from 2.8170348e-08 to 1.1268139e-07
- talking_ema: float32 [8, 17], replicated, may hold values from -3 to 3
Outputs:
- patch_out: float32 [8192, 384], P(('dp', 'seq'))
- class_out: float32 [32, 384], P('dp')
- grad_tokens: float32 [8192, 384], P(('dp', 'seq'))
- grad_class: float32 [32, 384], P('dp')
- clip_norm: float32 [], replicated
- matrices_new: float32 [2, 3, 384, 1536], P(None, None, 'dp')
- matrices_first: float32 [2, 3, 384, 1536], P(None, None, 'dp')
- matrices_second: float32 [2, 3, 384, 1536], P(None, None, 'dp')
- matrices_average: float32 [2, 3, 384, 1536], P(None, None, 'dp')
- vectors_new: float32 [28, 384], P(None, 'dp')
- vectors_first: float32 [28, 384], P(None, 'dp')
- vectors_second: float32 [28, 384], P(None, 'dp')
- vectors_average: float32 [28, 384], P(None, 'dp')
- talking_new: float32 [8, 17], replicated
- talking_first: float32 [8, 17], replicated
- talking_second: float32 [8, 17], replicated
- talking_average: float32 [8, 17], replicated
Inputs may be any that keep to these rules, and one draw needn't show every extreme that they name: In every data group the 4 lengths sum to 1024; one image of each group, neither the first nor the last and in a drawn place, begins within the first 256 positions of the group and ends within its last 256.
All inputs are finite; a program needn't handle non-finite values.
Results may differ from a plain program's by a relative error of at most 0.0003.
Values sent between devices are 32-bit elements; how exact they have to be, the bound alone decides.
No kernel may reach another device: no remote copies, remote signals or barrier semaphores. Data moves between devices by JAX's collectives and lax.ppermute only.
A program may use at most 256 MiB of HBM per device.

v0:
```python
import functools

import jax
import jax.numpy as jnp
from jax import lax
from jax.experimental import pallas as pl
from jax.experimental.pallas import tpu as pltpu
from jax.sharding import PartitionSpec as P

STEP = 10
EPS_NORM = 1e-06
MASKED = -1e30
LR_MATRIX = 0.05
LR_VECTOR = 0.1
LR_TALKING = 0.2
BETA_ONE = 0.9
BETA_TWO = 0.999
ADAM_EPS = 1e-08
WEIGHT_DECAY = 0.05
EMA_RATE = 0.9
CLIP_NORM = 1.0
F32 = jnp.float32
BF16 = jnp.bfloat16
NN = (((1,), (0,)), ((), ()))
NT = (((1,), (1,)), ((), ()))
TN = (((0,), (0,)), ((), ()))
KERNEL_MIB = 58


def split(value):
    high = value.astype(BF16)
    return high, (value - high.astype(F32)).astype(BF16)


def mm(left, right, dims=NN):
    return lax.dot_general(left, right, dims, preferred_element_type=F32)


def mm3(left, right, dims=NN):
    return mm(left[0], right[0], dims) + (mm(left[0], right[1], dims) + mm(left[1], right[0], dims))


def dot3(left, right, dims=NN):
    return mm3(split(left), split(right), dims)


def norm_rows(values):
    average = jnp.mean(values, axis=-1, keepdims=True)
    centered = values - average
    variance = jnp.mean(centered * centered, axis=-1, keepdims=True)
    scale = lax.rsqrt(variance + EPS_NORM)
    return centered * scale, scale


def norm_back(grad, unit, scale):
    inner = jnp.mean(grad * unit, axis=-1, keepdims=True)
    return scale * (grad - jnp.mean(grad, axis=-1, keepdims=True) - unit * inner)


def gelu_both(values):
    half = 0.5 * (1.0 + lax.erf(values * 0.7071067811865476))
    slope = half + values * (0.3989422804014327 * jnp.exp(-0.5 * values * values))
    return values * half, slope


def row_sum(values):
    return jnp.sum(values, axis=0, keepdims=True)


def tail_forward(inputs, attended, w_out, w_up, w_down, vecs):
    projected = dot3(attended, w_out) + vecs[4:5]
    mixed = inputs + vecs[5:6] * projected
    unit, _ = norm_rows(mixed)
    normed = unit * vecs[6:7] + vecs[7:8]
    up_bias = jnp.concatenate([vecs[row : row + 1] for row in range(8, 12)], axis=1)
    hidden, slope = gelu_both(dot3(normed, w_up) + up_bias)
    lowered = dot3(hidden, w_down, NT) + vecs[12:13]
    return mixed + vecs[13:14] * lowered, (projected, mixed, hidden, slope, lowered)


def tail_backward(cot, kept, w_out, w_up, w_down, vecs):
    projected, mixed, hidden, slope, lowered = kept
    width = cot.shape[1]
    unit, scale = norm_rows(mixed)
    normed = unit * vecs[6:7] + vecs[7:8]
    d_lowered = cot * vecs[13:14]
    d_hidden = dot3(d_lowered, w_down) * slope
    d_normed = dot3(d_hidden, w_up, NT)
    d_mixed = cot + norm_back(d_normed * vecs[6:7], unit, scale)
    d_projected = d_mixed * vecs[5:6]
    d_attended = dot3(d_projected, w_out, NT)
    d_up = row_sum(d_hidden)
    rows = [
        row_sum(d_projected), row_sum(d_mixed * projected), row_sum(d_normed * unit), row_sum(d_normed),
        *[d_up[:, i * width : (i + 1) * width] for i in range(4)],
        row_sum(d_lowered), row_sum(cot * lowered),
    ]
    return d_mixed, d_attended, d_projected, d_hidden, d_lowered, normed, rows


def image_of(lengths_ref, images, positions):
    end = lengths_ref[0, 0]
    inside = (positions >= end).astype(jnp.int32)
    for image in range(1, images):
        end = end + lengths_ref[0, image]
        inside = inside + (positions >= end).astype(jnp.int32)
    return inside


def same_image(lengths_ref, images, place, slots, rows):
    queries = place * rows + lax.broadcasted_iota(jnp.int32, (1, rows), 1)
    query_image = image_of(lengths_ref, images, queries)
    parts = []
    for slot in range(slots):
        keys = jnp.bitwise_xor(place, slot) * rows + lax.broadcasted_iota(jnp.int32, (rows, 1), 0)
        parts.append(image_of(lengths_ref, images, keys) == query_image)
    return parts


def column_of(table, number):
    lanes = lax.broadcasted_iota(jnp.int32, (1, table.shape[1]), 1)
    return jnp.sum(jnp.where(lanes == number, table, 0.0), axis=1, keepdims=True)


def head_mask(heads, width):
    row = lax.broadcasted_iota(jnp.int32, (heads, width), 0)
    return jnp.where(lax.broadcasted_iota(jnp.int32, (heads, width), 1) // (width // heads) == row, 1.0, 0.0)


def spread(value, mask):
    return jnp.concatenate([value[i : i + 1] * mask for i in range(value.shape[0])], axis=0)


def repeat_rows(value, heads):
    shape = (heads, value.shape[1])
    return jnp.concatenate(
        [jnp.broadcast_to(value[i : i + 1], shape) for i in range(value.shape[0])], axis=0
    )


def fold_heads(value, mask):
    heads = mask.shape[0]
    return jnp.concatenate(
        [row_sum(value[i : i + heads] * mask) for i in range(0, value.shape[0], heads)], axis=0
    )


def head_sums(value, mask):
    return jnp.sum(spread(value, mask), axis=1, keepdims=True)


def rows_of(value, heads):
    return jnp.concatenate(
        [row_sum(value[i : i + heads]) for i in range(0, value.shape[0], heads)], axis=0
    )


def wide(column):
    return jnp.broadcast_to(column, (column.shape[0], 128))


def whole(shape):
    return pl.BlockSpec(shape, lambda *_: (0,) * len(shape))


def struct(shape, dtype=F32):
    return jax.ShapeDtypeStruct(shape, dtype)


def smem():
    return pl.BlockSpec(memory_space=pltpu.SMEM)


def anywhere():
    return pl.BlockSpec(memory_space=pl.ANY)


def weight_block(block, matrix, shape):
    return pl.BlockSpec((None, None) + shape[2:], lambda *_: (block, matrix, 0, 0))


def limit(mebibytes):
    return pltpu.CompilerParams(vmem_limit_bytes=mebibytes << 20)


def prepare_kernel(
    own_ref, near_ref, class_ref, w_self_ref, w_class_ref, vecs_ref, talk_ref,
    normed_ref, query_c_ref, value_c_ref, key_rows_ref, score_ref, t1_ref, t2_ref, t1_rows_ref, t2_rows_ref,
    query_ref, k_high, k_low, v_high, v_low, kt_high, kt_low, vt_high, vt_low,
):
    rows, width = own_ref.shape
    heads = talk_ref.shape[0]
    size = width // heads
    scale = size ** (-0.5)
    vecs = vecs_ref[...]
    w_q, w_k, w_v = (split(w_self_ref[:, i * width : (i + 1) * width]) for i in range(3))
    tokens = jnp.concatenate([own_ref[...], near_ref[...]], axis=0)
    unit, _ = norm_rows(tokens)
    normed = split(unit * vecs[0:1] + vecs[1:2])
    query_ref[...] = (mm3((normed[0][:rows], normed[1][:rows]), w_q) + vecs[2:3]) * scale
    keys, values = mm3(normed, w_k), mm3(normed, w_v) + vecs[3:4]
    k_high[...], k_low[...] = split(keys)
    v_high[...], v_low[...] = split(values)
    kt_high[...], kt_low[...] = split(keys.T)
    vt_high[...], vt_low[...] = split(values.T)
    mask = head_mask(heads, width)
    unit, _ = norm_rows(class_ref[...])
    normed = unit * vecs[14:15] + vecs[15:16]
    both = dot3(normed, w_class_ref[:, : 3 * width])
    query = both[:, :width] + vecs[16:17]
    normed_ref[...] = normed
    query_c_ref[...] = query
    value_c_ref[...] = both[:, 2 * width :] + vecs[17:18]
    key_rows_ref[...] = dot3(spread(query, mask), w_class_ref[:, width : 2 * width], NT) * scale
    score_ref[...] = wide(head_sums(query * both[:, width : 2 * width], mask) * scale)
    head_of = lax.broadcasted_iota(jnp.int32, (width, 1), 0) // size
    talk = talk_ref[...]
    talk_t = jnp.concatenate([talk, jnp.zeros((heads, 128 - talk.shape[1]), F32)], axis=1).T[: talk.shape[1], :]
    t1 = t2 = t1_rows = t2_rows = 0.0
    for head in range(heads):
        here = head_of == head
        t1 = t1 + jnp.where(here, talk_t[head : head + 1, :], 0.0)
        t2 = t2 + jnp.where(here, talk[head : head + 1, heads:], 0.0)
        t1_rows = t1_rows + mask[head : head + 1] * talk[:, head : head + 1]
        t2_rows = t2_rows + mask[head : head + 1] * talk_t[heads:, head : head + 1]
    t1_ref[...], t2_ref[...], t1_rows_ref[...], t2_rows_ref[...] = t1, t2, t1_rows, t2_rows


def prepare(own, near, class_tokens, matrices, vectors, talking):
    images, width = class_tokens.shape
    rows = own.shape[0]
    heads = talking.shape[0]
    pairs = images * heads
    outs = [struct((images, width))] * 3 + [
        struct((pairs, width)), struct((pairs, 128)),
        struct((width, heads)), struct((width, heads + 1)),
        struct((heads, width)), struct((heads + 1, width)),
        struct((rows, width)),
    ]
    outs += [struct((2 * rows, width), BF16)] * 4 + [struct((width, 2 * rows), BF16)] * 4
    operands = [own, near, class_tokens, matrices, matrices, vectors, talking]
    specs = [whole(operand.shape) for operand in operands]
    specs[3] = weight_block(0, 0, matrices.shape)
    specs[4] = weight_block(1, 0, matrices.shape)
    return pl.pallas_call(
        prepare_kernel,
        grid=(1,),
        in_specs=specs,
        out_specs=[whole(out.shape) for out in outs],
        out_shape=outs,
        compiler_params=limit(KERNEL_MIB),
        cost_estimate=pl.CostEstimate(flops=4 << 30, bytes_accessed=8 << 20, transcendentals=0),
        name="prepare",
    )(*operands)


def forward_kernel(slots, images, unroll, *refs):
    place_ref, lengths_ref = refs[:2]
    token_refs = refs[2 : 2 + slots]
    (
        w_ref, vecs_ref, t1_ref, t2_ref, key_rows_ref, query_ref,
        k_high0, k_low0, v_high0, v_low0, kt_high0, kt_low0, vt_high0, vt_low0, mats_ref,
        e_high_ref, e_low_ref, pv_ref, inverse_ref, pv_bias_ref, attended_ref,
        kt_high, kt_low, v_high, v_low,
        patch_ref, projected_ref, mixed_ref, hidden_ref, slope_ref, lowered_ref, packed_ref, scores_ref,
        k_high, k_low, vt_high, vt_low, qt, bias, attended_t, w_up, w_down, arrived,
    ) = refs[2 + slots :]
    rows, width = token_refs[0].shape
    step = pl.program_id(0)
    place = place_ref[0]
    fetch_up = pltpu.make_async_copy(mats_ref.at[0, 1], w_up, arrived.at[0])
    fetch_down = pltpu.make_async_copy(mats_ref.at[0, 2], w_down, arrived.at[1])

    @pl.when(step == 0)
    def _():
        fetch_up.start()
        fetch_down.start()
        ready = pl.ds(0, 2 * rows)
        for ref, found in ((k_high, k_high0), (k_low, k_low0), (v_high, v_high0), (v_low, v_low0)):
            ref[ready, :] = found[...]
        for ref, found in ((kt_high, kt_high0), (kt_low, kt_low0), (vt_high, vt_high0), (vt_low, vt_low0)):
            ref[:, ready] = found[...]
        w_k, w_v = (split(w_ref[:, i * width : (i + 1) * width]) for i in (1, 2))
        vecs = vecs_ref[...]
        inside = same_image(lengths_ref, images, place, slots, rows)
        for slot in range(slots):
            here = pl.ds(slot * rows, rows)
            bias[here, :] = jnp.where(inside[slot], 0.0, MASKED)
            if slot < 2:
                continue
            unit, _ = norm_rows(token_refs[slot][...])
            normed = split(unit * vecs[0:1] + vecs[1:2])
            keys, values = mm3(normed, w_k), mm3(normed, w_v) + vecs[3:4]
            k_high[here, :], k_low[here, :] = split(keys)
            v_high[here, :], v_low[here, :] = split(values)
            kt_high[:, here], kt_low[:, here] = split(keys.T)
            vt_high[:, here], vt_low[:, here] = split(values.T)
        qt[...] = query_ref[...].T
        attended_t[...] = jnp.zeros_like(attended_t)

    scores = []
    for u in range(unroll):
        query = split(qt[...] * column_of(t1_ref[...], step * unroll + u))
        scores.append(mm3((k_high[...], k_low[...]), query) + bias[...])
    for u in range(unroll):
        exponentials = jnp.exp(scores[u] - jnp.max(scores[u], axis=0, keepdims=True))
        inverse = 1.0 / jnp.sum(exponentials, axis=0, keepdims=True)
        pair = split(exponentials)
        e_high_ref[u], e_low_ref[u] = pair
        inverse_ref[u] = inverse
        values = mm3((vt_high[...], vt_low[...]), pair) * inverse
        pv_ref[u] = values
        attended_t[...] += values * column_of(t2_ref[...], step * unroll + u)

    @pl.when(step == pl.num_programs(0) - 1)
    def _():
        inside = jnp.where(bias[...] < 0.0, 0.0, 1.0).astype(BF16)
        summed = mm(vt_high[...], inside) + mm(vt_low[...], inside)
        pv_bias_ref[...] = summed
        attended = (attended_t[...] + summed * t2_ref[:, 8:9]).T
        attended_ref[...] = attended
        fetch_up.wait()
        fetch_down.wait()
        vecs = vecs_ref[...]
        patch, kept = tail_forward(
            token_refs[0][...], attended, w_ref[:, 3 * width :], w_up[...], w_down[...], vecs
        )
        patch_ref[...] = patch
        for ref, value in zip((projected_ref, mixed_ref, hidden_ref, slope_ref, lowered_ref), kept):
            ref[...] = value
        unit, _ = norm_rows(patch)
        normed = split(unit * vecs[14:15] + vecs[15:16])
        pairs = images * 8
        image = lax.broadcasted_iota(jnp.int32, (pairs, 1), 0) // 8
        positions = place * rows + lax.broadcasted_iota(jnp.int32, (1, rows), 1)
        belong = image_of(lengths_ref, images, positions) == image
        class_scores = mm3(split(key_rows_ref[...]), normed, NT)
        class_scores = jnp.where(belong, class_scores, MASKED)
        scores_ref[...] = class_scores
        top = jnp.max(class_scores, axis=1, keepdims=True)
        weights = jnp.where(belong, jnp.exp(class_scores - top), 0.0)
        packed_ref[:, :width] = mm3(split(weights), normed)
        lane = lax.broadcasted_iota(jnp.int32, (1, 128), 1)
        total = jnp.sum(weights, axis=1, keepdims=True)
        packed_ref[:, width:] = jnp.where(lane < 64, top, total)


def by_head(unroll, shape):
    return pl.BlockSpec((unroll,) + shape[1:], lambda g: (g, 0, 0))


def forward(place, lengths, token_slots, matrices, vectors, t1, t2, key_rows, projected):
    slots, (rows, width) = len(token_slots), token_slots[0].shape
    total, heads = slots * rows, 8
    unroll = 4 if total <= 1024 else 1
    hidden = matrices.shape[3]
    pairs = key_rows.shape[0]
    outs = [struct((heads, total, rows), BF16)] * 2 + [struct((heads, width, rows)), struct((heads, 1, rows))]
    specs = [by_head(unroll, out.shape) for out in outs]
    rest = [
        struct((width, rows)), struct((rows, width)),
        struct((width, total), BF16), struct((width, total), BF16),
        struct((total, width), BF16), struct((total, width), BF16),
        struct((rows, width)), struct((rows, width)), struct((rows, width)),
        struct((rows, hidden)), struct((rows, hidden)), struct((rows, width)),
        struct((pairs, width + 128)), struct((pairs, rows)),
    ]
    operands = [*token_slots, matrices, vectors, t1, t2, key_rows, *projected, matrices]
    in_specs = [whole(operand.shape) for operand in operands]
    in_specs[slots] = weight_block(0, 0, matrices.shape)
    in_specs[-1] = anywhere()
    flops = 2 * 3 * ((2 * heads + 1) * total + 9 * width) * rows * width
    return pl.pallas_call(
        functools.partial(forward_kernel, slots, lengths.shape[1], unroll),
        grid=(heads // unroll,),
        in_specs=[smem(), smem()] + in_specs,
        out_specs=specs + [whole(out.shape) for out in rest],
        out_shape=outs + rest,
        scratch_shapes=[
            pltpu.VMEM((total, width), BF16),
            pltpu.VMEM((total, width), BF16),
            pltpu.VMEM((width, total), BF16),
            pltpu.VMEM((width, total), BF16),
            pltpu.VMEM((width, rows), F32),
            pltpu.VMEM((total, rows), F32),
            pltpu.VMEM((width, rows), F32),
            pltpu.VMEM((width, hidden), F32),
            pltpu.VMEM((width, hidden), F32),
            pltpu.SemaphoreType.DMA((2,)),
        ],
        compiler_params=limit(KERNEL_MIB),
        cost_estimate=pl.CostEstimate(
            flops=flops, bytes_accessed=24 << 20, transcendentals=heads * total * rows
        ),
        name="forward",
    )(place, lengths, *operands)


def middle_kernel(images, slots, *refs):
    place_ref = refs[0]
    parts = [ref[...] for ref in refs[1 : 1 + slots]]
    (
        vecs_ref, normed_c_ref, query_c_ref, value_c_ref, key_rows_ref, own_ref,
        class_ref, cot_class_ref, cot_patch_ref, patch_ref, scores_ref, attended_ref,
        projected_ref, mixed_ref, hidden_ref, slope_ref, lowered_ref, mats_ref,
        class_out_ref, d_attended_ref, d_mixed_ref, keep_ref, send_ref, partial_ref,
        factors_ref, vec_rows_ref, class_terms_ref,
        wc0, wc1, wc2, ws0, ws1, ws2, arrived,
    ) = refs[1 + slots :]
    width = class_ref.shape[1]
    heads = 8
    size = width // heads
    fetches = [
        pltpu.make_async_copy(source, target, arrived.at[number])
        for number, (source, target) in enumerate([
            (mats_ref.at[1, 0], wc0), (mats_ref.at[1, 1], wc1), (mats_ref.at[1, 2], wc2),
            (mats_ref.at[0, 2], ws2), (mats_ref.at[0, 1], ws1), (mats_ref.at[0, 0], ws0),
        ])
    ]
    for fetch in fetches:
        fetch.start()
    vecs = vecs_ref[...]
    vecs_s, vecs_c = vecs[:14], vecs[14:]
    mask = head_mask(heads, width)
    first = jnp.where(place_ref[0] == 0, 1.0, 0.0)
    own_score = own_ref[:, :1]
    normed_c = normed_c_ref[...]
    normed_rep = repeat_rows(normed_c, heads)
    top = own_score
    for part in parts:
        top = jnp.maximum(top, part[:, width : width + 1])
    own_weight = jnp.exp(own_score - top)
    total, summed = own_weight, own_weight * normed_rep
    for part in parts:
        rescale = jnp.exp(part[:, width : width + 1] - top)
        total = total + part[:, width + 64 : width + 65] * rescale
        summed = summed + part[:, :width] * rescale
    value_rows = summed / total
    own_prob = own_weight / total
    fetches[0].wait()
    w_v = split(wc0[:, 2 * width : 3 * width])
    class_attended = fold_heads(mm3(split(value_rows), w_v), mask) + vecs_c[3:4]
    fetches[1].wait()
    fetches[2].wait()
    w_out_c = wc0[:, 3 * width :]
    class_out, kept_c = tail_forward(class_ref[...], class_attended, w_out_c, wc1[...], wc2[...], vecs_c)
    class_out_ref[...] = class_out
    d_mixed_c, d_attended_c, d_projected_c, d_hidden_c, d_lowered_c, normed2_c, tail_rows_c = (
        tail_backward(cot_class_ref[...], kept_c, w_out_c, wc1[...], wc2[...], vecs_c)
    )
    delta = head_sums(d_attended_c * class_attended, mask)
    cot_rows = mm3(split(spread(d_attended_c, mask)), w_v, NT)
    cot_const = head_sums(d_attended_c * vecs_c[3:4], mask)
    scores = scores_ref[...]
    probs = jnp.where(scores > 0.5 * MASKED, jnp.exp(scores - top) * (1.0 / total), 0.0)
    unit_p, scale_p = norm_rows(patch_ref[...])
    normed_p = split(unit_p * vecs_c[0:1] + vecs_c[1:2])
    cot_split = split(cot_rows)
    d_scores = probs * (mm3(cot_split, normed_p, NT) + cot_const - delta)
    d_own = own_prob * (head_sums(d_attended_c * value_c_ref[...], mask) - delta)
    key_rows = key_rows_ref[...]
    d_split = split(d_scores)
    d_normed_p = mm3(d_split, split(key_rows), TN) + mm3(split(probs), cot_split, TN)
    partial_ref[...] = mm3(d_split, normed_p)
    cot = cot_patch_ref[...] + norm_back(d_normed_p * vecs_c[0:1], unit_p, scale_p)
    class_terms_ref[...] = jnp.concatenate(
        [rows_of(d_own * key_rows + own_prob * cot_rows, heads), d_mixed_c], axis=0
    )
    query_c = query_c_ref[...]
    chunks = lambda value: [value[:, i * width : (i + 1) * width] for i in range(4)]
    factors_ref[...] = jnp.concatenate(
        [normed_c, class_attended, normed2_c, d_lowered_c, d_own * normed_rep, value_rows,
         jnp.zeros_like(query_c), query_c * size ** (-0.5), d_attended_c, d_projected_c,
         *chunks(d_hidden_c), *chunks(kept_c[2])], axis=0)
    for fetch in fetches[3:]:
        fetch.wait()
    kept = tuple(ref[...] for ref in (projected_ref, mixed_ref, hidden_ref, slope_ref, lowered_ref))
    d_mixed, d_attended, d_projected, d_hidden, d_lowered, normed, tail_rows = tail_backward(
        cot, kept, ws0[:, 3 * width :], ws1[...], ws2[...], vecs_s
    )
    d_mixed_ref[...] = d_mixed
    d_attended_ref[...] = d_attended
    zero = jnp.zeros((1, width), F32)
    vec_rows_ref[...] = jnp.concatenate(
        [zero] * 4 + tail_rows
        + [row_sum(d_normed_p * unit_p), row_sum(d_normed_p), zero, row_sum(d_attended_c) * first]
        + [row * first for row in tail_rows_c], axis=0)
    g_out = dot3(attended_ref[...], d_projected, TN)
    g_up = dot3(normed, d_hidden, TN)
    g_down = dot3(d_lowered, hidden_ref[...], TN)
    even = jnp.bitwise_and(place_ref[0], 1) == 0
    hidden = g_up.shape[1]
    keep_ref[:, :hidden] = jnp.where(even, g_up, g_down)
    send_ref[:, :hidden] = jnp.where(even, g_down, g_up)
    left = g_out[:, :256]
    right = jnp.concatenate([g_out[:, 256:], jnp.zeros((width, 512 - width), F32)], axis=1)
    keep_ref[:, hidden:] = jnp.where(even, left, right)
    send_ref[:, hidden:] = jnp.where(even, right, left)


def middle(place, parts, vectors, prepared, class_tokens, cot_class, cot_patch, forwarded, matrices):
    images, width = class_tokens.shape
    rows = cot_patch.shape[0]
    hidden = matrices.shape[3]
    pairs = parts[0].shape[0]
    operands = [*parts, vectors, *prepared, class_tokens, cot_class, cot_patch, *forwarded, matrices]
    in_specs = [whole(operand.shape) for operand in operands]
    in_specs[-1] = anywhere()
    outs = [
        struct((images, width)), struct((rows, width)), struct((rows, width)),
        struct((width, hidden + 256)), struct((width, hidden + 256)), struct((pairs, width)),
        struct((16 * images + 2 * pairs, width)), struct((28, width)), struct((2 * images, width)),
    ]
    return pl.pallas_call(
        functools.partial(middle_kernel, images, len(parts)),
        grid=(1,),
        in_specs=[smem()] + in_specs,
        out_specs=[whole(out.shape) for out in outs],
        out_shape=outs,
        scratch_shapes=[pltpu.VMEM((width, hidden), F32)] * 6 + [pltpu.SemaphoreType.DMA((6,))],
        compiler_params=limit(KERNEL_MIB),
        cost_estimate=pl.CostEstimate(flops=8 << 30, bytes_accessed=28 << 20, transcendentals=1 << 19),
        name="middle",
    )(place, *operands)


def class_kernel(slots, *refs):
    partial_refs = refs[:slots]
    terms_ref, class_ref, vecs_ref, w_ref, factors_ref, grad_ref, factors_out_ref = refs[slots:]
    images, width = class_ref.shape
    pairs = partial_refs[0].shape[0]
    heads = pairs // images
    mask = head_mask(heads, width)
    at = 4 * images
    query_rows = sum_of([factors_ref[at : at + pairs, :]] + [ref[...] for ref in partial_refs])
    w_k, w_q = w_ref[:, width : 2 * width], w_ref[:, :width]
    d_query = fold_heads(dot3(query_rows, w_k), mask) * (width // heads) ** (-0.5)
    d_normed = dot3(d_query, w_q, NT) + terms_ref[:images, :]
    unit, scale = norm_rows(class_ref[...])
    grad_ref[...] = terms_ref[images:, :] + norm_back(d_normed * vecs_ref[14:15, :], unit, scale)
    count = factors_ref.shape[0]
    factors_out_ref[:count, :] = factors_ref[...]
    factors_out_ref[at : at + pairs, :] = query_rows
    at = at + 2 * pairs
    factors_out_ref[at : at + images, :] = d_query
    added = [row_sum(d_normed * unit), row_sum(d_normed), row_sum(d_query), jnp.zeros((5, width), F32)]
    factors_out_ref[count:, :] = jnp.concatenate(added, axis=0)


def class_finish(partials, terms, class_tokens, vectors, matrices, factors):
    operands = [*partials, terms, class_tokens, vectors, matrices, factors]
    specs = [whole(operand.shape) for operand in operands]
    specs[-2] = weight_block(1, 0, matrices.shape)
    outs = [struct(class_tokens.shape), struct((factors.shape[0] + 8, factors.shape[1]))]
    return pl.pallas_call(
        functools.partial(class_kernel, len(partials)),
        grid=(1,),
        in_specs=specs,
        out_specs=[whole(out.shape) for out in outs],
        out_shape=outs,
        compiler_params=limit(KERNEL_MIB),
        cost_estimate=pl.CostEstimate(flops=1 << 29, bytes_accessed=3 << 20, transcendentals=0),
        name="class_finish",
    )(*operands)


def class_weights_kernel(images, mine_ref, factors_ref, grads_ref, squares_ref, small_ref):
    groups, count, width = factors_ref.shape
    heads = 8
    pairs = images * heads
    mask = head_mask(heads, width)
    at = 4 * images + 2 * pairs

    def rows(ref, begin, count=images):
        return jnp.concatenate([ref[g, begin : begin + count, :] for g in range(groups)], axis=0)

    def chunked(begin):
        return jnp.concatenate([rows(factors_ref, begin + i * images) for i in range(4)], axis=1)

    def headed(left, right):
        return dot3(rows(mine_ref, left, pairs), spread(rows(factors_ref, right), mask), TN)

    grads_ref[0, :, :width] = dot3(rows(mine_ref, 0), rows(factors_ref, at), TN)
    grads_ref[0, :, width : 2 * width] = headed(4 * images, at + images)
    grads_ref[0, :, 2 * width : 3 * width] = headed(4 * images + pairs, at + 2 * images)
    grads_ref[0, :, 3 * width :] = dot3(rows(mine_ref, images), rows(factors_ref, at + 3 * images), TN)
    grads_ref[1] = dot3(rows(mine_ref, 2 * images), chunked(at + 4 * images), TN)
    grads_ref[2] = dot3(rows(mine_ref, 3 * images), chunked(at + 8 * images), TN)
    grads = grads_ref[...]
    squares_ref[...] = jnp.broadcast_to(jnp.sum(grads * grads), squares_ref.shape)
    added = sum_of([mine_ref[g, count - 8 :, :] for g in range(groups)])
    lanes = 128 - 22
    share = added.shape[1]
    added = jnp.concatenate([jnp.zeros((14, share), F32), added, jnp.zeros((lanes, share), F32)], axis=0)
    small_ref[...] = added.T


def class_weights(images, mine, factors):
    share = mine.shape[2]
    outs = [struct((3, share, 4 * factors.shape[2])), struct((8, 128)), struct((share, 128))]
    return pl.pallas_call(
        functools.partial(class_weights_kernel, images),
        grid=(1,),
        in_specs=[whole(mine.shape), whole(factors.shape)],
        out_specs=[whole(out.shape) for out in outs],
        out_shape=outs,
        compiler_params=limit(KERNEL_MIB),
        cost_estimate=pl.CostEstimate(flops=1 << 29, bytes_accessed=3 << 20, transcendentals=0),
        name="class_weights",
    )(mine, factors)


def mm3_wide(left, right):
    width = right[0].shape[1]
    both = mm(left[0], jnp.concatenate(right, axis=1))
    return both[:, :width] + (both[:, width:] + mm(left[1], right[0]))


def backward_kernel(slots, images, dp_size, unroll, *refs):
    place_ref, lengths_ref = refs[:2]
    token_refs = refs[2 : 2 + slots]
    (
        e_high_ref, e_low_ref, pv_ref, inverse_ref, pv_bias_ref, cot_ref,
        kt_high, kt_low, v_high, v_low, query_ref, t1_ref, t2_ref, t1_rows, t2_rows,
        vec_rows_ref, vecs_ref, w_ref,
    ) = refs[2 + slots : 20 + slots]
    (
        even_ref, odd_ref, keep_ref, send_ref,
        d_keys, d_values, c1, c2, cot_t, qt, d_qt, v_three,
    ) = refs[20 + slots :]
    rows, width = cot_ref.shape
    step = pl.program_id(0)
    size = width // 8
    lanes = lax.broadcasted_iota(jnp.int32, (1, 128), 1)

    @pl.when(step == 0)
    def _():
        cot_t[...] = cot_ref[...].T
        qt[...] = query_ref[...].T
        d_qt[...] = jnp.zeros_like(d_qt)
        d_keys[...] = jnp.zeros_like(d_keys)
        c1[...] = jnp.zeros_like(c1)
        v_three[...] = jnp.concatenate([v_high[...], v_high[...], v_low[...]], axis=1)
        c2[...] = jnp.where(
            lanes == 8, jnp.sum(cot_t[...] * pv_bias_ref[...], axis=1, keepdims=True), 0.0
        )
        inside = jnp.concatenate(same_image(lengths_ref, images, place_ref[0], slots, rows), axis=0)
        inside = jnp.where(inside, 1.0, 0.0).astype(BF16)
        high, low = split(cot_ref[...] * t2_rows[8:9, :])
        d_values[...] = mm(inside, high) + mm(inside, low)

    found = []
    for u in range(unroll):
        head = step * unroll + u
        t2_column, inverse = column_of(t2_ref[...], head), inverse_ref[u]
        crossed = cot_t[...] * pv_ref[u]
        c2[...] += jnp.where(lanes == head, jnp.sum(crossed, axis=1, keepdims=True), 0.0)
        delta = jnp.sum(crossed * t2_column, axis=0, keepdims=True) * inverse
        high, low = split(cot_t[...] * (t2_column * inverse))
        found.append((mm(v_three[...], jnp.concatenate([high, low, high], axis=0)), delta))
    for u in range(unroll):
        head = step * unroll + u
        d_probs, delta = found[u]
        pair = (e_high_ref[u], e_low_ref[u])
        d_mixed = split((pair[0].astype(F32) + pair[1].astype(F32)) * (d_probs - delta))
        inverse_rows = jnp.broadcast_to(inverse_ref[u], (8, rows)).T[:, :1]
        cot = split(cot_ref[...] * inverse_rows * t2_rows[pl.ds(head, 1), :])
        d_values[...] += mm3_wide(pair, cot)
        d_keys[...] += mm3_wide(d_mixed, split(query_ref[...] * t1_rows[pl.ds(head, 1), :]))
        back = mm3((kt_high[...], kt_low[...]), d_mixed)
        d_qt[...] += back * column_of(t1_ref[...], head)
        c1[...] += jnp.where(lanes == head, jnp.sum(back * qt[...], axis=1, keepdims=True), 0.0)

    @pl.when(step == pl.num_programs(0) - 1)
    def _():
        d_query = d_qt[...].T * size ** (-0.5)
        w_q, w_k, w_v = (split(w_ref[:, i * width : (i + 1) * width]) for i in range(3))
        gain = shift = g_k = g_v = 0.0
        for slot in range(slots):
            here = pl.ds(slot * rows, rows)
            unit, _ = norm_rows(token_refs[slot][...])
            normed = split(unit * vecs_ref[0:1, :] + vecs_ref[1:2, :])
            dk, dv = split(d_keys[here, :]), split(d_values[here, :])
            piece = mm3(dk, w_k, NT) + mm3(dv, w_v, NT)
            if slot == 0:
                dq = split(d_query)
                piece = piece + mm3(dq, w_q, NT)
                g_q = mm3(normed, dq, TN)
            (odd_ref if slot % 2 else even_ref)[slot // 2] = piece
            gain, shift = gain + row_sum(piece * unit), shift + row_sum(piece)
            g_k, g_v = g_k + mm3(normed, dk, TN), g_v + mm3(normed, dv, TN)
        added = jnp.concatenate(
            [gain, shift, row_sum(d_query), row_sum(d_values[...]), jnp.zeros((4, width), F32)], axis=0
        )
        vec_rows = jnp.concatenate([vec_rows_ref[0:8, :] + added, vec_rows_ref[8:28, :]], axis=0)
        fold = lambda value: jnp.concatenate(
            [row_sum(value[i * size : (i + 1) * size]) for i in range(8)], axis=0
        )
        pre, post = fold(c1[...]).T[:8, :], fold(c2[...])
        count = vec_rows.shape[0]
        talk = jnp.concatenate([pre, post[:, :9], jnp.zeros((8, 128 - count - 17), F32)], axis=1)
        block = width // dp_size
        talk = jnp.concatenate([talk, jnp.zeros((block - 8, 128 - count), F32)], axis=0)
        talk = jnp.concatenate([talk] * dp_size, axis=0)
        small = jnp.concatenate([vec_rows.T, talk], axis=1)
        even = jnp.bitwise_and(place_ref[0], 1) == 0
        left = jnp.concatenate([g_q, g_k[:, :256]], axis=1)
        right = jnp.concatenate([g_k[:, 256:], g_v, small], axis=1)
        keep_ref[...] = jnp.where(even, left, right)
        send_ref[...] = jnp.where(even, right, left)


def backward(dp_size, place, lengths, token_slots, found, cot, keys_values, query, tables,
             vec_rows, vectors, matrices):
    rows, width = cot.shape
    heads, total, _ = found[0].shape
    slots, unroll = total // rows, 2 if total <= 1024 else 1
    operands = [*token_slots, *found, cot, *keys_values, query, *tables, vec_rows, vectors, matrices]
    specs = [whole(operand.shape) for operand in operands]
    specs[slots : slots + 4] = [by_head(unroll, operand.shape) for operand in found[:4]]
    specs[-1] = weight_block(0, 0, matrices.shape)
    outs = [struct((slots // 2, rows, width))] * 2 + [struct((width, 640))] * 2
    return pl.pallas_call(
        functools.partial(backward_kernel, slots, lengths.shape[1], dp_size, unroll),
        grid=(heads // unroll,),
        in_specs=[smem(), smem()] + specs,
        out_specs=[whole(out.shape) for out in outs],
        out_shape=outs,
        scratch_shapes=[pltpu.VMEM((total, width), F32)] * 2
        + [pltpu.VMEM((width, 128), F32)] * 2
        + [pltpu.VMEM((width, rows), F32)] * 3
        + [pltpu.VMEM((total, 3 * width), BF16)],
        compiler_params=limit(KERNEL_MIB),
        cost_estimate=pl.CostEstimate(
            flops=6 * (4 * heads + 6) * total * rows * width, bytes_accessed=24 << 20, transcendentals=0
        ),
        name="backward",
    )(place, lengths, *operands)


def token_grad_kernel(tokens_ref, vecs_ref, near_ref, far_ref, tail_ref, grad_ref):
    unit, scale = norm_rows(tokens_ref[...])
    d_normed = near_ref[...] + far_ref[...]
    grad_ref[...] = tail_ref[...] + norm_back(d_normed * vecs_ref[0:1, :], unit, scale)


def token_grad(*operands):
    tokens = operands[0]
    return pl.pallas_call(
        token_grad_kernel,
        out_shape=struct(tokens.shape),
        compiler_params=limit(KERNEL_MIB),
        cost_estimate=pl.CostEstimate(flops=1 << 21, bytes_accessed=2 << 20, transcendentals=0),
        name="token_grad",
    )(*operands)


def squares_kernel(dp_size, place_ref, early_ref, late_ref, added_ref, class_ref, out_ref):
    odd = jnp.bitwise_and(place_ref[0], 1) == 1
    late = late_ref[...]
    small = late[:, 512:] + jnp.where(odd, added_ref[...], 0.0)
    lane = lax.broadcasted_iota(jnp.int32, small.shape, 1)
    talk = jnp.logical_and(odd, jnp.logical_and(lane >= 28, lane < 45))
    small = small * small * jnp.where(talk, 1.0 / dp_size, 1.0)
    total = jnp.sum(small)
    for value in (late[:, :512], early_ref[...]):
        total = total + jnp.sum(value * value)
    out_ref[...] = 0.5 * class_ref[...] + total


def squares_of(dp_size, place, *operands):
    vmem = pl.BlockSpec(memory_space=pltpu.VMEM)
    return pl.pallas_call(
        functools.partial(squares_kernel, dp_size),
        in_specs=[smem()] + [vmem] * len(operands),
        out_shape=struct((8, 128)),
        compiler_params=limit(KERNEL_MIB),
        cost_estimate=pl.CostEstimate(flops=1 << 18, bytes_accessed=1 << 19, transcendentals=0),
        name="squares",
    )(place, *operands)


def adam_step(weight, gradient, moment1, moment2, rate, decay):
    first = BETA_ONE * moment1 + (1.0 - BETA_ONE) * gradient
    second = BETA_TWO * moment2 + (1.0 - BETA_TWO) * gradient * gradient
    first_hat = first * (1.0 / (1.0 - BETA_ONE**STEP))
    second_hat = second * (1.0 / (1.0 - BETA_TWO**STEP))
    updated = weight - rate * (first_hat / (jnp.sqrt(second_hat) + ADAM_EPS) + decay * weight)
    return (updated, first, second)


def adam_kernel(*refs):
    (
        place_ref, squares_ref, early_own, early_other, late_own, late_other, added_ref,
        class_ref, w_ref, m1_ref, m2_ref, ema_ref, v_ref, v1_ref, v2_ref, v_ema_ref,
        t_ref, t1_ref, t2_ref, t_ema_ref,
    ) = refs[:20]
    norm_ref, new_ref, first_ref, second_ref, average_ref = refs[20:25]
    v_outs, t_outs = refs[25:29], refs[29:33]
    grads = refs[33]
    step = pl.program_id(0)
    norm = jnp.sqrt(squares_ref[0:1, 0:1])
    factor = jnp.minimum(1.0, CLIP_NORM / norm)

    def store(outs, weight, gradient, moment1, moment2, ema, rate, decay):
        updated, first, second = adam_step(weight, gradient * factor, moment1, moment2, rate, decay)
        average = EMA_RATE * ema + (1.0 - EMA_RATE) * updated
        for out, value in zip(outs, (updated, first, second, average)):
            out[...] = value

    @pl.when(step == 0)
    def _():
        norm_ref[...] = norm
        even = jnp.bitwise_and(place_ref[0], 1) == 0
        pair = lambda own, other: (jnp.where(even, own[...], other[...]), jnp.where(even, other[...], own[...]))
        early_left, early_right = pair(early_own, early_other)
        late_left, late_right = pair(late_own, late_other)
        hidden = grads.shape[2]
        grads[0] = jnp.concatenate(
            [late_left, late_right[:, :512], early_left[:, hidden:], early_right[:, hidden : hidden + 128]],
            axis=1,
        )
        grads[1] = early_left[:, :hidden]
        grads[2] = early_right[:, :hidden]
        small = late_right[:, 512:] + added_ref[...]
        count = v_ref.shape[0]
        store(v_outs, v_ref[...], small.T[:count, :], v1_ref[...], v2_ref[...], v_ema_ref[...], LR_VECTOR, 0.0)
        talk = small[:8, count : count + 17]
        store(t_outs, t_ref[...], talk, t1_ref[...], t2_ref[...], t_ema_ref[...], LR_TALKING, 0.0)

    self_grad = grads[jnp.minimum(step, 2)]
    grad = jnp.where(step < 3, self_grad, class_ref[jnp.maximum(step - 3, 0)])
    store((new_ref, first_ref, second_ref, average_ref), w_ref[...], grad, m1_ref[...], m2_ref[...],
          ema_ref[...], LR_MATRIX, WEIGHT_DECAY)


def optimizer(place, squares, grads, class_share, mats, vecs, talks):
    shape = mats[1].shape
    block = pl.BlockSpec((None, None) + shape[2:], lambda i: (i // 3, i % 3, 0, 0))
    operands = [squares, *grads, class_share, *mats, *vecs, *talks]
    specs = [whole(operand.shape) for operand in operands]
    specs[7:11] = [block] * 4
    outs = [struct((1, 1))] + [struct(shape)] * 4
    outs += [struct(vecs[0].shape)] * 4 + [struct(talks[0].shape)] * 4
    out_specs = [whole(out.shape) for out in outs]
    out_specs[1:5] = [block] * 4
    return pl.pallas_call(
        adam_kernel,
        grid=(6,),
        in_specs=[smem()] + specs,
        out_specs=out_specs,
        out_shape=outs,
        scratch_shapes=[pltpu.VMEM((3,) + shape[2:], F32)],
        compiler_params=limit(KERNEL_MIB),
        cost_estimate=pl.CostEstimate(flops=1 << 23, bytes_accessed=14 << 20, transcendentals=0),
        name="optimizer",
    )(place, *operands)


def swap(value, axis, size, bit):
    return lax.ppermute(value, axis, [(place, place ^ bit) for place in range(size)])


def bits_of(axis, size, bit=1):
    return [(axis, bit << i) for i in range((size // bit).bit_length() - 1)]


class Reduce:
    def __init__(self, terms, dp_size, seq_size, order, y_first=False):
        self.sizes = {"dp": dp_size, "seq": seq_size}
        dp = bits_of("dp", dp_size)
        chips = bits_of("seq", seq_size, 2)
        order = [dp[i] for i in order] + dp[len(order) :]
        self.left = dp[::-1] + (chips[::-1] if y_first else [])
        self.steps = [(step, "half") for step in (chips if y_first else []) + order]
        self.steps += [(step, "join" if y_first else "sum") for step in chips]
        shape = (2,) * len(self.left) + (-1, terms[0].shape[1])
        self.terms = [term.reshape(shape) for term in terms]

    def start(self):
        step, kind = self.steps[0]
        if kind != "half":
            self.terms = [sum_of(self.terms)]
            return self.terms[0]
        dim = self.left.index(step)
        self.left.pop(dim)
        mine = lax.axis_index(step[0]) // step[1] % 2
        take = lambda term, index: lax.dynamic_index_in_dim(term, index, dim, keepdims=False)
        sent = sum_of([take(term, 1 - mine) for term in self.terms])
        self.terms = [take(term, mine) for term in self.terms]
        return sent

    def swap(self, sent):
        (axis, bit), kind = self.steps.pop(0)
        other = swap(sent, axis, self.sizes[axis], bit)
        if kind == "join":
            low = lax.axis_index(axis) // bit % 2 == 0
            pair = [jnp.where(low, sent, other), jnp.where(low, other, sent)]
            self.terms = [jnp.concatenate(pair, axis=0)]
        else:
            self.terms.append(other)

    def value(self):
        return sum_of(self.terms)


def sum_of(terms):
    total = terms[0]
    for term in terms[1:]:
        total = total + term
    return total


def tie(value, *others):
    return lax.optimization_barrier((value, *others))[0]


def together(*values):
    return lax.optimization_barrier(values)


class Gather:
    def __init__(self, value, dp_size, seq_size):
        self.sizes = {"dp": dp_size, "seq": seq_size}
        self.value = value[None]
        dp = bits_of("dp", dp_size)
        self.steps = dp[2:] + dp[1:2] + dp[:1] + bits_of("seq", seq_size, 2) + bits_of("seq", 2)

    def swap(self):
        axis, bit = self.steps[0]
        self.other = swap(self.value, axis, self.sizes[axis], bit)

    def join(self):
        axis, bit = self.steps.pop(0)
        if axis == "dp":
            self.value = jnp.concatenate([self.value, self.other], axis=0)
        else:
            low = lax.axis_index("seq") // bit % 2 == 0
            pair = [jnp.where(low, self.value, self.other), jnp.where(low, self.other, self.value)]
            self.value = jnp.concatenate(pair, axis=1)


def on_device(
    dp_size, seq_size,
    tokens, class_tokens, cot_patch, cot_class, lengths,
    matrices, matrices_moment1, matrices_moment2, matrices_ema,
    vectors, vectors_moment1, vectors_moment2, vectors_ema,
    talking, talking_moment1, talking_moment2, talking_ema,
):
    rows, width = tokens.shape
    images = class_tokens.shape[0]
    seq_index = lax.axis_index("seq")
    dp_index = lax.axis_index("dp")
    place = seq_index.astype(jnp.int32).reshape(1)
    row_share = width // dp_size

    slots = {0: tokens}
    slots[1] = swap(tokens, "seq", seq_size, 1)
    bit = 2
    while bit < seq_size:
        for slot in sorted(slot for slot in slots if slot % 2 == 0):
            slots[slot | bit] = swap(slots[slot], "seq", seq_size, bit)
        bit *= 2
    *prepared, t1, t2, t1_rows, t2_rows, query, k1, k2, v1, v2, kt1, kt2, vt1, vt2 = prepare(
        tokens, slots[1], class_tokens, matrices, vectors, talking
    )
    for slot in range(2, seq_size, 2):
        slots[slot + 1] = swap(tie(slots[slot], query), "seq", seq_size, 1)
    token_slots = [slots[slot] for slot in range(seq_size)]
    (
        e_high, e_low, pv, inverse, pv_bias, attended, kt_high, kt_low, v_high, v_low,
        patch_out, *kept, packed, scores,
    ) = forward(
        place, lengths, token_slots, matrices, vectors, t1, t2, prepared[3],
        [query, k1, k2, v1, v2, kt1, kt2, vt1, vt2],
    )
    parts = [packed] + [swap(packed, "seq", seq_size, bit) for bit in range(1, seq_size)]
    (
        class_out, d_attended, d_mixed, early_keep, early_send, partial, factors, vec_rows, class_terms,
    ) = middle(
        place, parts, vectors, prepared, class_tokens, cot_class, cot_patch,
        [patch_out, scores, attended, *kept], matrices,
    )

    early = Reduce([early_keep, swap(early_send, "seq", seq_size, 1)], dp_size, seq_size, (1, 0))
    partials = [partial] + [swap(partial, "seq", seq_size, bit) for bit in range(1, seq_size)]
    grad_class, factors = class_finish(partials, class_terms, class_tokens, vectors, matrices, factors)
    share = factors.shape[0] // seq_size
    at = (seq_index % 2 * (seq_size // 2) + seq_index // 2) * share
    gather = Gather(lax.dynamic_slice_in_dim(factors, at, share, 0), dp_size, seq_size)
    sent, gather.value, d_attended = together(early.start(), gather.value, d_attended)
    early.swap(sent)
    gather.swap()
    even, odd, late_keep, late_send = backward(
        dp_size, place, lengths, token_slots, [e_high, e_low, pv, inverse, pv_bias], d_attended,
        [kt_high, kt_low, v_high, v_low], query, [t1, t2, t1_rows, t2_rows], vec_rows, vectors, matrices,
    )

    late_send, odd, gather.other, early.terms[-1] = together(
        late_send, odd, gather.other, early.terms[-1]
    )
    late = Reduce([late_keep, swap(late_send, "seq", seq_size, 1)], dp_size, seq_size, (1, 0))
    odd = swap(odd, "seq", seq_size, 1)
    early.swap(early.start())
    gather.join()
    gather.swap()
    sent = late.start()
    late.swap(sent)
    even = tie(even, sent)
    chips = [even[i] + odd[i] for i in range(seq_size // 2)]
    bit = 1
    while 2 * bit < len(chips):
        for slot in range(0, len(chips), 2 * bit):
            chips[slot] = chips[slot] + swap(chips[slot + bit], "seq", seq_size, 2 * bit)
        bit *= 2
    far = swap(chips[bit], "seq", seq_size, 2 * bit)
    weight_rows, vector_columns = (
        lax.dynamic_slice_in_dim(tie(value, sent), dp_index * row_share, row_share, dim)
        for value, dim in ((matrices, 2), (vectors, 1))
    )
    late.terms[-1], weight_rows, vector_columns = together(late.terms[-1], weight_rows, vector_columns)
    class_share = None
    while late.steps or early.steps or gather.steps:
        after = []
        if late.steps:
            after = [late.start()]
            late.swap(after[0])
        if early.steps:
            early.terms[-1] = tie(early.terms[-1], *after)
            early.swap(early.start())
        if gather.steps:
            gather.join()
            gather.value = tie(gather.value, *after)
            if gather.steps:
                gather.swap()
                late.terms[-1], gather.other = together(late.terms[-1], gather.other)
        if far is not None:
            grad_tokens = token_grad(tokens, vectors, tie(chips[0], *after), far, d_mixed)
            far = None
            late.terms[-1], grad_tokens = together(late.terms[-1], grad_tokens)
    factors = gather.value
    mine = lax.dynamic_slice_in_dim(factors, dp_index * row_share, row_share, 2)
    class_share, class_squares, added = class_weights(images, mine, factors)
    late, early = late.value(), early.value()
    squares = squares_of(dp_size, place, early, late, added, class_squares)
    squares = squares + swap(squares, "seq", seq_size, 1)
    bit = 1
    while bit < dp_size:
        squares = squares + swap(squares, "dp", dp_size, bit)
        bit *= 2
    grads = []
    for value in (early, late):
        grads += [value, swap(value, "seq", seq_size, 1)]
    norm, *updated = optimizer(
        place, squares, [*grads, added], class_share,
        [weight_rows, matrices_moment1, matrices_moment2, matrices_ema],
        [vector_columns, vectors_moment1, vectors_moment2, vectors_ema],
        [talking, talking_moment1, talking_moment2, talking_ema],
    )
    return (patch_out, class_out, grad_tokens, grad_class, norm.reshape(()), *updated)


def solution(mesh):
    tokens = P(("dp", "seq"), None)
    by_group = P("dp", None)
    mats = P(None, None, "dp", None)
    vecs = P(None, "dp")
    body = functools.partial(on_device, mesh.shape["dp"], mesh.shape["seq"])
    return jax.shard_map(
        body,
        mesh=mesh,
        in_specs=(tokens, by_group, tokens, by_group, by_group, P(), mats, mats, mats,
                  P(), vecs, vecs, vecs, P(), P(), P(), P()),
        out_specs=(tokens, by_group, tokens, by_group, P(), mats, mats, mats, mats,
                   vecs, vecs, vecs, vecs, P(), P(), P(), P()),
        check_vma=False,
    )
```

profile of v0, /device:TPU:0, one launch (start us, length us, event | category | flops | bytes accessed | tf_op | source)
XLA Modules:
  0.0 233.4 jit_solution(337415651412580354)
XLA Ops:
  1.2 2.6 %collective-permute-start.1 = (f32[256,384]{1,0:T(8,128)}, f32[256,384]{1,0:T(8,128)S(1)}, u32[]{:S(2)}, u32[]{:S(2)}) collective-permute-start(f32[256,384]{1,0:T(8,128)} %tokens_ref.1), channel_id=1, source_target_pairs={{0,2},{1,3},{2,0},{3,1},{4,6},{5,7},{6,4},{7,5},{8,10},{9,11},{10,... | collective-permute-start | bytes 1179656 | tf_op jit(solution)/shard_map/ppermute | solution.py:861
  4.5 7.1 %prepare.1 = (f32[4,384]{1,0:T(4,128)}, f32[4,384]{1,0:T(4,128)}, f32[4,384]{1,0:T(4,128)}, f32[32,384]{1,0:T(8,128)}, f32[32,128]{1,0:T(8,128)}, /*index=5*/f32...) custom-call(f32[256,384]{1,0:T(8,128)} %tokens_ref.1, ...), custom_call_target="tpu_custom_call" | custom-call | flops 4294967296 | bytes 8388608 | tf_op jit(solution)/shard_map/prepare/pallas_call | solution.py:245
  11.7 2.0 collective-permute-done.1.refs_4_
  16.2 31.7 %forward.1 = (bf16[8,1024,256]{2,1,0:T(8,128)(2,1)}, bf16[8,1024,256]{2,1,0:T(8,128)(2,1)}, f32[8,384,256]{2,1,0:T(8,128)}, f32[8,1,256]{2,1,0:T(1,128)}, f32[38...) custom-call(s32[1]{0:T(128)} %bitcast.refs_0_.place_ref, ...), custom_call_target="tpu_custom_call" | custom-call | flops 12306087936 | bytes 25165824 | tf_op jit(solution)/shard_map/forward/pallas_call | solution.py:373
  49.9 2.8 %collective-permute-done.4.refs_3_ = f32[32,512]{1,0:T(8,128)S(1)} collective-permute-done((f32[32,512]{1,0:T(8,128)}, f32[32,512]{1,0:T(8,128)S(1)}, u32[]{:S(2)}, u32[]{:S(2)}) %collective-permute-start.4) | collective-permute-done | bytes 65568 | tf_op jit(solution)/shard_map/ppermute | solution.py:861
  54.8 22.0 %middle.1 = (f32[4,384]{1,0:T(4,128)}, f32[256,384]{1,0:T(8,128)}, f32[256,384]{1,0:T(8,128)}, f32[384,1792]{1,0:T(8,128)}, f32[384,1792]{1,0:T(8,128)}, /*index...) custom-call(s32[1]{0:T(128)} %bitcast.refs_0_.place_ref, ...), custom_call_target="tpu_custom_call" | custom-call | flops 8589934592 | bytes 29360128 | tf_op jit(solution)/shard_map/middle/pallas_call | solution.py:514
  78.9 3.1 %collective-permute-done.7.refs_1_ = f32[32,384]{1,0:T(8,128)S(1)} collective-permute-done((f32[32,384]{1,0:T(8,128)}, f32[32,384]{1,0:T(8,128)S(1)}, u32[]{:S(2)}, u32[]{:S(2)}) %collective-permute-start.7) | collective-permute-done | bytes 49184 | tf_op jit(solution)/shard_map/ppermute | solution.py:861
  83.1 3.2 %class_finish.1 = (f32[4,384]{1,0:T(4,128)}, f32[136,384]{1,0:T(8,128)}) custom-call(f32[32,384]{1,0:T(8,128)} %get-tuple-element.146.refs_0_, f32[32,384]{1,0:T(8,128)} %copy-done.13, f32[32,384]{1,0:T(8,128)} %copy-done.14, f32[32,384]{1,0:T(8,128)} %copy-done.15, f32[8,384]{1,0:T(8,128)} %get-tuple-element.147.refs_4_, f32[4,384]{1,0:T(4,128)} %refs_5_.3, ...), custom_call_target="tpu_custom_call" | custom-call | flops 536870912 | bytes 3145728 | tf_op jit(solution)/shard_map/class_finish/pallas_call | solution.py:555
  90.4 2.6 %collective-permute-start.10 = (f32[1,34,384]{2,1,0:T(8,128)S(1)}, f32[1,34,384]{2,1,0:T(8,128)}, u32[]{:S(2)}, u32[]{:S(2)}) collective-permute-start(f32[1,34,384]{2,1,0:T(8,128)S(1)} %dynamic-slice_bitcast_fusion), channel_id=1, source_target_pairs={{0,16},{4,20},{8,24},{12,28},{16,0},{20,4},{24,8},{28,12},{1,17},{... | collective-permute-start | bytes 156680 | tf_op jit(solution)/shard_map/ppermute | solution.py:861
  93.0 37.5 %backward.1 = (f32[2,256,384]{2,1,0:T(8,128)}, f32[2,256,384]{2,1,0:T(8,128)}, f32[384,640]{1,0:T(8,128)}, f32[384,640]{1,0:T(8,128)}) custom-call(s32[1]{0:T(128)} %bitcast.refs_0_.place_ref, s32[1,4]{1,0:T(1,128)} %refs_1_.3, f32[256,384]{1,0:T(8,128)} %tokens_ref.1, f32[256,384]{1,0:T(8,128)} %copy-done.9, f32[256,384]{1,0:T(8,128)} %copy-done.16, ...), custom_call_target="tpu_custom_call" | custom-call | flops 22951231488 | bytes 25165824 | tf_op jit(solution)/shard_map/backward/pallas_call | solution.py:723
  132.6 2.3 bitcast_add_fusion
  142.6 2.9 %constant_dynamic-slice_fusion.1.refs_8_ = f32[2,3,48,1536]{3,2,1,0:T(8,128)} fusion(f32[2,3,384,1536]{3,2,1,0:T(8,128)} %refs_23_.1, s32[]{:T(128)S(6)} %select_n.154), kind=kLoop, calls=%fused_computation.29 | loop fusion | bytes 3538948 | tf_op jit(solution)/shard_map/dynamic_slice | solution.py:1018
  145.5 4.7 %collective-permute-done.13 = f32[2,2,48,640]{3,2,1,0:T(8,128)S(1)} collective-permute-done((f32[2,2,48,640]{3,2,1,0:T(8,128)S(1)}, f32[2,2,48,640]{3,2,1,0:T(8,128)S(1)}, u32[]{:S(2)}, u32[]{:S(2)}) %collective-permute-start.13) | collective-permute-done | bytes 491552 | tf_op jit(solution)/shard_map/ppermute | solution.py:861
  155.8 2.4 %token_grad.1 = f32[256,384]{1,0:T(8,128)} custom-call(f32[256,384]{1,0:T(8,128)} %tokens_ref.1, f32[28,384]{1,0:T(8,128)} %vecs_ref.3, f32[256,384]{1,0:T(8,128)} %get-tuple-element.174.near_ref, f32[256,384]{1,0:T(8,128)} %copy-done.10, f32[256,384]{1,0:T(8,128)} %get-tuple-element.175.tail_ref), custom_call_target="tpu_custom_call" | custom-call | flops 2097152 | bytes 2097152 | tf_op jit(solution)/shard_map/token_grad/pallas_call | solution.py:749
  158.2 6.0 %collective-permute-done.16 = f32[4,34,384]{2,1,0:T(8,128)} collective-permute-done((f32[4,34,384]{2,1,0:T(8,128)S(1)}, f32[4,34,384]{2,1,0:T(8,128)}, u32[]{:S(2)}, u32[]{:S(2)}) %collective-permute-start.16) | collective-permute-done | bytes 208928 | tf_op jit(solution)/shard_map/ppermute | solution.py:861
  169.7 2.6 %collective-permute-start.20 = (f32[48,1792]{1,0:T(8,128)S(1)}, f32[48,1792]{1,0:T(8,128)S(1)}, u32[]{:S(2)}, u32[]{:S(2)}) collective-permute-start(f32[48,1792]{1,0:T(8,128)S(1)} %bitcast_add_fusion.1), channel_id=1, source_target_pairs={{0,16},{4,20},{8,24},{12,28},{16,0},{20,4},{24,8},{28,12},{1,17},{... | collective-permute-start | bytes 1032200 | tf_op jit(solution)/shard_map/ppermute | solution.py:861
  172.3 10.8 %collective-permute-done.22 = f32[48,640]{1,0:T(8,128)S(1)} collective-permute-done((f32[48,640]{1,0:T(8,128)}, f32[48,640]{1,0:T(8,128)S(1)}, u32[]{:S(2)}, u32[]{:S(2)}) %collective-permute-start.22) | collective-permute-done | bytes 122912 | tf_op jit(solution)/shard_map/ppermute | solution.py:861
  185.7 3.6 %collective-permute-done.20 = f32[48,1792]{1,0:T(8,128)S(1)} collective-permute-done((f32[48,1792]{1,0:T(8,128)S(1)}, f32[48,1792]{1,0:T(8,128)S(1)}, u32[]{:S(2)}, u32[]{:S(2)}) %collective-permute-start.20) | collective-permute-done | bytes 344096 | tf_op jit(solution)/shard_map/ppermute | solution.py:861
  192.8 8.2 %collective-permute-done.21 = f32[48,1792]{1,0:T(8,128)S(1)} collective-permute-done((f32[48,1792]{1,0:T(8,128)S(1)}, f32[48,1792]{1,0:T(8,128)S(1)}, u32[]{:S(2)}, u32[]{:S(2)}) %collective-permute-start.21) | collective-permute-done | bytes 344096 | tf_op jit(solution)/shard_map/ppermute | solution.py:861
  204.0 3.2 %class_weights.1 = (f32[3,48,1536]{2,1,0:T(8,128)}, f32[8,128]{1,0:T(8,128)}, f32[48,128]{1,0:T(8,128)}) custom-call(f32[8,136,48]{2,1,0:T(8,128)} %constant_dynamic-slice_fusion.2.mine_ref, f32[8,136,384]{2,1,0:T(8,128)} %copy-done), custom_call_target="tpu_custom_call" | custom-call | flops 536870912 | bytes 3145728 | tf_op jit(solution)/shard_map/class_weights/pallas_call | solution.py:601
  211.7 3.1 %collective-permute-done.27 = f32[8,128]{1,0:T(8,128)S(1)} collective-permute-done((f32[8,128]{1,0:T(8,128)S(1)}, f32[8,128]{1,0:T(8,128)S(1)}, u32[]{:S(2)}, u32[]{:S(2)}) %collective-permute-start.27) | collective-permute-done | bytes 4128 | tf_op jit(solution)/shard_map/ppermute | solution.py:861
  214.8 3.6 %collective-permute-done.28 = f32[8,128]{1,0:T(8,128)S(1)} collective-permute-done((f32[8,128]{1,0:T(8,128)S(1)}, f32[8,128]{1,0:T(8,128)S(1)}, u32[]{:S(2)}, u32[]{:S(2)}) %collective-permute-start.28) | collective-permute-done | bytes 4128 | tf_op jit(solution)/shard_map/ppermute | solution.py:861
  218.8 4.1 %collective-permute-done.29 = f32[8,128]{1,0:T(8,128)S(1)} collective-permute-done((f32[8,128]{1,0:T(8,128)S(1)}, f32[8,128]{1,0:T(8,128)S(1)}, u32[]{:S(2)}, u32[]{:S(2)}) %collective-permute-start.29) | collective-permute-done | bytes 4128 | tf_op jit(solution)/shard_map/ppermute | solution.py:861
  224.3 8.9 %optimizer.1 = (f32[1,1]{1,0:T(1,128)}, f32[2,3,48,1536]{3,2,1,0:T(8,128)}, f32[2,3,48,1536]{3,2,1,0:T(8,128)}, f32[2,3,48,1536]{3,2,1,0:T(8,128)}, f32[2,3,48,1...) custom-call(s32[1]{0:T(128)} %bitcast.refs_0_.place_ref, ...), custom_call_target="tpu_custom_call" | custom-call | flops 8388608 | bytes 14680064 | tf_op jit(solution)/shard_map/optimizer/pallas_call | solution.py:847
  (118 shorter events, 51.0 us)
Async XLA Ops:
  1.2 12.5 %collective-permute-start.1 = (f32[256,384]{1,0:T(8,128)}, f32[256,384]{1,0:T(8,128)S(1)}, u32[]{:S(2)}, u32[]{:S(2)}) collective-permute-start(f32[256,384]{1,0:T(8,128)} %tokens_ref.1), channel_id=1, source_target_pairs={{0,2},{1,3},{2,0},{3,1},{4,6},{5,7},{6,4},{7,5},{8,10},{9,11},{10,... | collective-permute-start | bytes 1179656 | tf_op jit(solution)/shard_map/ppermute | solution.py:861
  48.1 4.6 %collective-permute-start.4 = (f32[32,512]{1,0:T(8,128)}, f32[32,512]{1,0:T(8,128)S(1)}, u32[]{:S(2)}, u32[]{:S(2)}) collective-permute-start(f32[32,512]{1,0:T(8,128)} %get-tuple-element.126.refs_1_), channel_id=1, source_target_pairs={{0,2},{1,3},{2,0},{3,1},{4,6},{5,7},{6,4},{7,5},{8,10},{9,11},{10,... | collective-permute-start | bytes 196616 | tf_op jit(solution)/shard_map/ppermute | solution.py:861
  76.8 10.4 %collective-permute-start.6 = (f32[384,1792]{1,0:T(8,128)}, f32[384,1792]{1,0:T(8,128)}, u32[]{:S(2)}, u32[]{:S(2)}) collective-permute-start(f32[384,1792]{1,0:T(8,128)} %get-tuple-element.145), channel_id=1, source_target_pairs={{0,1},{1,0},{2,3},{3,2},{4,5},{5,4},{6,7},{7,6},{8,9},{9,8},{10,11... | collective-permute-start | bytes 8257544 | tf_op jit(solution)/shard_map/ppermute | solution.py:861
  77.0 5.0 %collective-permute-start.7 = (f32[32,384]{1,0:T(8,128)}, f32[32,384]{1,0:T(8,128)S(1)}, u32[]{:S(2)}, u32[]{:S(2)}) collective-permute-start(f32[32,384]{1,0:T(8,128)} %get-tuple-element.146.refs_0_), channel_id=1, source_target_pairs={{0,1},{1,0},{2,3},{3,2},{4,5},{5,4},{6,7},{7,6},{8,9},{9,8},{10,11... | collective-permute-start | bytes 147464 | tf_op jit(solution)/shard_map/ppermute | solution.py:861
  77.4 4.6 %collective-permute-start.8 = (f32[32,384]{1,0:T(8,128)}, f32[32,384]{1,0:T(8,128)S(1)}, u32[]{:S(2)}, u32[]{:S(2)}) collective-permute-start(f32[32,384]{1,0:T(8,128)} %get-tuple-element.146.refs_0_), channel_id=1, source_target_pairs={{0,2},{1,3},{2,0},{3,1},{4,6},{5,7},{6,4},{7,5},{8,10},{9,11},{10,... | collective-permute-start | bytes 147464 | tf_op jit(solution)/shard_map/ppermute | solution.py:861
  88.8 41.8 %collective-permute-start.11 = (f32[2,2,48,1792]{3,2,1,0:T(8,128)S(1)}, f32[2,2,48,1792]{3,2,1,0:T(8,128)}, u32[]{:S(2)}, u32[]{:S(2)}) collective-permute-start(f32[2,2,48,1792]{3,2,1,0:T(8,128)S(1)} %add_bitcast_fusion), channel_id=1, source_target_pairs={{0,8},{4,12},{8,0},{12,4},{16,24},{20,28},{24,16},{28,20},{1,9},{5... | collective-permute-start | bytes 4128776 | tf_op jit(solution)/shard_map/ppermute | solution.py:861
  90.4 40.1 %collective-permute-start.10 = (f32[1,34,384]{2,1,0:T(8,128)S(1)}, f32[1,34,384]{2,1,0:T(8,128)}, u32[]{:S(2)}, u32[]{:S(2)}) collective-permute-start(f32[1,34,384]{2,1,0:T(8,128)S(1)} %dynamic-slice_bitcast_fusion), channel_id=1, source_target_pairs={{0,16},{4,20},{8,24},{12,28},{16,0},{20,4},{24,8},{28,12},{1,17},{... | collective-permute-start | bytes 156680 | tf_op jit(solution)/shard_map/ppermute | solution.py:861
  130.6 5.8 %collective-permute-start.12 = (f32[384,640]{1,0:T(8,128)}, f32[384,640]{1,0:T(8,128)}, u32[]{:S(2)}, u32[]{:S(2)}) collective-permute-start(f32[384,640]{1,0:T(8,128)} %get-tuple-element.164), channel_id=1, source_target_pairs={{0,1},{1,0},{2,3},{3,2},{4,5},{5,4},{6,7},{7,6},{8,9},{9,8},{10,11... | collective-permute-start | bytes 2949128 | tf_op jit(solution)/shard_map/ppermute | solution.py:861
  130.6 8.5 %collective-permute-start.17 = (f32[2,256,384]{2,1,0:T(8,128)}, f32[2,256,384]{2,1,0:T(8,128)S(1)}, u32[]{:S(2)}, u32[]{:S(2)}) collective-permute-start(f32[2,256,384]{2,1,0:T(8,128)} %get-tuple-element.173), channel_id=1, source_target_pairs={{0,1},{1,0},{2,3},{3,2},{4,5},{5,4},{6,7},{7,6},{8,9},{9,8},{10,11... | collective-permute-start | bytes 2359304 | tf_op jit(solution)/shard_map/ppermute | solution.py:861
  132.1 20.5 %collective-permute-start.15 = (f32[2,34,384]{2,1,0:T(8,128)S(1)}, f32[2,34,384]{2,1,0:T(8,128)S(1)}, u32[]{:S(2)}, u32[]{:S(2)}) collective-permute-start(f32[2,34,384]{2,1,0:T(8,128)S(1)} %pad_maximum_fusion.4), channel_id=1, source_target_pairs={{0,8},{4,12},{8,0},{12,4},{16,24},{20,28},{24,16},{28,20},{1,9},{5... | collective-permute-start | bytes 313352 | tf_op jit(solution)/shard_map/ppermute | solution.py:861
  134.9 33.2 %collective-permute-start.19 = (f32[2,48,1792]{2,1,0:T(8,128)}, f32[2,48,1792]{2,1,0:T(8,128)}, u32[]{:S(2)}, u32[]{:S(2)}) collective-permute-start(f32[2,48,1792]{2,1,0:T(8,128)} %bitcast_add_fusion), channel_id=1, source_target_pairs={{0,4},{4,0},{8,12},{12,8},{16,20},{20,16},{24,28},{28,24},{1,5},{5... | collective-permute-start | bytes 2064392 | tf_op jit(solution)/shard_map/ppermute | solution.py:861
  137.5 12.7 %collective-permute-start.13 = (f32[2,2,48,640]{3,2,1,0:T(8,128)S(1)}, f32[2,2,48,640]{3,2,1,0:T(8,128)S(1)}, u32[]{:S(2)}, u32[]{:S(2)}) collective-permute-start(f32[2,2,48,640]{3,2,1,0:T(8,128)S(1)} %add_bitcast_fusion.1), channel_id=1, source_target_pairs={{0,8},{4,12},{8,0},{12,4},{16,24},{20,28},{24,16},{28,20},{1,9},{5... | collective-permute-start | bytes 1474568 | tf_op jit(solution)/shard_map/ppermute | solution.py:861
  140.1 14.9 %collective-permute-start.18 = (f32[256,384]{1,0:T(8,128)}, f32[256,384]{1,0:T(8,128)S(1)}, u32[]{:S(2)}, u32[]{:S(2)}) collective-permute-start(f32[256,384]{1,0:T(8,128)} %get-tuple-element.209), channel_id=1, source_target_pairs={{0,2},{1,3},{2,0},{3,1},{4,6},{5,7},{6,4},{7,5},{8,10},{9,11},{10,... | collective-permute-start | bytes 1179656 | tf_op jit(solution)/shard_map/ppermute | solution.py:861
  152.1 12.2 %collective-permute-start.14 = (f32[2,48,640]{2,1,0:T(8,128)}, f32[2,48,640]{2,1,0:T(8,128)}, u32[]{:S(2)}, u32[]{:S(2)}) collective-permute-start(f32[2,48,640]{2,1,0:T(8,128)} %bitcast_add_fusion.5), channel_id=1, source_target_pairs={{0,4},{4,0},{8,12},{12,8},{16,20},{20,16},{24,28},{28,24},{1,5},{5... | collective-permute-start | bytes 737288 | tf_op jit(solution)/shard_map/ppermute | solution.py:861
  153.5 10.8 %collective-permute-start.16 = (f32[4,34,384]{2,1,0:T(8,128)S(1)}, f32[4,34,384]{2,1,0:T(8,128)}, u32[]{:S(2)}, u32[]{:S(2)}) collective-permute-start(f32[4,34,384]{2,1,0:T(8,128)S(1)} %pad_maximum_fusion.3), channel_id=1, source_target_pairs={{0,4},{4,0},{8,12},{12,8},{16,20},{20,16},{24,28},{28,24},{1,5},{5... | collective-permute-start | bytes 626696 | tf_op jit(solution)/shard_map/ppermute | solution.py:861
  166.9 16.2 %collective-permute-start.23 = (f32[8,34,384]{2,1,0:T(8,128)S(1)}, f32[8,34,384]{2,1,0:T(8,128)}, u32[]{:S(2)}, u32[]{:S(2)}) collective-permute-start(f32[8,34,384]{2,1,0:T(8,128)S(1)} %pad_maximum_fusion.2), channel_id=1, source_target_pairs={{0,2},{1,3},{2,0},{3,1},{4,6},{5,7},{6,4},{7,5},{8,10},{9,11},{10,... | collective-permute-start | bytes 1253384 | tf_op jit(solution)/shard_map/ppermute | solution.py:861
  168.1 15.0 %collective-permute-start.22 = (f32[48,640]{1,0:T(8,128)}, f32[48,640]{1,0:T(8,128)S(1)}, u32[]{:S(2)}, u32[]{:S(2)}) collective-permute-start(f32[48,640]{1,0:T(8,128)} %bitcast_add_fusion.8), channel_id=1, source_target_pairs={{0,16},{4,20},{8,24},{12,28},{16,0},{20,4},{24,8},{28,12},{1,17},{... | collective-permute-start | bytes 368648 | tf_op jit(solution)/shard_map/ppermute | solution.py:861
  169.7 19.6 %collective-permute-start.20 = (f32[48,1792]{1,0:T(8,128)S(1)}, f32[48,1792]{1,0:T(8,128)S(1)}, u32[]{:S(2)}, u32[]{:S(2)}) collective-permute-start(f32[48,1792]{1,0:T(8,128)S(1)} %bitcast_add_fusion.1), channel_id=1, source_target_pairs={{0,16},{4,20},{8,24},{12,28},{16,0},{20,4},{24,8},{28,12},{1,17},{... | collective-permute-start | bytes 1032200 | tf_op jit(solution)/shard_map/ppermute | solution.py:861
  185.6 16.7 %collective-permute-start.25 = (f32[8,68,384]{2,0,1:T(8,128)S(1)}, f32[8,68,384]{2,0,1:T(8,128)S(1)}, u32[]{:S(2)}, u32[]{:S(2)}) collective-permute-start(f32[8,68,384]{2,0,1:T(8,128)S(1)} %copy.34), channel_id=1, source_target_pairs={{0,1},{1,0},{2,3},{3,2},{4,5},{5,4},{6,7},{7,6},{8,9},{9,8},{10,11... | collective-permute-start | bytes 2506760 | tf_op jit(solution)/shard_map/ppermute | solution.py:861
  190.7 10.3 %collective-permute-start.21 = (f32[48,1792]{1,0:T(8,128)S(1)}, f32[48,1792]{1,0:T(8,128)S(1)}, u32[]{:S(2)}, u32[]{:S(2)}) collective-permute-start(f32[48,1792]{1,0:T(8,128)S(1)} %fusion.2), channel_id=1, source_target_pairs={{0,2},{1,3},{2,0},{3,1},{4,6},{5,7},{6,4},{7,5},{8,10},{9,11},{10,... | collective-permute-start | bytes 1032200 | tf_op jit(solution)/shard_map/ppermute | solution.py:861
  191.7 10.6 %collective-permute-start.24 = (f32[48,640]{1,0:T(8,128)S(1)}, f32[48,640]{1,0:T(8,128)S(1)}, u32[]{:S(2)}, u32[]{:S(2)}) collective-permute-start(f32[48,640]{1,0:T(8,128)S(1)} %fusion.3), channel_id=1, source_target_pairs={{0,2},{1,3},{2,0},{3,1},{4,6},{5,7},{6,4},{7,5},{8,10},{9,11},{10,... | collective-permute-start | bytes 368648 | tf_op jit(solution)/shard_map/ppermute | solution.py:861
  201.0 22.5 %collective-permute-start.30 = (f32[48,1792]{1,0:T(8,128)S(1)}, f32[48,1792]{1,0:T(8,128)S(1)}, u32[]{:S(2)}, u32[]{:S(2)}) collective-permute-start(f32[48,1792]{1,0:T(8,128)S(1)} %add.343.early_ref.refs_2_), channel_id=1, source_target_pairs={{0,1},{1,0},{2,3},{3,2},{4,5},{5,4},{6,7},{7,6},{8,9},{9,8},{10,11... | collective-permute-start | bytes 1032200 | tf_op jit(solution)/shard_map/ppermute | solution.py:861
  202.7 20.8 %collective-permute-start.31 = (f32[48,640]{1,0:T(8,128)S(1)}, f32[48,640]{1,0:T(8,128)S(1)}, u32[]{:S(2)}, u32[]{:S(2)}) collective-permute-start(f32[48,640]{1,0:T(8,128)S(1)} %add.350.late_ref.refs_4_), channel_id=1, source_target_pairs={{0,1},{1,0},{2,3},{3,2},{4,5},{5,4},{6,7},{7,6},{8,9},{9,8},{10,11... | collective-permute-start | bytes 368648 | tf_op jit(solution)/shard_map/ppermute | solution.py:861
  218.4 4.5 %collective-permute-start.29 = (f32[8,128]{1,0:T(8,128)S(1)}, f32[8,128]{1,0:T(8,128)S(1)}, u32[]{:S(2)}, u32[]{:S(2)}) collective-permute-start(f32[8,128]{1,0:T(8,128)S(1)} %add.353), channel_id=1, source_target_pairs={{0,16},{4,20},{8,24},{12,28},{16,0},{20,4},{24,8},{28,12},{1,17},{... | collective-permute-start | bytes 12296 | tf_op jit(solution)/shard_map/ppermute | solution.py:861
  (29 other events, 78.1 us)
where the time goes:
time: 237 us; the launch traced here: 233 us
  Pallas kernels  118 us (50%)
  waiting for transfers between devices  58.1 us (25%)
  starting transfers between devices  26.4 us (11%)
  other arithmetic  18.8 us (8%)
  local copies, waits for them, and re-layouts  11 us (5%)
    ppermute x32, waiting for transfers between devices, swap(): lax.ppermute(value, axis, [(place, place ^ bit) for place in range(size)])  58.1 us
    pallas_call x1, Pallas kernels, backward(): pl.pallas_call(functools.partial(backward_kernel, slots, lengths.shape[1]...  37.5 us
    pallas_call x1, Pallas kernels, forward(): pl.pallas_call(functools.partial(forward_kernel, slots, lengths.shape[1],...  31.7 us
    ppermute x32, starting transfers between devices, swap(): lax.ppermute(value, axis, [(place, place ^ bit) for place in range(size)])  26.4 us
    pallas_call x1, Pallas kernels, middle(): pl.pallas_call(functools.partial(middle_kernel, images, len(parts)), grid...  22 us
    add x10, other arithmetic, sum_of(): total = total + term  12.3 us
    pallas_call x1, Pallas kernels, optimizer(): pl.pallas_call(adam_kernel, grid=(6,), in_specs=[smem()] + specs, out_spe...  8.9 us
    pallas_call x1, Pallas kernels, prepare(): pl.pallas_call(prepare_kernel, grid=(1,), in_specs=specs, out_specs=[whol...  7.14 us
  transfers between devices with their start and end apart: 32, of which 16 were waited for; matrix products, arithmetic and copies ran while one was open for 10% of the time, Pallas kernels for 24%

commit v1 on v0

--- a/solution.py
+++ b/solution.py
@@ -24,7 +24,7 @@
 NN = (((1,), (0,)), ((), ()))
 NT = (((1,), (1,)), ((), ()))
 TN = (((0,), (0,)), ((), ()))
-KERNEL_MIB = 58
+KERNEL_MIB, SMALL_MIB = 58, 24
 
 
 def split(value):
@@ -38,6 +38,17 @@
 
 def mm3(left, right, dims=NN):
     return mm(left[0], right[0], dims) + (mm(left[0], right[1], dims) + mm(left[1], right[0], dims))
+
+
+def mm3_tall(left, right, dims=NN):
+    rows = left[0].shape[0]
+    stacked = jnp.concatenate([part.astype(F32) for part in left], axis=0).astype(BF16)
+    both = mm(stacked, right[0], dims)
+    return both[:rows] + (both[rows:] + mm(left[0], right[1], dims))
+
+
+def dot_tall(left, right, dims=NN):
+    return mm3_tall(split(left), split(right), dims)
 
 
 def dot3(left, right, dims=NN):
@@ -67,28 +78,28 @@
     return jnp.sum(values, axis=0, keepdims=True)
 
 
-def tail_forward(inputs, attended, w_out, w_up, w_down, vecs):
-    projected = dot3(attended, w_out) + vecs[4:5]
+def tail_forward(dot, inputs, attended, w_out, w_up, w_down, vecs):
+    projected = dot(attended, w_out) + vecs[4:5]
     mixed = inputs + vecs[5:6] * projected
     unit, _ = norm_rows(mixed)
     normed = unit * vecs[6:7] + vecs[7:8]
     up_bias = jnp.concatenate([vecs[row : row + 1] for row in range(8, 12)], axis=1)
-    hidden, slope = gelu_both(dot3(normed, w_up) + up_bias)
-    lowered = dot3(hidden, w_down, NT) + vecs[12:13]
+    hidden, slope = gelu_both(dot(normed, w_up) + up_bias)
+    lowered = dot(hidden, w_down, NT) + vecs[12:13]
     return mixed + vecs[13:14] * lowered, (projected, mixed, hidden, slope, lowered)
 
 
-def tail_backward(cot, kept, w_out, w_up, w_down, vecs):
+def tail_backward(dot, cot, kept, w_out, w_up, w_down, vecs):
     projected, mixed, hidden, slope, lowered = kept
     width = cot.shape[1]
     unit, scale = norm_rows(mixed)
     normed = unit * vecs[6:7] + vecs[7:8]
     d_lowered = cot * vecs[13:14]
-    d_hidden = dot3(d_lowered, w_down) * slope
-    d_normed = dot3(d_hidden, w_up, NT)
+    d_hidden = dot(d_lowered, w_down) * slope
+    d_normed = dot(d_hidden, w_up, NT)
     d_mixed = cot + norm_back(d_normed * vecs[6:7], unit, scale)
     d_projected = d_mixed * vecs[5:6]
-    d_attended = dot3(d_projected, w_out, NT)
+    d_attended = dot(d_projected, w_out, NT)
     d_up = row_sum(d_hidden)
     rows = [
         row_sum(d_projected), row_sum(d_mixed * projected), row_sum(d_normed * unit), row_sum(d_normed),
@@ -175,8 +186,19 @@
     return pl.BlockSpec(memory_space=pl.ANY)
 
 
-def weight_block(block, matrix, shape):
-    return pl.BlockSpec((None, None) + shape[2:], lambda *_: (block, matrix, 0, 0))
+def weight_block(block, matrix, shape, columns=None):
+    return pl.BlockSpec((None, None, shape[2], columns or shape[3]), lambda *_: (block, matrix, 0, 0))
+
+
+def far_off(*operands):
+    return [pltpu.with_memory_space_constraint(operand, pltpu.HBM) for operand in operands]
+
+
+def copy_in(pairs, arrived):
+    copies = [pltpu.make_async_copy(a, b, arrived.at[i]) for i, (a, b) in enumerate(pairs)]
+    for copy in copies:
+        copy.start()
+    return copies
 
 
 def limit(mebibytes):
@@ -206,7 +228,7 @@
     mask = head_mask(heads, width)
     unit, _ = norm_rows(class_ref[...])
     normed = unit * vecs[14:15] + vecs[15:16]
-    both = dot3(normed, w_class_ref[:, : 3 * width])
+    both = dot_tall(normed, w_class_ref[...])
     query = both[:, :width] + vecs[16:17]
     normed_ref[...] = normed
     query_c_ref[...] = query
@@ -238,10 +260,11 @@
         struct((rows, width)),
     ]
     outs += [struct((2 * rows, width), BF16)] * 4 + [struct((width, 2 * rows), BF16)] * 4
+    own, class_tokens, matrices, vectors, talking = far_off(own, class_tokens, matrices, vectors, talking)
     operands = [own, near, class_tokens, matrices, matrices, vectors, talking]
     specs = [whole(operand.shape) for operand in operands]
-    specs[3] = weight_block(0, 0, matrices.shape)
-    specs[4] = weight_block(1, 0, matrices.shape)
+    specs[3] = weight_block(0, 0, matrices.shape, 3 * width)
+    specs[4] = weight_block(1, 0, matrices.shape, 3 * width)
     return pl.pallas_call(
         prepare_kernel,
         grid=(1,),
@@ -258,76 +281,108 @@
     place_ref, lengths_ref = refs[:2]
     token_refs = refs[2 : 2 + slots]
     (
-        w_ref, vecs_ref, t1_ref, t2_ref, key_rows_ref, query_ref,
+        vecs_ref, t1_ref, t2_ref, key_rows_ref, query_ref,
         k_high0, k_low0, v_high0, v_low0, kt_high0, kt_low0, vt_high0, vt_low0, mats_ref,
-        e_high_ref, e_low_ref, pv_ref, inverse_ref, pv_bias_ref, attended_ref,
-        kt_high, kt_low, v_high, v_low,
-        patch_ref, projected_ref, mixed_ref, hidden_ref, slope_ref, lowered_ref, packed_ref, scores_ref,
-        k_high, k_low, vt_high, vt_low, qt, bias, attended_t, w_up, w_down, arrived,
+        e_high_hbm, e_low_hbm, pv_hbm, inverse_ref, pv_bias_ref, attended_ref,
+        kt_high_hbm, kt_low_hbm, v_high_hbm, v_low_hbm,
+        patch_ref, projected_ref, mixed_ref, hidden_hbm, slope_hbm, lowered_ref, packed_ref, scores_ref,
+        k_three, vt_two, qt, bias, attended_t, w_kv, w_up, w_down, w_out, arrived,
+        kt_high, kt_low, v_high, v_low, hidden_ref, slope_ref, e_high_ref, e_low_ref, pv_ref, leaving,
     ) = refs[2 + slots :]
     rows, width = token_refs[0].shape
     step = pl.program_id(0)
     place = place_ref[0]
-    fetch_up = pltpu.make_async_copy(mats_ref.at[0, 1], w_up, arrived.at[0])
-    fetch_down = pltpu.make_async_copy(mats_ref.at[0, 2], w_down, arrived.at[1])
+    ready, columns = pl.ds(0, 2 * rows), lambda i: pl.ds(i * width, width)
+    pairs = [
+        (mats_ref.at[0, 0, :, pl.ds(width, 2 * width)], w_kv),
+        (k_high0, k_three.at[ready, columns(0)]), (k_high0, k_three.at[ready, columns(1)]),
+        (k_low0, k_three.at[ready, columns(2)]), (v_high0, v_high.at[ready, :]), (v_low0, v_low.at[ready, :]),
+        (kt_high0, kt_high.at[:, ready]), (kt_low0, kt_low.at[:, ready]),
+        (vt_high0, vt_two.at[columns(0), ready]), (vt_low0, vt_two.at[columns(1), ready]),
+        (mats_ref.at[0, 0, :, pl.ds(3 * width, width)], w_out),
+        (mats_ref.at[0, 1], w_up), (mats_ref.at[0, 2], w_down),
+    ]
+    fetches = [pltpu.make_async_copy(a, b, arrived.at[i]) for i, (a, b) in enumerate(pairs)]
+    pairs = [(kt_high, kt_high_hbm), (kt_low, kt_low_hbm), (v_high, v_high_hbm), (v_low, v_low_hbm),
+             (hidden_ref, hidden_hbm), (slope_ref, slope_hbm)]
+    stores = [pltpu.make_async_copy(a, b, leaving.at[i]) for i, (a, b) in enumerate(pairs)]
+    heads = inverse_ref.shape[0]
+    groups = []
+    for number in range(heads // unroll):
+        here = pl.ds(number * unroll, unroll)
+        groups.append([
+            pltpu.make_async_copy(a.at[here], b.at[here], leaving.at[6 + 3 * number + i])
+            for i, (a, b) in enumerate([(e_high_ref, e_high_hbm), (e_low_ref, e_low_hbm), (pv_ref, pv_hbm)])
+        ])
 
     @pl.when(step == 0)
     def _():
-        fetch_up.start()
-        fetch_down.start()
-        ready = pl.ds(0, 2 * rows)
-        for ref, found in ((k_high, k_high0), (k_low, k_low0), (v_high, v_high0), (v_low, v_low0)):
-            ref[ready, :] = found[...]
-        for ref, found in ((kt_high, kt_high0), (kt_low, kt_low0), (vt_high, vt_high0), (vt_low, vt_low0)):
-            ref[:, ready] = found[...]
-        w_k, w_v = (split(w_ref[:, i * width : (i + 1) * width]) for i in (1, 2))
+        for fetch in fetches:
+            fetch.start()
         vecs = vecs_ref[...]
         inside = same_image(lengths_ref, images, place, slots, rows)
         for slot in range(slots):
+            bias[pl.ds(slot * rows, rows), :] = jnp.where(inside[slot], 0.0, MASKED)
+        units = [norm_rows(ref[...])[0] for ref in token_refs[2:]]
+        fetches[0].wait()
+        w_k, w_v = split(w_kv[:, :width]), split(w_kv[:, width:])
+        for slot in range(2, slots):
             here = pl.ds(slot * rows, rows)
-            bias[here, :] = jnp.where(inside[slot], 0.0, MASKED)
-            if slot < 2:
-                continue
-            unit, _ = norm_rows(token_refs[slot][...])
-            normed = split(unit * vecs[0:1] + vecs[1:2])
+            normed = split(units[slot - 2] * vecs[0:1] + vecs[1:2])
             keys, values = mm3(normed, w_k), mm3(normed, w_v) + vecs[3:4]
-            k_high[here, :], k_low[here, :] = split(keys)
+            high, low = split(keys)
+            k_three[here, :] = jnp.concatenate([high, high, low], axis=1)
             v_high[here, :], v_low[here, :] = split(values)
             kt_high[:, here], kt_low[:, here] = split(keys.T)
-            vt_high[:, here], vt_low[:, here] = split(values.T)
+            vt_two[:, here] = jnp.concatenate(split(values.T), axis=0)
         qt[...] = query_ref[...].T
         attended_t[...] = jnp.zeros_like(attended_t)
+        for fetch in fetches[1:10]:
+            fetch.wait()
+        for store in stores[:4]:
+            store.start()
 
     scores = []
     for u in range(unroll):
-        query = split(qt[...] * column_of(t1_ref[...], step * unroll + u))
-        scores.append(mm3((k_high[...], k_low[...]), query) + bias[...])
+        high, low = split(qt[...] * column_of(t1_ref[...], step * unroll + u))
+        scores.append(mm(k_three[...], jnp.concatenate([high, low, high], axis=0)) + bias[...])
     for u in range(unroll):
         exponentials = jnp.exp(scores[u] - jnp.max(scores[u], axis=0, keepdims=True))
         inverse = 1.0 / jnp.sum(exponentials, axis=0, keepdims=True)
         pair = split(exponentials)
-        e_high_ref[u], e_low_ref[u] = pair
-        inverse_ref[u] = inverse
-        values = mm3((vt_high[...], vt_low[...]), pair) * inverse
-        pv_ref[u] = values
-        attended_t[...] += values * column_of(t2_ref[...], step * unroll + u)
+        head = step * unroll + u
+        e_high_ref[head], e_low_ref[head] = pair
+        inverse_ref[head] = inverse
+        both = mm(vt_two[...], pair[0])
+        values = (both[:width] + (both[width:] + mm(vt_two[:width, :], pair[1]))) * inverse
+        pv_ref[head] = values
+        attended_t[...] += values * column_of(t2_ref[...], head)
+    for number, group in enumerate(groups):
+
+        @pl.when(step == number)
+        def _(group=group):
+            for copy in group:
+                copy.start()
 
     @pl.when(step == pl.num_programs(0) - 1)
     def _():
         inside = jnp.where(bias[...] < 0.0, 0.0, 1.0).astype(BF16)
-        summed = mm(vt_high[...], inside) + mm(vt_low[...], inside)
+        both = mm(vt_two[...], inside)
+        summed = both[:width] + both[width:]
         pv_bias_ref[...] = summed
         attended = (attended_t[...] + summed * t2_ref[:, 8:9]).T
         attended_ref[...] = attended
-        fetch_up.wait()
-        fetch_down.wait()
+        for fetch in fetches[10:]:
+            fetch.wait()
         vecs = vecs_ref[...]
         patch, kept = tail_forward(
-            token_refs[0][...], attended, w_ref[:, 3 * width :], w_up[...], w_down[...], vecs
+            dot3, token_refs[0][...], attended, w_out[...], w_up[...], w_down[...], vecs
         )
         patch_ref[...] = patch
         for ref, value in zip((projected_ref, mixed_ref, hidden_ref, slope_ref, lowered_ref), kept):
             ref[...] = value
+        for store in stores[4:]:
+            store.start()
         unit, _ = norm_rows(patch)
         normed = split(unit * vecs[14:15] + vecs[15:16])
         pairs = images * 8
@@ -343,6 +398,8 @@
         lane = lax.broadcasted_iota(jnp.int32, (1, 128), 1)
         total = jnp.sum(weights, axis=1, keepdims=True)
         packed_ref[:, width:] = jnp.where(lane < 64, top, total)
+        for store in stores + [copy for group in groups for copy in group]:
+            store.wait()
 
 
 def by_head(unroll, shape):
@@ -355,38 +412,48 @@
     unroll = 4 if total <= 1024 else 1
     hidden = matrices.shape[3]
     pairs = key_rows.shape[0]
-    outs = [struct((heads, total, rows), BF16)] * 2 + [struct((heads, width, rows)), struct((heads, 1, rows))]
-    specs = [by_head(unroll, out.shape) for out in outs]
-    rest = [
-        struct((width, rows)), struct((rows, width)),
+    outs = [
+        struct((heads, total, rows), BF16), struct((heads, total, rows), BF16), struct((heads, width, rows)),
+        struct((heads, 1, rows)), struct((width, rows)), struct((rows, width)),
         struct((width, total), BF16), struct((width, total), BF16),
         struct((total, width), BF16), struct((total, width), BF16),
         struct((rows, width)), struct((rows, width)), struct((rows, width)),
         struct((rows, hidden)), struct((rows, hidden)), struct((rows, width)),
         struct((pairs, width + 128)), struct((pairs, rows)),
     ]
-    operands = [*token_slots, matrices, vectors, t1, t2, key_rows, *projected, matrices]
+    away = (0, 1, 2, 6, 7, 8, 9, 13, 14)
+    out_specs = [anywhere() if i in away else whole(out.shape) for i, out in enumerate(outs)]
+    operands = [*token_slots, vectors, t1, t2, key_rows, *projected, matrices]
     in_specs = [whole(operand.shape) for operand in operands]
-    in_specs[slots] = weight_block(0, 0, matrices.shape)
-    in_specs[-1] = anywhere()
+    in_specs[-9:] = [anywhere()] * 9
     flops = 2 * 3 * ((2 * heads + 1) * total + 9 * width) * rows * width
     return pl.pallas_call(
         functools.partial(forward_kernel, slots, lengths.shape[1], unroll),
         grid=(heads // unroll,),
         in_specs=[smem(), smem()] + in_specs,
-        out_specs=specs + [whole(out.shape) for out in rest],
-        out_shape=outs + rest,
+        out_specs=out_specs,
+        out_shape=outs,
         scratch_shapes=[
-            pltpu.VMEM((total, width), BF16),
-            pltpu.VMEM((total, width), BF16),
-            pltpu.VMEM((width, total), BF16),
-            pltpu.VMEM((width, total), BF16),
+            pltpu.VMEM((total, 3 * width), BF16),
+            pltpu.VMEM((2 * width, total), BF16),
             pltpu.VMEM((width, rows), F32),
             pltpu.VMEM((total, rows), F32),
             pltpu.VMEM((width, rows), F32),
+            pltpu.VMEM((width, 2 * width), F32),
             pltpu.VMEM((width, hidden), F32),
             pltpu.VMEM((width, hidden), F32),
-            pltpu.SemaphoreType.DMA((2,)),
+            pltpu.VMEM((width, width), F32),
+            pltpu.SemaphoreType.DMA((13,)),
+            pltpu.VMEM((width, total), BF16),
+            pltpu.VMEM((width, total), BF16),
+            pltpu.VMEM((total, width), BF16),
+            pltpu.VMEM((total, width), BF16),
+            pltpu.VMEM((rows, hidden), F32),
+            pltpu.VMEM((rows, hidden), F32),
+            pltpu.VMEM((heads, total, rows), BF16),
+            pltpu.VMEM((heads, total, rows), BF16),
+            pltpu.VMEM((heads, width, rows), F32),
+            pltpu.SemaphoreType.DMA((6 + 3 * heads // unroll,)),
         ],
         compiler_params=limit(KERNEL_MIB),
         cost_estimate=pl.CostEstimate(
@@ -401,24 +468,21 @@
     parts = [ref[...] for ref in refs[1 : 1 + slots]]
     (
         vecs_ref, normed_c_ref, query_c_ref, value_c_ref, key_rows_ref, own_ref,
-        class_ref, cot_class_ref, cot_patch_ref, patch_ref, scores_ref, attended_ref,
-        projected_ref, mixed_ref, hidden_ref, slope_ref, lowered_ref, mats_ref,
+        class_ref, cot_class_ref, cot_patch_ref, patch_ref, scores_ref,
+        attended_hbm, projected_hbm, mixed_hbm, hidden_hbm, slope_hbm, lowered_hbm, mats_ref,
         class_out_ref, d_attended_ref, d_mixed_ref, keep_ref, send_ref, partial_ref,
         factors_ref, vec_rows_ref, class_terms_ref,
-        wc0, wc1, wc2, ws0, ws1, ws2, arrived,
+        wc0, wc1, wc2, ws0, ws1, ws2, attended_ref, projected_ref, mixed_ref, hidden_ref, slope_ref, lowered_ref,
+        keep, send, arrived, stored,
     ) = refs[1 + slots :]
     width = class_ref.shape[1]
     heads = 8
     size = width // heads
-    fetches = [
-        pltpu.make_async_copy(source, target, arrived.at[number])
-        for number, (source, target) in enumerate([
-            (mats_ref.at[1, 0], wc0), (mats_ref.at[1, 1], wc1), (mats_ref.at[1, 2], wc2),
-            (mats_ref.at[0, 2], ws2), (mats_ref.at[0, 1], ws1), (mats_ref.at[0, 0], ws0),
-        ])
-    ]
-    for fetch in fetches:
-        fetch.start()
+    copies = copy_in(
+        [(mats_ref.at[1, 0, :, pl.ds(2 * width, 2 * width)], wc0), (mats_ref.at[1, 1], wc1), (mats_ref.at[1, 2], wc2),
+         (lowered_hbm, lowered_ref), (hidden_hbm, hidden_ref), (mats_ref.at[0, 2], ws2), (slope_hbm, slope_ref),
+         (mixed_hbm, mixed_ref), (mats_ref.at[0, 1], ws1), (projected_hbm, projected_ref),
+         (attended_hbm, attended_ref), (mats_ref.at[0, 0, :, pl.ds(3 * width, width)], ws0)], arrived)
     vecs = vecs_ref[...]
     vecs_s, vecs_c = vecs[:14], vecs[14:]
     mask = head_mask(heads, width)
@@ -437,31 +501,32 @@
         summed = summed + part[:, :width] * rescale
     value_rows = summed / total
     own_prob = own_weight / total
-    fetches[0].wait()
-    w_v = split(wc0[:, 2 * width : 3 * width])
-    class_attended = fold_heads(mm3(split(value_rows), w_v), mask) + vecs_c[3:4]
-    fetches[1].wait()
-    fetches[2].wait()
-    w_out_c = wc0[:, 3 * width :]
-    class_out, kept_c = tail_forward(class_ref[...], class_attended, w_out_c, wc1[...], wc2[...], vecs_c)
+    unit_p, scale_p = norm_rows(patch_ref[...])
+    normed_p = split(unit_p * vecs_c[0:1] + vecs_c[1:2])
+    scores = scores_ref[...]
+    probs = jnp.where(scores > 0.5 * MASKED, jnp.exp(scores - top) * (1.0 / total), 0.0)
+    for copy in copies[:3]:
+        copy.wait()
+    w_v = split(wc0[:, :width])
+    class_attended = fold_heads(mm3_tall(split(value_rows), w_v), mask) + vecs_c[3:4]
+    w_out_c = wc0[:, width:]
+    class_out, kept_c = tail_forward(
+        dot_tall, class_ref[...], class_attended, w_out_c, wc1[...], wc2[...], vecs_c
+    )
     class_out_ref[...] = class_out
     d_mixed_c, d_attended_c, d_projected_c, d_hidden_c, d_lowered_c, normed2_c, tail_rows_c = (
-        tail_backward(cot_class_ref[...], kept_c, w_out_c, wc1[...], wc2[...], vecs_c)
+        tail_backward(dot_tall, cot_class_ref[...], kept_c, w_out_c, wc1[...], wc2[...], vecs_c)
     )
     delta = head_sums(d_attended_c * class_attended, mask)
-    cot_rows = mm3(split(spread(d_attended_c, mask)), w_v, NT)
+    cot_rows = mm3_tall(split(spread(d_attended_c, mask)), w_v, NT)
     cot_const = head_sums(d_attended_c * vecs_c[3:4], mask)
-    scores = scores_ref[...]
-    probs = jnp.where(scores > 0.5 * MASKED, jnp.exp(scores - top) * (1.0 / total), 0.0)
-    unit_p, scale_p = norm_rows(patch_ref[...])
-    normed_p = split(unit_p * vecs_c[0:1] + vecs_c[1:2])
     cot_split = split(cot_rows)
-    d_scores = probs * (mm3(cot_split, normed_p, NT) + cot_const - delta)
+    d_scores = probs * (mm3_tall(cot_split, normed_p, NT) + cot_const - delta)
     d_own = own_prob * (head_sums(d_attended_c * value_c_ref[...], mask) - delta)
     key_rows = key_rows_ref[...]
     d_split = split(d_scores)
     d_normed_p = mm3(d_split, split(key_rows), TN) + mm3(split(probs), cot_split, TN)
-    partial_ref[...] = mm3(d_split, normed_p)
+    partial_ref[...] = mm3_tall(d_split, normed_p)
     cot = cot_patch_ref[...] + norm_back(d_normed_p * vecs_c[0:1], unit_p, scale_p)
     class_terms_ref[...] = jnp.concatenate(
         [rows_of(d_own * key_rows + own_prob * cot_rows, heads), d_mixed_c], axis=0
@@ -472,52 +537,83 @@
         [normed_c, class_attended, normed2_c, d_lowered_c, d_own * normed_rep, value_rows,
          jnp.zeros_like(query_c), query_c * size ** (-0.5), d_attended_c, d_projected_c,
          *chunks(d_hidden_c), *chunks(kept_c[2])], axis=0)
-    for fetch in fetches[3:]:
-        fetch.wait()
-    kept = tuple(ref[...] for ref in (projected_ref, mixed_ref, hidden_ref, slope_ref, lowered_ref))
-    d_mixed, d_attended, d_projected, d_hidden, d_lowered, normed, tail_rows = tail_backward(
-        cot, kept, ws0[:, 3 * width :], ws1[...], ws2[...], vecs_s
-    )
+    for copy in copies[3:]:
+        copy.wait()
+    projected, mixed, hidden, lowered = projected_ref[...], mixed_ref[...], split(hidden_ref[...]), lowered_ref[...]
+    unit, scale = norm_rows(mixed)
+    normed = split(unit * vecs_s[6:7] + vecs_s[7:8])
+    d_lowered = cot * vecs_s[13:14]
+    d_low_split = split(d_lowered)
+    d_hidden = mm3(d_low_split, split(ws2[...])) * slope_ref[...]
+    d_hid_split = split(d_hidden)
+    g_down = mm3(d_low_split, hidden, TN)
+    g_up = mm3(normed, d_hid_split, TN)
+    even = jnp.bitwise_and(place_ref[0], 1) == 0
+    size_up = g_up.shape[1]
+    send[:, :size_up] = jnp.where(even, g_down, g_up)
+    keep[:, :size_up] = jnp.where(even, g_up, g_down)
+    bulk = pl.ds(0, size_up)
+    leaving = copy_in(
+        [(send.at[:, bulk], send_ref.at[:, bulk]), (keep.at[:, bulk], keep_ref.at[:, bulk])], stored
+    )
+    d_normed = mm3(d_hid_split, split(ws1[...]), NT)
+    d_mixed = cot + norm_back(d_normed * vecs_s[6:7], unit, scale)
+    d_projected = d_mixed * vecs_s[5:6]
+    d_proj_split = split(d_projected)
+    g_out = mm3(split(attended_ref[...]), d_proj_split, TN)
+    left = g_out[:, :256]
+    right = jnp.concatenate([g_out[:, 256:], jnp.zeros((width, 512 - width), F32)], axis=1)
+    send[:, size_up:] = jnp.where(even, right, left)
+    keep[:, size_up:] = jnp.where(even, left, right)
+    rest = pl.ds(size_up, 256)
+    for i, (a, b) in enumerate([(send, send_ref), (keep, keep_ref)]):
+        leaving.append(pltpu.make_async_copy(a.at[:, rest], b.at[:, rest], stored.at[2 + i]))
+        leaving[-1].start()
     d_mixed_ref[...] = d_mixed
-    d_attended_ref[...] = d_attended
+    d_attended_ref[...] = mm3(d_proj_split, split(ws0[...]), NT)
+    d_up = row_sum(d_hidden)
+    tail_rows = [
+        row_sum(d_projected), row_sum(d_mixed * projected), row_sum(d_normed * unit), row_sum(d_normed),
+        *[d_up[:, i * width : (i + 1) * width] for i in range(4)],
+        row_sum(d_lowered), row_sum(cot * lowered),
+    ]
     zero = jnp.zeros((1, width), F32)
     vec_rows_ref[...] = jnp.concatenate(
         [zero] * 4 + tail_rows
         + [row_sum(d_normed_p * unit_p), row_sum(d_normed_p), zero, row_sum(d_attended_c) * first]
         + [row * first for row in tail_rows_c], axis=0)
-    g_out = dot3(attended_ref[...], d_projected, TN)
-    g_up = dot3(normed, d_hidden, TN)
-    g_down = dot3(d_lowered, hidden_ref[...], TN)
-    even = jnp.bitwise_and(place_ref[0], 1) == 0
-    hidden = g_up.shape[1]
-    keep_ref[:, :hidden] = jnp.where(even, g_up, g_down)
-    send_ref[:, :hidden] = jnp.where(even, g_down, g_up)
-    left = g_out[:, :256]
-    right = jnp.concatenate([g_out[:, 256:], jnp.zeros((width, 512 - width), F32)], axis=1)
-    keep_ref[:, hidden:] = jnp.where(even, left, right)
-    send_ref[:, hidden:] = jnp.where(even, right, left)
-
-
-def middle(place, parts, vectors, prepared, class_tokens, cot_class, cot_patch, forwarded, matrices):
+    for copy in leaving:
+        copy.wait()
+
+
+def middle(place, parts, vectors, prepared, class_tokens, cot_class, cot_patch, patch, scores, kept, matrices):
     images, width = class_tokens.shape
     rows = cot_patch.shape[0]
     hidden = matrices.shape[3]
     pairs = parts[0].shape[0]
-    operands = [*parts, vectors, *prepared, class_tokens, cot_class, cot_patch, *forwarded, matrices]
-    in_specs = [whole(operand.shape) for operand in operands]
-    in_specs[-1] = anywhere()
+    operands = [*parts, vectors, *prepared, class_tokens, cot_class, cot_patch, patch, scores, *kept, matrices]
     outs = [
         struct((images, width)), struct((rows, width)), struct((rows, width)),
         struct((width, hidden + 256)), struct((width, hidden + 256)), struct((pairs, width)),
         struct((16 * images + 2 * pairs, width)), struct((28, width)), struct((2 * images, width)),
     ]
+    in_specs = [whole(operand.shape) for operand in operands]
+    in_specs[-1 - len(kept) :] = [anywhere()] * (1 + len(kept))
+    out_specs = [whole(out.shape) for out in outs]
+    out_specs[3:5] = [anywhere()] * 2
     return pl.pallas_call(
         functools.partial(middle_kernel, images, len(parts)),
         grid=(1,),
         in_specs=[smem()] + in_specs,
-        out_specs=[whole(out.shape) for out in outs],
+        out_specs=out_specs,
         out_shape=outs,
-        scratch_shapes=[pltpu.VMEM((width, hidden), F32)] * 6 + [pltpu.SemaphoreType.DMA((6,))],
+        scratch_shapes=[pltpu.VMEM((width, 2 * width), F32)]
+        + [pltpu.VMEM((width, hidden), F32)] * 2
+        + [pltpu.VMEM((width, width), F32)]
+        + [pltpu.VMEM((width, hidden), F32)] * 2
+        + [pltpu.VMEM(value.shape, F32) for value in kept]
+        + [pltpu.VMEM((width, hidden + 256), F32)] * 2
+        + [pltpu.SemaphoreType.DMA((12,)), pltpu.SemaphoreType.DMA((4,))],
         compiler_params=limit(KERNEL_MIB),
         cost_estimate=pl.CostEstimate(flops=8 << 30, bytes_accessed=28 << 20, transcendentals=1 << 19),
         name="middle",
@@ -534,8 +630,8 @@
     at = 4 * images
     query_rows = sum_of([factors_ref[at : at + pairs, :]] + [ref[...] for ref in partial_refs])
     w_k, w_q = w_ref[:, width : 2 * width], w_ref[:, :width]
-    d_query = fold_heads(dot3(query_rows, w_k), mask) * (width // heads) ** (-0.5)
-    d_normed = dot3(d_query, w_q, NT) + terms_ref[:images, :]
+    d_query = fold_heads(dot_tall(query_rows, w_k), mask) * (width // heads) ** (-0.5)
+    d_normed = dot_tall(d_query, w_q, NT) + terms_ref[:images, :]
     unit, scale = norm_rows(class_ref[...])
     grad_ref[...] = terms_ref[images:, :] + norm_back(d_normed * vecs_ref[14:15, :], unit, scale)
     count = factors_ref.shape[0]
@@ -548,9 +644,9 @@
 
 
 def class_finish(partials, terms, class_tokens, vectors, matrices, factors):
-    operands = [*partials, terms, class_tokens, vectors, matrices, factors]
+    operands = [*partials, *far_off(terms, class_tokens, vectors, matrices, factors)]
     specs = [whole(operand.shape) for operand in operands]
-    specs[-2] = weight_block(1, 0, matrices.shape)
+    specs[-2] = weight_block(1, 0, matrices.shape, 2 * class_tokens.shape[1])
     outs = [struct(class_tokens.shape), struct((factors.shape[0] + 8, factors.shape[1]))]
     return pl.pallas_call(
         functools.partial(class_kernel, len(partials)),
@@ -558,7 +654,7 @@
         in_specs=specs,
         out_specs=[whole(out.shape) for out in outs],
         out_shape=outs,
-        compiler_params=limit(KERNEL_MIB),
+        compiler_params=limit(SMALL_MIB),
         cost_estimate=pl.CostEstimate(flops=1 << 29, bytes_accessed=3 << 20, transcendentals=0),
         name="class_finish",
     )(*operands)
@@ -618,23 +714,28 @@
 
 def backward_kernel(slots, images, dp_size, unroll, *refs):
     place_ref, lengths_ref = refs[:2]
-    token_refs = refs[2 : 2 + slots]
+    token_hbm = refs[2 : 2 + slots]
     (
         e_high_ref, e_low_ref, pv_ref, inverse_ref, pv_bias_ref, cot_ref,
         kt_high, kt_low, v_high, v_low, query_ref, t1_ref, t2_ref, t1_rows, t2_rows,
-        vec_rows_ref, vecs_ref, w_ref,
+        vec_rows_ref, vecs_ref, mats_ref,
     ) = refs[2 + slots : 20 + slots]
     (
         even_ref, odd_ref, keep_ref, send_ref,
-        d_keys, d_values, c1, c2, cot_t, qt, d_qt, v_three,
+        d_keys, d_values, c1, c2, cot_t, qt, d_qt, v_three, w_ref, tokens, arrived,
     ) = refs[20 + slots :]
     rows, width = cot_ref.shape
     step = pl.program_id(0)
     size = width // 8
     lanes = lax.broadcasted_iota(jnp.int32, (1, 128), 1)
+    pairs = [(mats_ref.at[0, 0, :, pl.ds(0, 3 * width)], w_ref)]
+    pairs += [(ref, tokens.at[i]) for i, ref in enumerate(token_hbm)]
+    copies = [pltpu.make_async_copy(a, b, arrived.at[i]) for i, (a, b) in enumerate(pairs)]
 
     @pl.when(step == 0)
     def _():
+        for copy in copies:
+            copy.start()
         cot_t[...] = cot_ref[...].T
         qt[...] = query_ref[...].T
         d_qt[...] = jnp.zeros_like(d_qt)
@@ -673,12 +774,14 @@
 
     @pl.when(step == pl.num_programs(0) - 1)
     def _():
+        for copy in copies:
+            copy.wait()
         d_query = d_qt[...].T * size ** (-0.5)
         w_q, w_k, w_v = (split(w_ref[:, i * width : (i + 1) * width]) for i in range(3))
         gain = shift = g_k = g_v = 0.0
         for slot in range(slots):
             here = pl.ds(slot * rows, rows)
-            unit, _ = norm_rows(token_refs[slot][...])
+            unit, _ = norm_rows(tokens[slot])
             normed = split(unit * vecs_ref[0:1, :] + vecs_ref[1:2, :])
             dk, dv = split(d_keys[here, :]), split(d_values[here, :])
             piece = mm3(dk, w_k, NT) + mm3(dv, w_v, NT)
@@ -717,8 +820,9 @@
     slots, unroll = total // rows, 2 if total <= 1024 else 1
     operands = [*token_slots, *found, cot, *keys_values, query, *tables, vec_rows, vectors, matrices]
     specs = [whole(operand.shape) for operand in operands]
+    specs[:slots] = [anywhere()] * slots
     specs[slots : slots + 4] = [by_head(unroll, operand.shape) for operand in found[:4]]
-    specs[-1] = weight_block(0, 0, matrices.shape)
+    specs[-1] = anywhere()
     outs = [struct((slots // 2, rows, width))] * 2 + [struct((width, 640))] * 2
     return pl.pallas_call(
         functools.partial(backward_kernel, slots, lengths.shape[1], dp_size, unroll),
@@ -729,7 +833,12 @@
         scratch_shapes=[pltpu.VMEM((total, width), F32)] * 2
         + [pltpu.VMEM((width, 128), F32)] * 2
         + [pltpu.VMEM((width, rows), F32)] * 3
-        + [pltpu.VMEM((total, 3 * width), BF16)],
+        + [
+            pltpu.VMEM((total, 3 * width), BF16),
+            pltpu.VMEM((width, 3 * width), F32),
+            pltpu.VMEM((slots, rows, width), F32),
+            pltpu.SemaphoreType.DMA((1 + slots,)),
+        ],
         compiler_params=limit(KERNEL_MIB),
         cost_estimate=pl.CostEstimate(
             flops=6 * (4 * heads + 6) * total * rows * width, bytes_accessed=24 << 20, transcendentals=0
@@ -738,44 +847,53 @@
     )(place, lengths, *operands)
 
 
-def token_grad_kernel(tokens_ref, vecs_ref, near_ref, far_ref, tail_ref, grad_ref):
+def token_grad_kernel(tokens_ref, vecs_ref, own_ref, near_ref, far_ref, tail_ref, grad_ref):
     unit, scale = norm_rows(tokens_ref[...])
-    d_normed = near_ref[...] + far_ref[...]
+    d_normed = own_ref[...] + near_ref[...] + far_ref[...]
     grad_ref[...] = tail_ref[...] + norm_back(d_normed * vecs_ref[0:1, :], unit, scale)
 
 
-def token_grad(*operands):
-    tokens = operands[0]
+def token_grad(tokens, vectors, own, near, far, tail):
+    operands = [*far_off(tokens, vectors), own, near, far, *far_off(tail)]
     return pl.pallas_call(
         token_grad_kernel,
         out_shape=struct(tokens.shape),
-        compiler_params=limit(KERNEL_MIB),
+        compiler_params=limit(SMALL_MIB),
         cost_estimate=pl.CostEstimate(flops=1 << 21, bytes_accessed=2 << 20, transcendentals=0),
         name="token_grad",
     )(*operands)
 
 
-def squares_kernel(dp_size, place_ref, early_ref, late_ref, added_ref, class_ref, out_ref):
+def squares_kernel(dp_size, counts, *refs):
+    place_ref, added_ref, class_ref = refs[:3]
+    early_refs = refs[3 : 3 + counts[0]]
+    late_refs = refs[3 + counts[0] : 3 + sum(counts)]
+    out_ref, early_ref, late_ref = refs[3 + sum(counts) :]
     odd = jnp.bitwise_and(place_ref[0], 1) == 1
-    late = late_ref[...]
+    early = sum_of([ref[...] for ref in early_refs])
+    late = sum_of([ref[...] for ref in late_refs])
+    early_ref[...], late_ref[...] = early, late
     small = late[:, 512:] + jnp.where(odd, added_ref[...], 0.0)
     lane = lax.broadcasted_iota(jnp.int32, small.shape, 1)
     talk = jnp.logical_and(odd, jnp.logical_and(lane >= 28, lane < 45))
     small = small * small * jnp.where(talk, 1.0 / dp_size, 1.0)
     total = jnp.sum(small)
-    for value in (late[:, :512], early_ref[...]):
+    for value in (late[:, :512], early):
         total = total + jnp.sum(value * value)
     out_ref[...] = 0.5 * class_ref[...] + total
 
 
-def squares_of(dp_size, place, *operands):
-    vmem = pl.BlockSpec(memory_space=pltpu.VMEM)
+def squares_of(dp_size, place, added, class_squares, early, late):
+    operands = [added, class_squares, *early, *late]
+    outs = [struct((8, 128)), struct(early[0].shape), struct(late[0].shape)]
     return pl.pallas_call(
-        functools.partial(squares_kernel, dp_size),
-        in_specs=[smem()] + [vmem] * len(operands),
-        out_shape=struct((8, 128)),
-        compiler_params=limit(KERNEL_MIB),
-        cost_estimate=pl.CostEstimate(flops=1 << 18, bytes_accessed=1 << 19, transcendentals=0),
+        functools.partial(squares_kernel, dp_size, (len(early), len(late))),
+        grid=(1,),
+        in_specs=[smem()] + [whole(operand.shape) for operand in operands],
+        out_specs=[whole(out.shape) for out in outs],
+        out_shape=outs,
+        compiler_params=limit(SMALL_MIB),
+        cost_estimate=pl.CostEstimate(flops=1 << 18, bytes_accessed=1 << 20, transcendentals=0),
         name="squares",
     )(place, *operands)
 
@@ -789,7 +907,7 @@
     return (updated, first, second)
 
 
-def adam_kernel(*refs):
+def adam_kernel(sliced, *refs):
     (
         place_ref, squares_ref, early_own, early_other, late_own, late_other, added_ref,
         class_ref, w_ref, m1_ref, m2_ref, ema_ref, v_ref, v1_ref, v2_ref, v_ema_ref,
@@ -797,7 +915,7 @@
     ) = refs[:20]
     norm_ref, new_ref, first_ref, second_ref, average_ref = refs[20:25]
     v_outs, t_outs = refs[25:29], refs[29:33]
-    grads = refs[33]
+    grads, columns = refs[33:35]
     step = pl.program_id(0)
     norm = jnp.sqrt(squares_ref[0:1, 0:1])
     factor = jnp.minimum(1.0, CLIP_NORM / norm)
@@ -824,7 +942,14 @@
         grads[2] = early_right[:, :hidden]
         small = late_right[:, 512:] + added_ref[...]
         count = v_ref.shape[0]
-        store(v_outs, v_ref[...], small.T[:count, :], v1_ref[...], v2_ref[...], v_ema_ref[...], LR_VECTOR, 0.0)
+        if sliced:
+            columns[:, :count] = v_ref[...].T
+            share = small.shape[0]
+            begin = pl.multiple_of(place_ref[1] * share, share)
+            weight = columns[pl.ds(begin, share), :].T[:count, :]
+        else:
+            weight = v_ref[...]
+        store(v_outs, weight, small.T[:count, :], v1_ref[...], v2_ref[...], v_ema_ref[...], LR_VECTOR, 0.0)
         talk = small[:8, count : count + 17]
         store(t_outs, t_ref[...], talk, t1_ref[...], t2_ref[...], t_ema_ref[...], LR_TALKING, 0.0)
 
@@ -836,22 +961,29 @@
 
 def optimizer(place, squares, grads, class_share, mats, vecs, talks):
     shape = mats[1].shape
-    block = pl.BlockSpec((None, None) + shape[2:], lambda i: (i // 3, i % 3, 0, 0))
-    operands = [squares, *grads, class_share, *mats, *vecs, *talks]
+    sliced = mats[0].shape != shape
+    block = pl.BlockSpec((None, None) + shape[2:], lambda i, _: (i // 3, i % 3, 0, 0))
+    operands = [squares, *grads, class_share, *far_off(*mats, *vecs, *talks)]
     specs = [whole(operand.shape) for operand in operands]
-    specs[7:11] = [block] * 4
+    at = 3 + len(grads) - 1
+    specs[at : at + 4] = [block] * 4
+    if sliced:
+        specs[at] = pl.BlockSpec((None, None) + shape[2:], lambda i, ref: (i // 3, i % 3, ref[1], 0))
     outs = [struct((1, 1))] + [struct(shape)] * 4
-    outs += [struct(vecs[0].shape)] * 4 + [struct(talks[0].shape)] * 4
+    outs += [struct(vecs[1].shape)] * 4 + [struct(talks[0].shape)] * 4
     out_specs = [whole(out.shape) for out in outs]
     out_specs[1:5] = [block] * 4
     return pl.pallas_call(
-        adam_kernel,
-        grid=(6,),
-        in_specs=[smem()] + specs,
-        out_specs=out_specs,
+        functools.partial(adam_kernel, sliced),
+        grid_spec=pltpu.PrefetchScalarGridSpec(
+            num_scalar_prefetch=1,
+            grid=(6,),
+            in_specs=specs,
+            out_specs=out_specs,
+            scratch_shapes=[pltpu.VMEM((3,) + shape[2:], F32), pltpu.VMEM((vecs[0].shape[1], 128), F32)],
+        ),
         out_shape=outs,
-        scratch_shapes=[pltpu.VMEM((3,) + shape[2:], F32)],
-        compiler_params=limit(KERNEL_MIB),
+        compiler_params=limit(SMALL_MIB),
         cost_estimate=pl.CostEstimate(flops=1 << 23, bytes_accessed=14 << 20, transcendentals=0),
         name="optimizer",
     )(place, *operands)
@@ -865,43 +997,152 @@
     return [(axis, bit << i) for i in range((size // bit).bit_length() - 1)]
 
 
+class Places:
+    def __init__(self, dp_size, seq_size, row_share):
+        seq, dp = lax.axis_index("seq"), lax.axis_index("dp")
+        self.sizes = {"dp": dp_size, "seq": seq_size}
+        steps = bits_of("dp", dp_size) + bits_of("seq", seq_size)
+        names = {"dp": dp, "seq": seq}
+        bits = {step: jnp.bitwise_and(lax.shift_right_logical(names[step[0]], step[1].bit_length() - 1), 1) for step in steps}
+        self.found = {
+            "seq": seq.astype(jnp.int32).reshape(1),
+            "dp": dp.astype(jnp.int32).reshape(1),
+            "rows": (dp * row_share).astype(jnp.uint32),
+            "share": (bits["seq", 1] * (seq_size // 2) + lax.shift_right_logical(seq, 1)).astype(jnp.uint32),
+        }
+        for step, bit in bits.items():
+            self.found[step, "mine"] = bit.astype(jnp.uint32)
+            self.found[step, "other"] = (1 - bit).astype(jnp.uint32)
+            self.found[step, "low"] = bit == 0
+
+    def before(self, value):
+        names = list(self.found)
+        value, *found = together(value, *[self.found[name] for name in names])
+        self.found = dict(zip(names, found))
+        return value
+
+    def take(self, value, picks):
+        at = [jnp.uint32(0)] * value.ndim
+        sizes = list(value.shape)
+        for dim, (step, which) in picks.items():
+            at[dim] = self.found[step, which]
+            sizes[dim] = 1
+        return lax.squeeze(lax.dynamic_slice(value, at, sizes), tuple(picks))
+
+    def share(self, value, rows):
+        at = self.found["share"] * jnp.uint32(rows)
+        return lax.dynamic_slice(value, (at, jnp.uint32(0)), (rows, value.shape[1]))
+
+    def rows(self, value, size, dim):
+        at = [jnp.uint32(0)] * value.ndim
+        at[dim] = self.found["rows"]
+        sizes = list(value.shape)
+        sizes[dim] = size
+        return lax.dynamic_slice(value, at, sizes)
+
+    def swap(self, value, steps):
+        flip = sum(bit * (self.sizes["seq"] if axis == "dp" else 1) for axis, bit in steps)
+        count = self.sizes["dp"] * self.sizes["seq"]
+        return lax.ppermute(value, ("dp", "seq"), [(place, place ^ flip) for place in range(count)])
+
+    def pair(self, value, other, step):
+        low = self.found[step, "low"]
+        return [jnp.where(low, value, other), jnp.where(low, other, value)]
+
+
+def subsets(group):
+    found = [()]
+    for step in group:
+        found += [one + (step,) for one in found]
+    return found[1:]
+
+
 class Reduce:
-    def __init__(self, terms, dp_size, seq_size, order, y_first=False):
-        self.sizes = {"dp": dp_size, "seq": seq_size}
-        dp = bits_of("dp", dp_size)
-        chips = bits_of("seq", seq_size, 2)
-        order = [dp[i] for i in order] + dp[len(order) :]
-        self.left = dp[::-1] + (chips[::-1] if y_first else [])
-        self.steps = [(step, "half") for step in (chips if y_first else []) + order]
-        self.steps += [(step, "join" if y_first else "sum") for step in chips]
+    def __init__(self, terms, places, groups):
+        self.places, self.groups = places, list(groups)
+        self.left = bits_of("dp", places.sizes["dp"])[::-1]
         shape = (2,) * len(self.left) + (-1, terms[0].shape[1])
         self.terms = [term.reshape(shape) for term in terms]
-
-    def start(self):
-        step, kind = self.steps[0]
-        if kind != "half":
+        self.got = 0
+
+    def sends(self):
+        group = self.groups[0]
+        halves = [step for step in group if step[0] == "dp"]
+        dims = {step: self.left.index(step) for step in halves}
+        if not halves:
             self.terms = [sum_of(self.terms)]
-            return self.terms[0]
-        dim = self.left.index(step)
-        self.left.pop(dim)
-        mine = lax.axis_index(step[0]) // step[1] % 2
-        take = lambda term, index: lax.dynamic_index_in_dim(term, index, dim, keepdims=False)
-        sent = sum_of([take(term, 1 - mine) for term in self.terms])
-        self.terms = [take(term, mine) for term in self.terms]
+
+        def taken(others):
+            picks = {dims[step]: (step, "other" if step in others else "mine") for step in halves}
+            return [self.places.take(term, picks) if picks else term for term in self.terms]
+
+        sent = [sum_of(taken(others)) for others in subsets(group)]
+        self.terms = taken(())
+        self.left = [step for step in self.left if step not in halves]
         return sent
 
-    def swap(self, sent):
-        (axis, bit), kind = self.steps.pop(0)
-        other = swap(sent, axis, self.sizes[axis], bit)
-        if kind == "join":
-            low = lax.axis_index(axis) // bit % 2 == 0
-            pair = [jnp.where(low, sent, other), jnp.where(low, other, sent)]
-            self.terms = [jnp.concatenate(pair, axis=0)]
-        else:
-            self.terms.append(other)
+    def post(self, sent):
+        group = self.groups.pop(0)
+        self.got = len(sent)
+        self.terms += [self.places.swap(value, steps) for value, steps in zip(sent, subsets(group))]
+
+    def received(self):
+        return self.terms[len(self.terms) - self.got :]
+
+    def set_received(self, values):
+        self.terms[len(self.terms) - self.got :] = values
 
     def value(self):
         return sum_of(self.terms)
+
+
+class Gather:
+    def __init__(self, value, places):
+        self.places = places
+        dp = bits_of("dp", places.sizes["dp"])
+        self.value = value[None]
+        self.groups = [(step,) for step in dp[2:]] + [tuple(dp[:2])]
+        self.groups += [(step,) for step in bits_of("seq", places.sizes["seq"], 2) + bits_of("seq", 2)]
+
+    def sends(self):
+        return [self.value]
+
+    def post(self, sent):
+        self.value = sent[0]
+        self.others = [self.places.swap(self.value, steps) for steps in subsets(self.groups[0])]
+
+    def received(self):
+        return list(self.others)
+
+    def set_received(self, values):
+        group = self.groups.pop(0)
+        if group[0][0] == "dp":
+            self.value = jnp.concatenate([self.value, *values], axis=0)
+        else:
+            self.value = jnp.concatenate(self.places.pair(self.value, values[0], group[0]), axis=1)
+        self.others = []
+
+
+def settle(streams, *work):
+    streams = [stream for stream in streams if stream.received()]
+    counts = [len(stream.received()) for stream in streams]
+    found = together(*[value for stream in streams for value in stream.received()], *work)
+    at = 0
+    for stream, count in zip(streams, counts):
+        stream.set_received(list(found[at : at + count]))
+        at += count
+    return found[at:]
+
+
+def launch(streams, *after):
+    streams = [stream for stream in streams if stream.groups]
+    sent = [stream.sends() for stream in streams]
+    found = together(*[value for one in sent for value in one], *after)
+    at = 0
+    for stream, one in zip(streams, sent):
+        stream.post(list(found[at : at + len(one)]))
+        at += len(one)
+    return found[at:]
 
 
 def sum_of(terms):
@@ -917,27 +1158,6 @@
 
 def together(*values):
     return lax.optimization_barrier(values)
-
-
-class Gather:
-    def __init__(self, value, dp_size, seq_size):
-        self.sizes = {"dp": dp_size, "seq": seq_size}
-        self.value = value[None]
-        dp = bits_of("dp", dp_size)
-        self.steps = dp[2:] + dp[1:2] + dp[:1] + bits_of("seq", seq_size, 2) + bits_of("seq", 2)
-
-    def swap(self):
-        axis, bit = self.steps[0]
-        self.other = swap(self.value, axis, self.sizes[axis], bit)
-
-    def join(self):
-        axis, bit = self.steps.pop(0)
-        if axis == "dp":
-            self.value = jnp.concatenate([self.value, self.other], axis=0)
-        else:
-            low = lax.axis_index("seq") // bit % 2 == 0
-            pair = [jnp.where(low, self.value, self.other), jnp.where(low, self.other, self.value)]
-            self.value = jnp.concatenate(pair, axis=1)
 
 
 def on_device(
@@ -949,10 +1169,10 @@
 ):
     rows, width = tokens.shape
     images = class_tokens.shape[0]
-    seq_index = lax.axis_index("seq")
-    dp_index = lax.axis_index("dp")
-    place = seq_index.astype(jnp.int32).reshape(1)
     row_share = width // dp_size
+    places = Places(dp_size, seq_size, row_share)
+    tokens = places.before(tokens)
+    place = places.found["seq"]
 
     slots = {0: tokens}
     slots[1] = swap(tokens, "seq", seq_size, 1)
@@ -979,82 +1199,74 @@
         class_out, d_attended, d_mixed, early_keep, early_send, partial, factors, vec_rows, class_terms,
     ) = middle(
         place, parts, vectors, prepared, class_tokens, cot_class, cot_patch,
-        [patch_out, scores, attended, *kept], matrices,
-    )
-
-    early = Reduce([early_keep, swap(early_send, "seq", seq_size, 1)], dp_size, seq_size, (1, 0))
+        patch_out, scores, [attended, *kept], matrices,
+    )
+
+    core, chips, dp = ("seq", 1), bits_of("seq", seq_size, 2), bits_of("dp", dp_size)
+    pairs = lambda steps: [tuple(steps[i : i + 2]) for i in range(0, len(steps), 2)]
+    other = places.swap(early_send, [core])
     partials = [partial] + [swap(partial, "seq", seq_size, bit) for bit in range(1, seq_size)]
     grad_class, factors = class_finish(partials, class_terms, class_tokens, vectors, matrices, factors)
-    share = factors.shape[0] // seq_size
-    at = (seq_index % 2 * (seq_size // 2) + seq_index // 2) * share
-    gather = Gather(lax.dynamic_slice_in_dim(factors, at, share, 0), dp_size, seq_size)
-    sent, gather.value, d_attended = together(early.start(), gather.value, d_attended)
-    early.swap(sent)
-    gather.swap()
+    gather = Gather(places.share(factors, factors.shape[0] // seq_size), places)
+    other, gather.value = together(other, gather.value)
+    early = Reduce(
+        [early_keep, other], places, [tuple(dp[:2])] + [(step,) for step in dp[2:] + chips]
+    )
+    (later,) = launch([early, gather], place)
     even, odd, late_keep, late_send = backward(
-        dp_size, place, lengths, token_slots, [e_high, e_low, pv, inverse, pv_bias], d_attended,
+        dp_size, later, lengths, token_slots, [e_high, e_low, pv, inverse, pv_bias], d_attended,
         [kt_high, kt_low, v_high, v_low], query, [t1, t2, t1_rows, t2_rows], vec_rows, vectors, matrices,
     )
 
-    late_send, odd, gather.other, early.terms[-1] = together(
-        late_send, odd, gather.other, early.terms[-1]
-    )
-    late = Reduce([late_keep, swap(late_send, "seq", seq_size, 1)], dp_size, seq_size, (1, 0))
-    odd = swap(odd, "seq", seq_size, 1)
-    early.swap(early.start())
-    gather.join()
-    gather.swap()
-    sent = late.start()
-    late.swap(sent)
-    even = tie(even, sent)
-    chips = [even[i] + odd[i] for i in range(seq_size // 2)]
+    late_send, odd = settle([early, gather], late_send, odd)
+    late_other, odd = places.swap(late_send, [core]), places.swap(odd, [core])
+    late = Reduce([late_keep, late_other], places, pairs(dp + chips))
+    (late.terms[1],) = launch([early], late.terms[1])
+    (even,) = launch([late], even)
+    own = [even[0]] + [even[i] + odd[i] for i in range(1, seq_size // 2)]
+    near = odd[0]
     bit = 1
-    while 2 * bit < len(chips):
-        for slot in range(0, len(chips), 2 * bit):
-            chips[slot] = chips[slot] + swap(chips[slot + bit], "seq", seq_size, 2 * bit)
+    while 2 * bit < len(own):
+        for slot in range(0, len(own), 2 * bit):
+            own[slot] = own[slot] + swap(own[slot + bit], "seq", seq_size, 2 * bit)
         bit *= 2
-    far = swap(chips[bit], "seq", seq_size, 2 * bit)
-    weight_rows, vector_columns = (
-        lax.dynamic_slice_in_dim(tie(value, sent), dp_index * row_share, row_share, dim)
-        for value, dim in ((matrices, 2), (vectors, 1))
-    )
-    late.terms[-1], weight_rows, vector_columns = together(late.terms[-1], weight_rows, vector_columns)
-    class_share = None
-    while late.steps or early.steps or gather.steps:
-        after = []
-        if late.steps:
-            after = [late.start()]
-            late.swap(after[0])
-        if early.steps:
-            early.terms[-1] = tie(early.terms[-1], *after)
-            early.swap(early.start())
-        if gather.steps:
-            gather.join()
-            gather.value = tie(gather.value, *after)
-            if gather.steps:
-                gather.swap()
-                late.terms[-1], gather.other = together(late.terms[-1], gather.other)
-        if far is not None:
-            grad_tokens = token_grad(tokens, vectors, tie(chips[0], *after), far, d_mixed)
-            far = None
-            late.terms[-1], grad_tokens = together(late.terms[-1], grad_tokens)
-    factors = gather.value
-    mine = lax.dynamic_slice_in_dim(factors, dp_index * row_share, row_share, 2)
-    class_share, class_squares, added = class_weights(images, mine, factors)
-    late, early = late.value(), early.value()
-    squares = squares_of(dp_size, place, early, late, added, class_squares)
-    squares = squares + swap(squares, "seq", seq_size, 1)
-    bit = 1
-    while bit < dp_size:
-        squares = squares + swap(squares, "dp", dp_size, bit)
-        bit *= 2
+    far = swap(own[bit], "seq", seq_size, 2 * bit)
+    (own[bit],) = launch([gather], own[bit])
+    (own[bit],) = settle([gather], own[bit])
+    while len(gather.groups) > len(chips) + 1:
+        launch([gather])
+        settle([gather])
+    launch([gather], own[bit])
+    (far,) = settle([late, early], far)
+    (far,) = launch([late, early], far)
+    (far,) = settle([gather], far)
+    while gather.groups:
+        launch([gather])
+        settle([gather])
+    mine = places.rows(gather.value, row_share, 2)
+    class_share, class_squares, added = class_weights(images, mine, gather.value)
+    class_share, class_squares, added = settle([late, early], class_share, class_squares, added)
+    while late.groups or early.groups:
+        launch([late, early])
+        settle([late, early])
+    last = [[term.reshape(row_share, -1) for term in stream.terms] for stream in (early, late)]
+    squares, early, late = squares_of(dp_size, place, added, class_squares, *last)
+    sliced = row_share % 8 == 0
+    if not sliced:
+        matrices_rows, vectors_columns = places.rows(matrices, row_share, 2), places.rows(vectors, row_share, 1)
+    else:
+        matrices_rows, vectors_columns = matrices, vectors
+    far, squares = together(far, squares)
+    for group in pairs([core] + dp):
+        squares = sum_of([squares] + [places.swap(squares, steps) for steps in subsets(group)])
+    grad_tokens = token_grad(tokens, vectors, own[0], near, far, d_mixed)
     grads = []
     for value in (early, late):
-        grads += [value, swap(value, "seq", seq_size, 1)]
+        grads += [value, places.swap(value, [core])]
     norm, *updated = optimizer(
-        place, squares, [*grads, added], class_share,
-        [weight_rows, matrices_moment1, matrices_moment2, matrices_ema],
-        [vector_columns, vectors_moment1, vectors_moment2, vectors_ema],
+        jnp.concatenate([place, places.found["dp"]]), squares, [*grads, added], class_share,
+        [matrices_rows, matrices_moment1, matrices_moment2, matrices_ema],
+        [vectors_columns, vectors_moment1, vectors_moment2, vectors_ema],
         [talking, talking_moment1, talking_moment2, talking_ema],
     )
     return (patch_out, class_out, grad_tokens, grad_class, norm.reshape(()), *updated)

time: 237 us -> 198 us (0.84)
  waiting for transfers between devices: 58.1 us -> 38.6 us
  Pallas kernels: 118 us -> 103 us
  starting transfers between devices: 26.4 us -> 35 us
  local copies, waits for them, and re-layouts: 11 us -> 4.54 us
  other arithmetic: 18.8 us -> 12.4 us
    ppermute x32 -> x10, waiting for transfers between devices: 58.1 us -> 12.1 us  [swap(): lax.ppermute(value, axis, [(place, place ^ bit) for place in range(size)])]
    ppermute x0 -> x28, starting transfers between devices: none -> 26.9 us  [swap(): lax.ppermute(value, ('dp', 'seq'), [(place, place ^ flip) for place in ra...]
    ppermute x0 -> x28, waiting for transfers between devices: none -> 26.6 us  [swap(): lax.ppermute(value, ('dp', 'seq'), [(place, place ^ flip) for place in ra...]
    ppermute x32 -> x10, starting transfers between devices: 26.4 us -> 8.12 us  [swap(): lax.ppermute(value, axis, [(place, place ^ bit) for place in range(size)])]
    pallas_call x1, Pallas kernels: 31.7 us -> 25.8 us  [forward(): pl.pallas_call(functools.partial(forward_kernel, slots, lengths.shape[1],...]
    dynamic_slice x3 -> x0, local copies, waits for them, and re-layouts: 5.62 us -> none  [the longest x2 4.35 us: on_device(): lax.dynamic_slice_in_dim(tie(value, sent), dp_index * row_share, row_shar...]
    pallas_call x1, Pallas kernels: 22 us -> 16.6 us  [middle(): pl.pallas_call(functools.partial(middle_kernel, images, len(parts)), grid...]
    add x10 -> x7, other arithmetic: 12.3 us -> 7.43 us  [sum_of(): total = total + term]
  transfers between devices with their start and end apart: 32 -> 38, of which waited for: 16 -> 19; matrix products, arithmetic and copies ran while one was open for 10% -> 5% of each run, Pallas kernels for 24% -> 26%
where the time goes in v1:
time: 198 us; the launch traced here: 195 us
  Pallas kernels  103 us (52%)
  waiting for transfers between devices  38.6 us (19%)
  starting transfers between devices  35 us (18%)
  other arithmetic  12.4 us (6%)
  local copies, waits for them, and re-layouts  4.54 us (2%)
    pallas_call x1, Pallas kernels, backward(): pl.pallas_call(functools.partial(backward_kernel, slots, lengths.shape[1]...  36.4 us
    ppermute x28, starting transfers between devices, swap(): lax.ppermute(value, ('dp', 'seq'), [(place, place ^ flip) for place in ra...  26.9 us
    ppermute x28, waiting for transfers between devices, swap(): lax.ppermute(value, ('dp', 'seq'), [(place, place ^ flip) for place in ra...  26.6 us
    pallas_call x1, Pallas kernels, forward(): pl.pallas_call(functools.partial(forward_kernel, slots, lengths.shape[1],...  25.8 us
    pallas_call x1, Pallas kernels, middle(): pl.pallas_call(functools.partial(middle_kernel, images, len(parts)), grid...  16.6 us
    ppermute x10, waiting for transfers between devices, swap(): lax.ppermute(value, axis, [(place, place ^ bit) for place in range(size)])  12.1 us
    pallas_call x1, Pallas kernels, optimizer(): pl.pallas_call(functools.partial(adam_kernel, sliced), grid_spec=pltpu.Pr...  8.93 us
    ppermute x10, starting transfers between devices, swap(): lax.ppermute(value, axis, [(place, place ^ bit) for place in range(size)])  8.12 us
  transfers between devices with their start and end apart: 38, of which 19 were waited for; matrix products, arithmetic and copies ran while one was open for 5% of the time, Pallas kernels for 26%

profile of v1, /device:TPU:0, one launch (start us, length us, event | category | flops | bytes accessed | tf_op | source)
XLA Modules:
  0.0 194.8 jit_solution(12745300192711139957)
XLA Ops:
  1.2 2.6 %collective-permute-start.1 = (f32[256,384]{1,0:T(8,128)}, f32[256,384]{1,0:T(8,128)S(1)}, u32[]{:S(2)}, u32[]{:S(2)}) collective-permute-start(f32[256,384]{1,0:T(8,128)} %tokens_ref), channel_id=1, source_target_pairs={{0,2},{1,3},{2,0},{3,1},{4,6},{5,7},{6,4},{7,5},{8,10},{9,11},{10,... | collective-permute-start | bytes 1179656 | tf_op jit(solution)/shard_map/ppermute | solution.py:993
  4.5 6.9 %prepare.1 = (f32[4,384]{1,0:T(4,128)}, f32[4,384]{1,0:T(4,128)}, f32[4,384]{1,0:T(4,128)}, f32[32,384]{1,0:T(8,128)}, f32[32,128]{1,0:T(8,128)}, /*index=5*/f32...) custom-call(f32[256,384]{1,0:T(8,128)} %tokens_ref, ...), custom_call_target="tpu_custom_call" | custom-call | flops 4294967296 | bytes 8388608 | tf_op jit(solution)/shard_map/prepare/pallas_call | solution.py:268
  11.4 2.3 %collective-permute-done.1.refs_4_ = f32[256,384]{1,0:T(8,128)S(1)} collective-permute-done((f32[256,384]{1,0:T(8,128)}, f32[256,384]{1,0:T(8,128)S(1)}, u32[]{:S(2)}, u32[]{:S(2)}) %collective-permute-start.1) | collective-permute-done | bytes 393248 | tf_op jit(solution)/shard_map/ppermute | solution.py:993
  13.7 1.7 collective-permute-done.2.refs_5_
  16.2 25.8 %forward.1 = (bf16[8,1024,256]{2,1,0:T(8,128)(2,1)}, bf16[8,1024,256]{2,1,0:T(8,128)(2,1)}, f32[8,384,256]{2,1,0:T(8,128)}, f32[8,1,256]{2,1,0:T(1,128)}, f32[38...) custom-call(s32[1]{0:T(128)} %bitcast.refs_0_, ...), custom_call_target="tpu_custom_call" | custom-call | flops 12306087936 | bytes 25165824 | tf_op jit(solution)/shard_map/forward/pallas_call | solution.py:430
  42.2 1.7 collective-permute-start.4
  44.0 2.8 %collective-permute-done.4.refs_3_ = f32[32,512]{1,0:T(8,128)S(1)} collective-permute-done((f32[32,512]{1,0:T(8,128)}, f32[32,512]{1,0:T(8,128)S(1)}, u32[]{:S(2)}, u32[]{:S(2)}) %collective-permute-start.4) | collective-permute-done | bytes 65568 | tf_op jit(solution)/shard_map/ppermute | solution.py:993
  48.9 16.6 %middle.1 = (f32[4,384]{1,0:T(4,128)}, f32[256,384]{1,0:T(8,128)}, f32[256,384]{1,0:T(8,128)}, f32[384,1792]{1,0:T(8,128)}, f32[384,1792]{1,0:T(8,128)}, /*index...) custom-call(s32[1]{0:T(128)} %bitcast.refs_0_, f32[32,512]{1,0:T(8,128)} %get-tuple-element.161.refs_1_, ...), custom_call_target="tpu_custom_call" | custom-call | flops 8589934592 | bytes 29360128 | tf_op jit(solution)/shard_map/middle/pallas_call | solution.py:604
  67.6 2.9 %collective-permute-done.7.refs_1_ = f32[32,384]{1,0:T(8,128)S(1)} collective-permute-done((f32[32,384]{1,0:T(8,128)}, f32[32,384]{1,0:T(8,128)S(1)}, u32[]{:S(2)}, u32[]{:S(2)}) %collective-permute-start.7) | collective-permute-done | bytes 49184 | tf_op jit(solution)/shard_map/ppermute | solution.py:993
  72.2 2.7 %class_finish.1 = (f32[4,384]{1,0:T(4,128)}, f32[136,384]{1,0:T(8,128)S(1)}) custom-call(f32[32,384]{1,0:T(8,128)S(1)} %copy-done.2, f32[32,384]{1,0:T(8,128)S(1)} %collective-permute-done.7.refs_1_, f32[32,384]{1,0:T(8,128)S(1)} %collective-permute-done.8.refs_2_, f32[32,384]{1,0:T(8,128)S(1)} %collective-permute-done.9.refs_3_, ...), custom_call_target="tpu_custom_call" | custom-call | flops 536870912 | bytes 3145728 | tf_op jit(solution)/shard_map/class_finish/pallas_call | solution.py:651
  74.9 1.8 add_bitcast_fusion
  80.2 2.5 %collective-permute-start.13 = (f32[1,34,384]{2,1,0:T(8,128)S(1)}, f32[1,34,384]{2,1,0:T(8,128)S(1)}, u32[]{:S(2)}, u32[]{:S(2)}) collective-permute-start(f32[1,34,384]{2,1,0:T(8,128)S(1)} %dynamic-slice_bitcast_fusion.5), channel_id=1, source_target_pairs={{0,16},{1,17},{2,18},{3,19},{4,20},{5,21},{6,22},{7,23},{8,24},{9,... | collective-permute-start | bytes 156680 | tf_op jit(solution)/shard_map/ppermute | solution.py:1046
  82.7 36.4 %backward.1 = (f32[2,256,384]{2,1,0:T(8,128)}, f32[2,256,384]{2,1,0:T(8,128)}, f32[384,640]{1,0:T(8,128)}, f32[384,640]{1,0:T(8,128)}) custom-call(s32[1]{0:T(128)} %bitcast.refs_0_, s32[1,4]{1,0:T(1,128)} %refs_1_.3, f32[256,384]{1,0:T(8,128)} %tokens_ref, f32[256,384]{1,0:T(8,128)} %copy-done.7, f32[256,384]{1,0:T(8,128)} %copy-done.8, ...), custom_call_target="tpu_custom_call" | custom-call | flops 22951231488 | bytes 25165824 | tf_op jit(solution)/shard_map/backward/pallas_call | solution.py:827
  131.0 1.7 collective-permute-start.20
  132.7 3.7 %collective-permute-done.17 = f32[2,34,384]{2,1,0:T(8,128)} collective-permute-done((f32[2,34,384]{2,1,0:T(8,128)S(1)}, f32[2,34,384]{2,1,0:T(8,128)}, u32[]{:S(2)}, u32[]{:S(2)}) %collective-permute-start.17) | collective-permute-done | bytes 104480 | tf_op jit(solution)/shard_map/ppermute | solution.py:1046
  141.0 9.1 %collective-permute-done.21 = f32[2,48,640]{2,1,0:T(8,128)} collective-permute-done((f32[2,48,640]{2,1,0:T(8,128)S(1)}, f32[2,48,640]{2,1,0:T(8,128)}, u32[]{:S(2)}, u32[]{:S(2)}) %collective-permute-start.21) | collective-permute-done | bytes 245792 | tf_op jit(solution)/shard_map/ppermute | solution.py:1046
  150.1 2.8 %collective-permute-done.22 = f32[2,48,640]{2,1,0:T(8,128)} collective-permute-done((f32[2,48,640]{2,1,0:T(8,128)S(1)}, f32[2,48,640]{2,1,0:T(8,128)}, u32[]{:S(2)}, u32[]{:S(2)}) %collective-permute-start.22) | collective-permute-done | bytes 245792 | tf_op jit(solution)/shard_map/ppermute | solution.py:1046
  158.6 3.0 %collective-permute-start.27 = (f32[48,640]{1,0:T(8,128)S(1)}, f32[48,640]{1,0:T(8,128)S(1)}, u32[]{:S(2)}, u32[]{:S(2)}) collective-permute-start(f32[48,640]{1,0:T(8,128)S(1)} %get-tuple-element.236), channel_id=1, source_target_pairs={{0,18},{1,19},{2,16},{3,17},{4,22},{5,23},{6,20},{7,21},{8,26},{9,... | collective-permute-start | bytes 368648 | tf_op jit(solution)/shard_map/ppermute | solution.py:1046
  164.2 3.2 %class_weights.1 = (f32[3,48,1536]{2,1,0:T(8,128)}, f32[8,128]{1,0:T(8,128)}, f32[48,128]{1,0:T(8,128)}) custom-call(f32[8,136,48]{2,1,0:T(8,128)} %fusion.mine_ref, f32[8,136,384]{2,1,0:T(8,128)} %pad_maximum_fusion.factors_ref), custom_call_target="tpu_custom_call" | custom-call | flops 536870912 | bytes 3145728 | tf_op jit(solution)/shard_map/class_weights/pallas_call | solution.py:697
  167.4 2.1 %collective-permute-done.25.refs_10_ = f32[48,640]{1,0:T(8,128)S(1)} collective-permute-done((f32[48,640]{1,0:T(8,128)S(1)}, f32[48,640]{1,0:T(8,128)S(1)}, u32[]{:S(2)}, u32[]{:S(2)}) %collective-permute-start.25) | collective-permute-done | bytes 122912 | tf_op jit(solution)/shard_map/ppermute | solution.py:1046
  170.1 1.8 collective-permute-done.27.refs_12_
  180.2 2.4 %collective-permute-start.35 = (f32[8,128]{1,0:T(8,128)S(1)}, f32[8,128]{1,0:T(8,128)S(1)}, u32[]{:S(2)}, u32[]{:S(2)}) collective-permute-start(f32[8,128]{1,0:T(8,128)S(1)} %add_add_fusion.2), channel_id=1, source_target_pairs={{0,24},{1,25},{2,26},{3,27},{4,28},{5,29},{6,30},{7,31},{8,16},{9,... | collective-permute-start | bytes 12296 | tf_op jit(solution)/shard_map/ppermute | solution.py:1046
  182.7 2.2 %token_grad.1 = f32[256,384]{1,0:T(8,128)} custom-call(f32[256,384]{1,0:T(8,128)} %tokens_ref, f32[28,384]{1,0:T(8,128)} %refs_12_.3, f32[256,384]{1,0:T(8,128)S(1)} %get-tuple-element.291.own_ref, f32[256,384]{1,0:T(8,128)S(1)} %get-tuple-element.292.near_ref, f32[256,384]{1,0:T(8,128)S(1)} %collective-permute-done.24.far_ref, ...), custom_call_target="tpu_custom_call" | custom-call | flops 2097152 | bytes 2097152 | tf_op jit(solution)/shard_map/token_grad/pallas_call | solution.py:858
  185.6 8.9 %optimizer.1 = (f32[1,1]{1,0:T(1,128)}, f32[2,3,48,1536]{3,2,1,0:T(8,128)}, f32[2,3,48,1536]{3,2,1,0:T(8,128)}, f32[2,3,48,1536]{3,2,1,0:T(8,128)}, f32[2,3,48,1...) custom-call(s32[2]{0:T(128)S(1)} %pad_add_fusion.refs_0_, ...), custom_call_target="tpu_custom_call" | custom-call | flops 8388608 | bytes 14680064 | tf_op jit(solution)/shard_map/optimizer/pallas_call | solution.py:976
  (105 shorter events, 45.8 us)
Async XLA Ops:
  1.2 12.5 %collective-permute-start.1 = (f32[256,384]{1,0:T(8,128)}, f32[256,384]{1,0:T(8,128)S(1)}, u32[]{:S(2)}, u32[]{:S(2)}) collective-permute-start(f32[256,384]{1,0:T(8,128)} %tokens_ref), channel_id=1, source_target_pairs={{0,2},{1,3},{2,0},{3,1},{4,6},{5,7},{6,4},{7,5},{8,10},{9,11},{10,... | collective-permute-start | bytes 1179656 | tf_op jit(solution)/shard_map/ppermute | solution.py:993
  65.5 9.4 %collective-permute-start.6 = (f32[384,1792]{1,0:T(8,128)}, f32[384,1792]{1,0:T(8,128)}, u32[]{:S(2)}, u32[]{:S(2)}) collective-permute-start(f32[384,1792]{1,0:T(8,128)} %get-tuple-element.177), channel_id=1, source_target_pairs={{0,1},{1,0},{2,3},{3,2},{4,5},{5,4},{6,7},{7,6},{8,9},{9,8},{10,11... | collective-permute-start | bytes 8257544 | tf_op jit(solution)/shard_map/ppermute | solution.py:1046
  76.7 42.5 %collective-permute-start.10 = (f32[2,48,1792]{2,1,0:T(8,128)S(1)}, f32[2,48,1792]{2,1,0:T(8,128)}, u32[]{:S(2)}, u32[]{:S(2)}) collective-permute-start(f32[2,48,1792]{2,1,0:T(8,128)S(1)} %get-tuple-element.203), channel_id=1, source_target_pairs={{0,4},{1,5},{2,6},{3,7},{4,0},{5,1},{6,2},{7,3},{8,12},{9,13},{10,... | collective-permute-start | bytes 2064392 | tf_op jit(solution)/shard_map/ppermute | solution.py:1046
  78.1 41.1 %collective-permute-start.11 = (f32[2,48,1792]{2,1,0:T(8,128)S(1)}, f32[2,48,1792]{2,1,0:T(8,128)}, u32[]{:S(2)}, u32[]{:S(2)}) collective-permute-start(f32[2,48,1792]{2,1,0:T(8,128)S(1)} %get-tuple-element.204), channel_id=1, source_target_pairs={{0,8},{1,9},{2,10},{3,11},{4,12},{5,13},{6,14},{7,15},{8,0},{9,1},... | collective-permute-start | bytes 2064392 | tf_op jit(solution)/shard_map/ppermute | solution.py:1046
  79.7 39.5 %collective-permute-start.12 = (f32[2,48,1792]{2,1,0:T(8,128)S(1)}, f32[2,48,1792]{2,1,0:T(8,128)}, u32[]{:S(2)}, u32[]{:S(2)}) collective-permute-start(f32[2,48,1792]{2,1,0:T(8,128)S(1)} %get-tuple-element.205), channel_id=1, source_target_pairs={{0,12},{1,13},{2,14},{3,15},{4,8},{5,9},{6,10},{7,11},{8,4},{9,5},... | collective-permute-start | bytes 2064392 | tf_op jit(solution)/shard_map/ppermute | solution.py:1046
  80.2 38.9 %collective-permute-start.13 = (f32[1,34,384]{2,1,0:T(8,128)S(1)}, f32[1,34,384]{2,1,0:T(8,128)S(1)}, u32[]{:S(2)}, u32[]{:S(2)}) collective-permute-start(f32[1,34,384]{2,1,0:T(8,128)S(1)} %dynamic-slice_bitcast_fusion.5), channel_id=1, source_target_pairs={{0,16},{1,17},{2,18},{3,19},{4,20},{5,21},{6,22},{7,23},{8,24},{9,... | collective-permute-start | bytes 156680 | tf_op jit(solution)/shard_map/ppermute | solution.py:1046
  124.7 28.2 %collective-permute-start.24 = (f32[256,384]{1,0:T(8,128)S(1)}, f32[256,384]{1,0:T(8,128)S(1)}, u32[]{:S(2)}, u32[]{:S(2)}) collective-permute-start(f32[256,384]{1,0:T(8,128)S(1)} %get-tuple-element.290), channel_id=1, source_target_pairs={{0,2},{1,3},{2,0},{3,1},{4,6},{5,7},{6,4},{7,5},{8,10},{9,11},{10,... | collective-permute-start | bytes 1179656 | tf_op jit(solution)/shard_map/ppermute | solution.py:993
  125.8 5.1 %collective-permute-start.16 = (f32[2,34,384]{2,1,0:T(8,128)S(1)}, f32[2,34,384]{2,1,0:T(8,128)S(1)}, u32[]{:S(2)}, u32[]{:S(2)}) collective-permute-start(f32[2,34,384]{2,1,0:T(8,128)S(1)} %pad_maximum_fusion.3), channel_id=1, source_target_pairs={{0,4},{1,5},{2,6},{3,7},{4,0},{5,1},{6,2},{7,3},{8,12},{9,13},{10,... | collective-permute-start | bytes 313352 | tf_op jit(solution)/shard_map/ppermute | solution.py:1046
  127.4 9.1 %collective-permute-start.17 = (f32[2,34,384]{2,1,0:T(8,128)S(1)}, f32[2,34,384]{2,1,0:T(8,128)}, u32[]{:S(2)}, u32[]{:S(2)}) collective-permute-start(f32[2,34,384]{2,1,0:T(8,128)S(1)} %pad_maximum_fusion.3), channel_id=1, source_target_pairs={{0,8},{1,9},{2,10},{3,11},{4,12},{5,13},{6,14},{7,15},{8,0},{9,1},... | collective-permute-start | bytes 313352 | tf_op jit(solution)/shard_map/ppermute | solution.py:1046
  128.9 8.5 %collective-permute-start.18 = (f32[2,34,384]{2,1,0:T(8,128)S(1)}, f32[2,34,384]{2,1,0:T(8,128)}, u32[]{:S(2)}, u32[]{:S(2)}) collective-permute-start(f32[2,34,384]{2,1,0:T(8,128)S(1)} %pad_maximum_fusion.3), channel_id=1, source_target_pairs={{0,12},{1,13},{2,14},{3,15},{4,8},{5,9},{6,10},{7,11},{8,4},{9,5},... | collective-permute-start | bytes 313352 | tf_op jit(solution)/shard_map/ppermute | solution.py:1046
  129.4 23.5 %collective-permute-start.23 = (f32[48,1792]{1,0:T(8,128)S(1)}, f32[48,1792]{1,0:T(8,128)S(1)}, u32[]{:S(2)}, u32[]{:S(2)}) collective-permute-start(f32[48,1792]{1,0:T(8,128)S(1)} %bitcast_add_fusion.3), channel_id=1, source_target_pairs={{0,16},{1,17},{2,18},{3,19},{4,20},{5,21},{6,22},{7,23},{8,24},{9,... | collective-permute-start | bytes 1032200 | tf_op jit(solution)/shard_map/ppermute | solution.py:1046
  131.0 9.1 %collective-permute-start.20 = (f32[2,48,640]{2,1,0:T(8,128)S(1)}, f32[2,48,640]{2,1,0:T(8,128)S(1)}, u32[]{:S(2)}, u32[]{:S(2)}) collective-permute-start(f32[2,48,640]{2,1,0:T(8,128)S(1)} %get-tuple-element.222), channel_id=1, source_target_pairs={{0,4},{1,5},{2,6},{3,7},{4,0},{5,1},{6,2},{7,3},{8,12},{9,13},{10,... | collective-permute-start | bytes 737288 | tf_op jit(solution)/shard_map/ppermute | solution.py:1046
  136.4 13.6 %collective-permute-start.21 = (f32[2,48,640]{2,1,0:T(8,128)S(1)}, f32[2,48,640]{2,1,0:T(8,128)}, u32[]{:S(2)}, u32[]{:S(2)}) collective-permute-start(f32[2,48,640]{2,1,0:T(8,128)S(1)} %get-tuple-element.223), channel_id=1, source_target_pairs={{0,8},{1,9},{2,10},{3,11},{4,12},{5,13},{6,14},{7,15},{8,0},{9,1},... | collective-permute-start | bytes 737288 | tf_op jit(solution)/shard_map/ppermute | solution.py:1046
  137.5 15.4 %collective-permute-start.22 = (f32[2,48,640]{2,1,0:T(8,128)S(1)}, f32[2,48,640]{2,1,0:T(8,128)}, u32[]{:S(2)}, u32[]{:S(2)}) collective-permute-start(f32[2,48,640]{2,1,0:T(8,128)S(1)} %get-tuple-element.224), channel_id=1, source_target_pairs={{0,12},{1,13},{2,14},{3,15},{4,8},{5,9},{6,10},{7,11},{8,4},{9,5},... | collective-permute-start | bytes 737288 | tf_op jit(solution)/shard_map/ppermute | solution.py:1046
  140.0 15.8 %collective-permute-start.19 = (f32[8,34,384]{2,1,0:T(8,128)S(1)}, f32[8,34,384]{2,1,0:T(8,128)S(1)}, u32[]{:S(2)}, u32[]{:S(2)}) collective-permute-start(f32[8,34,384]{2,1,0:T(8,128)S(1)} %pad_maximum_fusion.2), channel_id=1, source_target_pairs={{0,2},{1,3},{2,0},{3,1},{4,6},{5,7},{6,4},{7,5},{8,10},{9,11},{10,... | collective-permute-start | bytes 1253384 | tf_op jit(solution)/shard_map/ppermute | solution.py:1046
  156.1 5.5 %collective-permute-start.29 = (f32[8,68,384]{2,0,1:T(8,128)S(1)}, f32[8,68,384]{2,0,1:T(8,128)S(1)}, u32[]{:S(2)}, u32[]{:S(2)}) collective-permute-start(f32[8,68,384]{2,0,1:T(8,128)S(1)} %copy.34), channel_id=1, source_target_pairs={{0,1},{1,0},{2,3},{3,2},{4,5},{5,4},{6,7},{7,6},{8,9},{9,8},{10,11... | collective-permute-start | bytes 2506760 | tf_op jit(solution)/shard_map/ppermute | solution.py:1046
  156.2 15.7 %collective-permute-start.28 = (f32[48,1792]{1,0:T(8,128)S(1)}, f32[48,1792]{1,0:T(8,128)S(1)}, u32[]{:S(2)}, u32[]{:S(2)}) collective-permute-start(f32[48,1792]{1,0:T(8,128)S(1)} %fusion.2.refs_3_), channel_id=1, source_target_pairs={{0,2},{1,3},{2,0},{3,1},{4,6},{5,7},{6,4},{7,5},{8,10},{9,11},{10,... | collective-permute-start | bytes 1032200 | tf_op jit(solution)/shard_map/ppermute | solution.py:1046
  157.2 12.3 %collective-permute-start.25 = (f32[48,640]{1,0:T(8,128)S(1)}, f32[48,640]{1,0:T(8,128)S(1)}, u32[]{:S(2)}, u32[]{:S(2)}) collective-permute-start(f32[48,640]{1,0:T(8,128)S(1)} %get-tuple-element.236), channel_id=1, source_target_pairs={{0,16},{1,17},{2,18},{3,19},{4,20},{5,21},{6,22},{7,23},{8,24},{9,... | collective-permute-start | bytes 368648 | tf_op jit(solution)/shard_map/ppermute | solution.py:1046
  157.6 12.4 %collective-permute-start.26 = (f32[48,640]{1,0:T(8,128)S(1)}, f32[48,640]{1,0:T(8,128)S(1)}, u32[]{:S(2)}, u32[]{:S(2)}) collective-permute-start(f32[48,640]{1,0:T(8,128)S(1)} %get-tuple-element.235), channel_id=1, source_target_pairs={{0,2},{1,3},{2,0},{3,1},{4,6},{5,7},{6,4},{7,5},{8,10},{9,11},{10,... | collective-permute-start | bytes 368648 | tf_op jit(solution)/shard_map/ppermute | solution.py:1046
  158.6 13.3 %collective-permute-start.27 = (f32[48,640]{1,0:T(8,128)S(1)}, f32[48,640]{1,0:T(8,128)S(1)}, u32[]{:S(2)}, u32[]{:S(2)}) collective-permute-start(f32[48,640]{1,0:T(8,128)S(1)} %get-tuple-element.236), channel_id=1, source_target_pairs={{0,18},{1,19},{2,16},{3,17},{4,22},{5,23},{6,20},{7,21},{8,26},{9,... | collective-permute-start | bytes 368648 | tf_op jit(solution)/shard_map/ppermute | solution.py:1046
  175.6 10.0 %collective-permute-start.36 = (f32[48,1792]{1,0:T(8,128)S(1)}, f32[48,1792]{1,0:T(8,128)S(1)}, u32[]{:S(2)}, u32[]{:S(2)}) collective-permute-start(f32[48,1792]{1,0:T(8,128)S(1)} %get-tuple-element.257.refs_2_), channel_id=1, source_target_pairs={{0,1},{1,0},{2,3},{3,2},{4,5},{5,4},{6,7},{7,6},{8,9},{9,8},{10,11... | collective-permute-start | bytes 1032200 | tf_op jit(solution)/shard_map/ppermute | solution.py:1046
  178.2 6.7 %collective-permute-start.33 = (f32[8,128]{1,0:T(8,128)S(1)}, f32[8,128]{1,0:T(8,128)S(1)}, u32[]{:S(2)}, u32[]{:S(2)}) collective-permute-start(f32[8,128]{1,0:T(8,128)S(1)} %add_add_fusion.2), channel_id=1, source_target_pairs={{0,8},{1,9},{2,10},{3,11},{4,12},{5,13},{6,14},{7,15},{8,0},{9,1},... | collective-permute-start | bytes 12296 | tf_op jit(solution)/shard_map/ppermute | solution.py:1046
  179.9 5.0 %collective-permute-start.34 = (f32[8,128]{1,0:T(8,128)S(1)}, f32[8,128]{1,0:T(8,128)S(1)}, u32[]{:S(2)}, u32[]{:S(2)}) collective-permute-start(f32[8,128]{1,0:T(8,128)S(1)} %add_add_fusion.2), channel_id=1, source_target_pairs={{0,16},{1,17},{2,18},{3,19},{4,20},{5,21},{6,22},{7,23},{8,24},{9,... | collective-permute-start | bytes 12296 | tf_op jit(solution)/shard_map/ppermute | solution.py:1046
  180.2 5.4 %collective-permute-start.35 = (f32[8,128]{1,0:T(8,128)S(1)}, f32[8,128]{1,0:T(8,128)S(1)}, u32[]{:S(2)}, u32[]{:S(2)}) collective-permute-start(f32[8,128]{1,0:T(8,128)S(1)} %add_add_fusion.2), channel_id=1, source_target_pairs={{0,24},{1,25},{2,26},{3,27},{4,28},{5,29},{6,30},{7,31},{8,16},{9,... | collective-permute-start | bytes 12296 | tf_op jit(solution)/shard_map/ppermute | solution.py:1046
  (27 other events, 80.7 us)

commit v2 on v1

--- a/solution.py
+++ b/solution.py
@@ -24,7 +24,7 @@
 NN = (((1,), (0,)), ((), ()))
 NT = (((1,), (1,)), ((), ()))
 TN = (((0,), (0,)), ((), ()))
-KERNEL_MIB, SMALL_MIB = 58, 24
+KERNEL_MIB, NEAR_MIB, SMALL_MIB = 58, 52, 24
 
 
 def split(value):
@@ -178,6 +178,10 @@
     return jax.ShapeDtypeStruct(shape, dtype)
 
 
+def far_struct(shape, dtype=F32):
+    return pltpu.HBM(shape, dtype)
+
+
 def smem():
     return pl.BlockSpec(memory_space=pltpu.SMEM)
 
@@ -215,12 +219,13 @@
     size = width // heads
     scale = size ** (-0.5)
     vecs = vecs_ref[...]
-    w_q, w_k, w_v = (split(w_self_ref[:, i * width : (i + 1) * width]) for i in range(3))
+    w_q, w_kv = split(w_self_ref[:, :width]), split(w_self_ref[:, width:])
     tokens = jnp.concatenate([own_ref[...], near_ref[...]], axis=0)
     unit, _ = norm_rows(tokens)
     normed = split(unit * vecs[0:1] + vecs[1:2])
     query_ref[...] = (mm3((normed[0][:rows], normed[1][:rows]), w_q) + vecs[2:3]) * scale
-    keys, values = mm3(normed, w_k), mm3(normed, w_v) + vecs[3:4]
+    both = mm3(normed, w_kv)
+    keys, values = both[:, :width], both[:, width:] + vecs[3:4]
     k_high[...], k_low[...] = split(keys)
     v_high[...], v_low[...] = split(values)
     kt_high[...], kt_low[...] = split(keys.T)
@@ -253,13 +258,13 @@
     rows = own.shape[0]
     heads = talking.shape[0]
     pairs = images * heads
-    outs = [struct((images, width))] * 3 + [
-        struct((pairs, width)), struct((pairs, 128)),
-        struct((width, heads)), struct((width, heads + 1)),
-        struct((heads, width)), struct((heads + 1, width)),
-        struct((rows, width)),
+    outs = [far_struct((images, width))] * 3 + [
+        far_struct((pairs, width)), far_struct((pairs, 128)),
+        far_struct((width, heads)), far_struct((width, heads + 1)),
+        far_struct((heads, width)), far_struct((heads + 1, width)),
+        far_struct((rows, width)),
     ]
-    outs += [struct((2 * rows, width), BF16)] * 4 + [struct((width, 2 * rows), BF16)] * 4
+    outs += [far_struct((2 * rows, width), BF16)] * 4 + [far_struct((width, 2 * rows), BF16)] * 4
     own, class_tokens, matrices, vectors, talking = far_off(own, class_tokens, matrices, vectors, talking)
     operands = [own, near, class_tokens, matrices, matrices, vectors, talking]
     specs = [whole(operand.shape) for operand in operands]
@@ -271,7 +276,7 @@
         in_specs=specs,
         out_specs=[whole(out.shape) for out in outs],
         out_shape=outs,
-        compiler_params=limit(KERNEL_MIB),
+        compiler_params=limit(NEAR_MIB),
         cost_estimate=pl.CostEstimate(flops=4 << 30, bytes_accessed=8 << 20, transcendentals=0),
         name="prepare",
     )(*operands)
@@ -279,7 +284,7 @@
 
 def forward_kernel(slots, images, unroll, *refs):
     place_ref, lengths_ref = refs[:2]
-    token_refs = refs[2 : 2 + slots]
+    token_refs = refs[2 : 1 + slots]
     (
         vecs_ref, t1_ref, t2_ref, key_rows_ref, query_ref,
         k_high0, k_low0, v_high0, v_low0, kt_high0, kt_low0, vt_high0, vt_low0, mats_ref,
@@ -288,7 +293,7 @@
         patch_ref, projected_ref, mixed_ref, hidden_hbm, slope_hbm, lowered_ref, packed_ref, scores_ref,
         k_three, vt_two, qt, bias, attended_t, w_kv, w_up, w_down, w_out, arrived,
         kt_high, kt_low, v_high, v_low, hidden_ref, slope_ref, e_high_ref, e_low_ref, pv_ref, leaving,
-    ) = refs[2 + slots :]
+    ) = refs[1 + slots :]
     rows, width = token_refs[0].shape
     step = pl.program_id(0)
     place = place_ref[0]
@@ -323,13 +328,14 @@
         inside = same_image(lengths_ref, images, place, slots, rows)
         for slot in range(slots):
             bias[pl.ds(slot * rows, rows), :] = jnp.where(inside[slot], 0.0, MASKED)
-        units = [norm_rows(ref[...])[0] for ref in token_refs[2:]]
+        units = [norm_rows(ref[...])[0] for ref in token_refs[1:]]
         fetches[0].wait()
-        w_k, w_v = split(w_kv[:, :width]), split(w_kv[:, width:])
+        w_both = split(w_kv[...])
         for slot in range(2, slots):
             here = pl.ds(slot * rows, rows)
             normed = split(units[slot - 2] * vecs[0:1] + vecs[1:2])
-            keys, values = mm3(normed, w_k), mm3(normed, w_v) + vecs[3:4]
+            both = mm3(normed, w_both)
+            keys, values = both[:, :width], both[:, width:] + vecs[3:4]
             high, low = split(keys)
             k_three[here, :] = jnp.concatenate([high, high, low], axis=1)
             v_high[here, :], v_low[here, :] = split(values)
@@ -413,17 +419,17 @@
     hidden = matrices.shape[3]
     pairs = key_rows.shape[0]
     outs = [
-        struct((heads, total, rows), BF16), struct((heads, total, rows), BF16), struct((heads, width, rows)),
-        struct((heads, 1, rows)), struct((width, rows)), struct((rows, width)),
-        struct((width, total), BF16), struct((width, total), BF16),
-        struct((total, width), BF16), struct((total, width), BF16),
-        struct((rows, width)), struct((rows, width)), struct((rows, width)),
-        struct((rows, hidden)), struct((rows, hidden)), struct((rows, width)),
-        struct((pairs, width + 128)), struct((pairs, rows)),
+        far_struct((heads, total, rows), BF16), far_struct((heads, total, rows), BF16), far_struct((heads, width, rows)),
+        far_struct((heads, 1, rows)), far_struct((width, rows)), far_struct((rows, width)),
+        far_struct((width, total), BF16), far_struct((width, total), BF16),
+        far_struct((total, width), BF16), far_struct((total, width), BF16),
+        far_struct((rows, width)), far_struct((rows, width)), far_struct((rows, width)),
+        far_struct((rows, hidden)), far_struct((rows, hidden)), far_struct((rows, width)),
+        far_struct((pairs, width + 128)), far_struct((pairs, rows)),
     ]
     away = (0, 1, 2, 6, 7, 8, 9, 13, 14)
     out_specs = [anywhere() if i in away else whole(out.shape) for i, out in enumerate(outs)]
-    operands = [*token_slots, vectors, t1, t2, key_rows, *projected, matrices]
+    operands = [token_slots[0], *token_slots[2:], *far_off(vectors, t1, t2, key_rows, *projected, matrices)]
     in_specs = [whole(operand.shape) for operand in operands]
     in_specs[-9:] = [anywhere()] * 9
     flops = 2 * 3 * ((2 * heads + 1) * total + 9 * width) * rows * width
@@ -455,7 +461,7 @@
             pltpu.VMEM((heads, width, rows), F32),
             pltpu.SemaphoreType.DMA((6 + 3 * heads // unroll,)),
         ],
-        compiler_params=limit(KERNEL_MIB),
+        compiler_params=limit(NEAR_MIB if total <= 1024 else KERNEL_MIB),
         cost_estimate=pl.CostEstimate(
             flops=flops, bytes_accessed=24 << 20, transcendentals=heads * total * rows
         ),
@@ -591,11 +597,12 @@
     rows = cot_patch.shape[0]
     hidden = matrices.shape[3]
     pairs = parts[0].shape[0]
-    operands = [*parts, vectors, *prepared, class_tokens, cot_class, cot_patch, patch, scores, *kept, matrices]
+    rest = [vectors, *prepared, class_tokens, cot_class, cot_patch, patch, scores, *kept, matrices]
+    operands = [*parts, *far_off(*rest)]
     outs = [
-        struct((images, width)), struct((rows, width)), struct((rows, width)),
-        struct((width, hidden + 256)), struct((width, hidden + 256)), struct((pairs, width)),
-        struct((16 * images + 2 * pairs, width)), struct((28, width)), struct((2 * images, width)),
+        far_struct((images, width)), far_struct((rows, width)), far_struct((rows, width)),
+        far_struct((width, hidden + 256)), far_struct((width, hidden + 256)), far_struct((pairs, width)),
+        far_struct((16 * images + 2 * pairs, width)), far_struct((28, width)), far_struct((2 * images, width)),
     ]
     in_specs = [whole(operand.shape) for operand in operands]
     in_specs[-1 - len(kept) :] = [anywhere()] * (1 + len(kept))
@@ -614,7 +621,7 @@
         + [pltpu.VMEM(value.shape, F32) for value in kept]
         + [pltpu.VMEM((width, hidden + 256), F32)] * 2
         + [pltpu.SemaphoreType.DMA((12,)), pltpu.SemaphoreType.DMA((4,))],
-        compiler_params=limit(KERNEL_MIB),
+        compiler_params=limit(NEAR_MIB),
         cost_estimate=pl.CostEstimate(flops=8 << 30, bytes_accessed=28 << 20, transcendentals=1 << 19),
         name="middle",
     )(place, *operands)
@@ -700,7 +707,7 @@
         in_specs=[whole(mine.shape), whole(factors.shape)],
         out_specs=[whole(out.shape) for out in outs],
         out_shape=outs,
-        compiler_params=limit(KERNEL_MIB),
+        compiler_params=limit(SMALL_MIB),
         cost_estimate=pl.CostEstimate(flops=1 << 29, bytes_accessed=3 << 20, transcendentals=0),
         name="class_weights",
     )(mine, factors)
@@ -777,21 +784,22 @@
         for copy in copies:
             copy.wait()
         d_query = d_qt[...].T * size ** (-0.5)
-        w_q, w_k, w_v = (split(w_ref[:, i * width : (i + 1) * width]) for i in range(3))
-        gain = shift = g_k = g_v = 0.0
+        w_q, w_kv = split(w_ref[:, :width]), split(w_ref[:, width:])
+        gain = shift = g_kv = 0.0
         for slot in range(slots):
             here = pl.ds(slot * rows, rows)
             unit, _ = norm_rows(tokens[slot])
             normed = split(unit * vecs_ref[0:1, :] + vecs_ref[1:2, :])
-            dk, dv = split(d_keys[here, :]), split(d_values[here, :])
-            piece = mm3(dk, w_k, NT) + mm3(dv, w_v, NT)
+            d_kv = split(jnp.concatenate([d_keys[here, :], d_values[here, :]], axis=1))
+            piece = mm3(d_kv, w_kv, NT)
             if slot == 0:
                 dq = split(d_query)
                 piece = piece + mm3(dq, w_q, NT)
                 g_q = mm3(normed, dq, TN)
             (odd_ref if slot % 2 else even_ref)[slot // 2] = piece
             gain, shift = gain + row_sum(piece * unit), shift + row_sum(piece)
-            g_k, g_v = g_k + mm3(normed, dk, TN), g_v + mm3(normed, dv, TN)
+            g_kv = g_kv + mm3(normed, d_kv, TN)
+        g_k, g_v = g_kv[:, :width], g_kv[:, width:]
         added = jnp.concatenate(
             [gain, shift, row_sum(d_query), row_sum(d_values[...]), jnp.zeros((4, width), F32)], axis=0
         )
@@ -818,12 +826,12 @@
     rows, width = cot.shape
     heads, total, _ = found[0].shape
     slots, unroll = total // rows, 2 if total <= 1024 else 1
-    operands = [*token_slots, *found, cot, *keys_values, query, *tables, vec_rows, vectors, matrices]
+    operands = far_off(*token_slots, *found, cot, *keys_values, query, *tables, vec_rows, vectors, matrices)
     specs = [whole(operand.shape) for operand in operands]
     specs[:slots] = [anywhere()] * slots
     specs[slots : slots + 4] = [by_head(unroll, operand.shape) for operand in found[:4]]
     specs[-1] = anywhere()
-    outs = [struct((slots // 2, rows, width))] * 2 + [struct((width, 640))] * 2
+    outs = [far_struct((slots // 2, rows, width))] * 2 + [far_struct((width, 640))] * 2
     return pl.pallas_call(
         functools.partial(backward_kernel, slots, lengths.shape[1], dp_size, unroll),
         grid=(heads // unroll,),
@@ -839,7 +847,7 @@
             pltpu.VMEM((slots, rows, width), F32),
             pltpu.SemaphoreType.DMA((1 + slots,)),
         ],
-        compiler_params=limit(KERNEL_MIB),
+        compiler_params=limit(NEAR_MIB if total <= 1024 else KERNEL_MIB),
         cost_estimate=pl.CostEstimate(
             flops=6 * (4 * heads + 6) * total * rows * width, bytes_accessed=24 << 20, transcendentals=0
         ),
@@ -907,82 +915,96 @@
     return (updated, first, second)
 
 
+def stage_kernel(sliced, place_ref, w_ref, m1_ref, m2_ref, ema_ref, w_out, m1_out, m2_out, ema_out, arrived):
+    rows = w_out.shape[2]
+    if sliced:
+        w_ref = w_ref.at[:, :, pl.ds(pl.multiple_of(place_ref[1] * rows, rows), rows), :]
+    pairs = [(w_ref, w_out), (m1_ref, m1_out), (m2_ref, m2_out), (ema_ref, ema_out)]
+    for copy in copy_in(pairs, arrived):
+        copy.wait()
+
+
+def stage(place, mats):
+    shape = mats[1].shape
+    return pl.pallas_call(
+        functools.partial(stage_kernel, mats[0].shape != shape),
+        in_specs=[smem()] + [anywhere()] * 4,
+        out_specs=[pl.BlockSpec(memory_space=pltpu.VMEM)] * 4,
+        out_shape=[pltpu.VMEM(shape, F32)] * 4,
+        scratch_shapes=[pltpu.SemaphoreType.DMA((4,))],
+        compiler_params=limit(8),
+        cost_estimate=pl.CostEstimate(flops=1, bytes_accessed=1, transcendentals=0),
+        name="stage",
+    )(place, *far_off(*mats))
+
+
 def adam_kernel(sliced, *refs):
     (
         place_ref, squares_ref, early_own, early_other, late_own, late_other, added_ref,
         class_ref, w_ref, m1_ref, m2_ref, ema_ref, v_ref, v1_ref, v2_ref, v_ema_ref,
         t_ref, t1_ref, t2_ref, t_ema_ref,
     ) = refs[:20]
-    norm_ref, new_ref, first_ref, second_ref, average_ref = refs[20:25]
-    v_outs, t_outs = refs[25:29], refs[29:33]
-    grads, columns = refs[33:35]
-    step = pl.program_id(0)
+    norm_ref, mat_outs, v_outs, t_outs = refs[20], refs[21:25], refs[25:29], refs[29:33]
+    stored, leaving, columns = refs[33:37], refs[37], refs[38]
     norm = jnp.sqrt(squares_ref[0:1, 0:1])
     factor = jnp.minimum(1.0, CLIP_NORM / norm)
-
-    def store(outs, weight, gradient, moment1, moment2, ema, rate, decay):
+    norm_ref[...] = norm
+
+    def updates(weight, gradient, moment1, moment2, ema, rate, decay):
         updated, first, second = adam_step(weight, gradient * factor, moment1, moment2, rate, decay)
-        average = EMA_RATE * ema + (1.0 - EMA_RATE) * updated
-        for out, value in zip(outs, (updated, first, second, average)):
-            out[...] = value
-
-    @pl.when(step == 0)
-    def _():
-        norm_ref[...] = norm
-        even = jnp.bitwise_and(place_ref[0], 1) == 0
-        pair = lambda own, other: (jnp.where(even, own[...], other[...]), jnp.where(even, other[...], own[...]))
-        early_left, early_right = pair(early_own, early_other)
-        late_left, late_right = pair(late_own, late_other)
-        hidden = grads.shape[2]
-        grads[0] = jnp.concatenate(
-            [late_left, late_right[:, :512], early_left[:, hidden:], early_right[:, hidden : hidden + 128]],
-            axis=1,
-        )
-        grads[1] = early_left[:, :hidden]
-        grads[2] = early_right[:, :hidden]
-        small = late_right[:, 512:] + added_ref[...]
-        count = v_ref.shape[0]
-        if sliced:
-            columns[:, :count] = v_ref[...].T
-            share = small.shape[0]
-            begin = pl.multiple_of(place_ref[1] * share, share)
-            weight = columns[pl.ds(begin, share), :].T[:count, :]
-        else:
-            weight = v_ref[...]
-        store(v_outs, weight, small.T[:count, :], v1_ref[...], v2_ref[...], v_ema_ref[...], LR_VECTOR, 0.0)
-        talk = small[:8, count : count + 17]
-        store(t_outs, t_ref[...], talk, t1_ref[...], t2_ref[...], t_ema_ref[...], LR_TALKING, 0.0)
-
-    self_grad = grads[jnp.minimum(step, 2)]
-    grad = jnp.where(step < 3, self_grad, class_ref[jnp.maximum(step - 3, 0)])
-    store((new_ref, first_ref, second_ref, average_ref), w_ref[...], grad, m1_ref[...], m2_ref[...],
-          ema_ref[...], LR_MATRIX, WEIGHT_DECAY)
+        return updated, first, second, EMA_RATE * ema + (1.0 - EMA_RATE) * updated
+
+    even = jnp.bitwise_and(place_ref[0], 1) == 0
+    pair = lambda own, other: (jnp.where(even, own[...], other[...]), jnp.where(even, other[...], own[...]))
+    early_left, early_right = pair(early_own, early_other)
+    late_left, late_right = pair(late_own, late_other)
+    hidden = w_ref.shape[3]
+    first = jnp.concatenate(
+        [late_left, late_right[:, :512], early_left[:, hidden:], early_right[:, hidden : hidden + 128]], axis=1
+    )
+    grads = [first, early_left[:, :hidden], early_right[:, :hidden], *[class_ref[i] for i in range(3)]]
+    copies = []
+    for number in (3, 4, 5, 1, 2, 0):
+        at = (number // 3, number % 3)
+        values = updates(w_ref[at], grads[number], m1_ref[at], m2_ref[at], ema_ref[at], LR_MATRIX, WEIGHT_DECAY)
+        for i, value in enumerate(values):
+            stored[i][at] = value
+            copies.append(pltpu.make_async_copy(stored[i].at[at], mat_outs[i].at[at], leaving.at[i, number]))
+            copies[-1].start()
+    small = late_right[:, 512:] + added_ref[...]
+    count = v1_ref.shape[0]
+    if sliced:
+        columns[:, :count] = v_ref[...].T
+        share = small.shape[0]
+        begin = pl.multiple_of(place_ref[1] * share, share)
+        weight = columns[pl.ds(begin, share), :].T[:count, :]
+    else:
+        weight = v_ref[...]
+    values = updates(weight, small.T[:count, :], v1_ref[...], v2_ref[...], v_ema_ref[...], LR_VECTOR, 0.0)
+    for ref, value in zip(v_outs, values):
+        ref[...] = value
+    talk = small[:8, count : count + 17]
+    values = updates(t_ref[...], talk, t1_ref[...], t2_ref[...], t_ema_ref[...], LR_TALKING, 0.0)
+    for ref, value in zip(t_outs, values):
+        ref[...] = value
+    for copy in copies:
+        copy.wait()
 
 
 def optimizer(place, squares, grads, class_share, mats, vecs, talks):
-    shape = mats[1].shape
-    sliced = mats[0].shape != shape
-    block = pl.BlockSpec((None, None) + shape[2:], lambda i, _: (i // 3, i % 3, 0, 0))
-    operands = [squares, *grads, class_share, *far_off(*mats, *vecs, *talks)]
-    specs = [whole(operand.shape) for operand in operands]
-    at = 3 + len(grads) - 1
-    specs[at : at + 4] = [block] * 4
-    if sliced:
-        specs[at] = pl.BlockSpec((None, None) + shape[2:], lambda i, ref: (i // 3, i % 3, ref[1], 0))
+    shape = mats[0].shape
+    sliced = vecs[0].shape != vecs[1].shape
+    operands = [squares, *grads, class_share, *mats, *far_off(*vecs, *talks)]
+    vmem = pl.BlockSpec(memory_space=pltpu.VMEM)
     outs = [struct((1, 1))] + [struct(shape)] * 4
     outs += [struct(vecs[1].shape)] * 4 + [struct(talks[0].shape)] * 4
-    out_specs = [whole(out.shape) for out in outs]
-    out_specs[1:5] = [block] * 4
     return pl.pallas_call(
         functools.partial(adam_kernel, sliced),
-        grid_spec=pltpu.PrefetchScalarGridSpec(
-            num_scalar_prefetch=1,
-            grid=(6,),
-            in_specs=specs,
-            out_specs=out_specs,
-            scratch_shapes=[pltpu.VMEM((3,) + shape[2:], F32), pltpu.VMEM((vecs[0].shape[1], 128), F32)],
-        ),
+        in_specs=[smem()] + [vmem] * len(operands),
+        out_specs=[vmem] + [anywhere()] * 4 + [vmem] * 8,
         out_shape=outs,
+        scratch_shapes=[pltpu.VMEM(shape, F32)] * 4
+        + [pltpu.SemaphoreType.DMA((4, 6)), pltpu.VMEM((vecs[0].shape[1], 128), F32)],
         compiler_params=limit(SMALL_MIB),
         cost_estimate=pl.CostEstimate(flops=1 << 23, bytes_accessed=14 << 20, transcendentals=0),
         name="optimizer",
@@ -1220,7 +1242,7 @@
 
     late_send, odd = settle([early, gather], late_send, odd)
     late_other, odd = places.swap(late_send, [core]), places.swap(odd, [core])
-    late = Reduce([late_keep, late_other], places, pairs(dp + chips))
+    late = Reduce([late_keep, late_other], places, [tuple(dp[:2])] + [(step,) for step in dp[2:] + chips])
     (late.terms[1],) = launch([early], late.terms[1])
     (even,) = launch([late], even)
     own = [even[0]] + [even[i] + odd[i] for i in range(1, seq_size // 2)]
@@ -1243,19 +1265,26 @@
     while gather.groups:
         launch([gather])
         settle([gather])
-    mine = places.rows(gather.value, row_share, 2)
-    class_share, class_squares, added = class_weights(images, mine, gather.value)
-    class_share, class_squares, added = settle([late, early], class_share, class_squares, added)
-    while late.groups or early.groups:
-        launch([late, early])
-        settle([late, early])
-    last = [[term.reshape(row_share, -1) for term in stream.terms] for stream in (early, late)]
-    squares, early, late = squares_of(dp_size, place, added, class_squares, *last)
     sliced = row_share % 8 == 0
     if not sliced:
         matrices_rows, vectors_columns = places.rows(matrices, row_share, 2), places.rows(vectors, row_share, 1)
     else:
         matrices_rows, vectors_columns = matrices, vectors
+    both_places = tie(jnp.concatenate([place, places.found["dp"]]), gather.value)
+    staged = stage(both_places, [matrices_rows, matrices_moment1, matrices_moment2, matrices_ema])
+    gather.value, *staged = settle([late], gather.value, *staged)
+    while late.groups[1:]:
+        launch([late])
+        settle([late])
+    (gather.value,) = launch([late], gather.value)
+    mine = places.rows(gather.value, row_share, 2)
+    class_share, class_squares, added = class_weights(images, mine, gather.value)
+    while early.groups:
+        settle([early])
+        launch([early])
+    class_share, class_squares, added = settle([late, early], class_share, class_squares, added)
+    last = [[term.reshape(row_share, -1) for term in stream.terms] for stream in (early, late)]
+    squares, early, late = squares_of(dp_size, place, added, class_squares, *last)
     far, squares = together(far, squares)
     for group in pairs([core] + dp):
         squares = sum_of([squares] + [places.swap(squares, steps) for steps in subsets(group)])
@@ -1264,8 +1293,7 @@
     for value in (early, late):
         grads += [value, places.swap(value, [core])]
     norm, *updated = optimizer(
-        jnp.concatenate([place, places.found["dp"]]), squares, [*grads, added], class_share,
-        [matrices_rows, matrices_moment1, matrices_moment2, matrices_ema],
+        both_places, squares, [*grads, added], class_share, staged,
         [vectors_columns, vectors_moment1, vectors_moment2, vectors_ema],
         [talking, talking_moment1, talking_moment2, talking_ema],
     )

time: 198 us -> 192 us (0.970)
  Pallas kernels: 103 us -> 99.8 us
  waiting for transfers between devices: 38.6 us -> 41.6 us
  local copies, waits for them, and re-layouts: 4.54 us -> 2.06 us
  starting transfers between devices: 35 us -> 32.6 us
    unnamed x26 -> x24, local copies, waits for them, and re-layouts: 4.37 us -> 1.68 us
    concatenate x3 -> x2, other arithmetic: 2.46 us -> 0.18 us  [set_received(): jnp.concatenate(self.places.pair(self.value, values[0], group[0]), axis=1)]
    pallas_call x1, Pallas kernels: 3.22 us -> 0.97 us  [class_weights(): pl.pallas_call(functools.partial(class_weights_kernel, images), grid=(1,)...]
    ppermute x28 -> x27, starting transfers between devices: 26.9 us -> 24.7 us  [swap(): lax.ppermute(value, ('dp', 'seq'), [(place, place ^ flip) for place in ra...]
    ppermute x28 -> x27, waiting for transfers between devices: 26.6 us -> 28.2 us  [swap(): lax.ppermute(value, ('dp', 'seq'), [(place, place ^ flip) for place in ra...]
    add x7 -> x8, other arithmetic: 7.43 us -> 8.93 us  [sum_of(): total = total + term]
    pallas_call x1 -> x2, Pallas kernels: 8.93 us -> 9.67 us  [the longest x1 6.02 us: optimizer(): pl.pallas_call(functools.partial(adam_kernel, sliced), in_specs=[smem()]...]
  transfers between devices with their start and end apart: 38 -> 37, of which waited for: 19 -> 19; matrix products, arithmetic and copies ran while one was open for 5% -> 5% of each run, Pallas kernels for 26% -> 27%
where the time goes in v2:
time: 192 us; the launch traced here: 189 us
  Pallas kernels  99.8 us (52%)
  waiting for transfers between devices  41.6 us (22%)
  starting transfers between devices  32.6 us (17%)
  other arithmetic  11.7 us (6%)
  local copies, waits for them, and re-layouts  2.06 us (1%)
    pallas_call x1, Pallas kernels, backward(): pl.pallas_call(functools.partial(backward_kernel, slots, lengths.shape[1]...  35.7 us
    ppermute x27, waiting for transfers between devices, swap(): lax.ppermute(value, ('dp', 'seq'), [(place, place ^ flip) for place in ra...  28.2 us
    pallas_call x1, Pallas kernels, forward(): pl.pallas_call(functools.partial(forward_kernel, slots, lengths.shape[1],...  25.4 us
    ppermute x27, starting transfers between devices, swap(): lax.ppermute(value, ('dp', 'seq'), [(place, place ^ flip) for place in ra...  24.7 us
    pallas_call x1, Pallas kernels, middle(): pl.pallas_call(functools.partial(middle_kernel, images, len(parts)), grid...  16.6 us
    ppermute x10, waiting for transfers between devices, swap(): lax.ppermute(value, axis, [(place, place ^ bit) for place in range(size)])  13.4 us
    add x8, other arithmetic, sum_of(): total = total + term  8.93 us
    ppermute x10, starting transfers between devices, swap(): lax.ppermute(value, axis, [(place, place ^ bit) for place in range(size)])  7.9 us
  transfers between devices with their start and end apart: 37, of which 19 were waited for; matrix products, arithmetic and copies ran while one was open for 5% of the time, Pallas kernels for 27%

profile of v2, /device:TPU:0, one launch (start us, length us, event | category | flops | bytes accessed | tf_op | source)
XLA Modules:
  0.0 188.9 jit_solution(6945694961736189338)
XLA Ops:
  1.2 2.6 %collective-permute-start = (f32[256,384]{1,0:T(8,128)}, f32[256,384]{1,0:T(8,128)S(1)}, u32[]{:S(2)}, u32[]{:S(2)}) collective-permute-start(f32[256,384]{1,0:T(8,128)} %tokens_ref), channel_id=1, source_target_pairs={{0,2},{1,3},{2,0},{3,1},{4,6},{5,7},{6,4},{7,5},{8,10},{9,11},{10,... | collective-permute-start | bytes 1179656 | tf_op jit(solution)/shard_map/ppermute | solution.py:1015
  3.8 6.4 %prepare.1 = (f32[4,384]{1,0:T(4,128)}, f32[4,384]{1,0:T(4,128)}, f32[4,384]{1,0:T(4,128)}, f32[32,384]{1,0:T(8,128)}, f32[32,128]{1,0:T(8,128)}, /*index=5*/f32...) custom-call(f32[256,384]{1,0:T(8,128)} %tokens_ref, ...), custom_call_target="tpu_custom_call" | custom-call | flops 4294967296 | bytes 8388608 | tf_op jit(solution)/shard_map/prepare/pallas_call | solution.py:273
  10.2 3.5 %collective-permute-done.refs_3_.refs_4_ = f32[256,384]{1,0:T(8,128)S(1)} collective-permute-done((f32[256,384]{1,0:T(8,128)}, f32[256,384]{1,0:T(8,128)S(1)}, u32[]{:S(2)}, u32[]{:S(2)}) %collective-permute-start) | collective-permute-done | bytes 393248 | tf_op jit(solution)/shard_map/ppermute | solution.py:1015
  15.5 25.4 %forward.1 = (bf16[8,1024,256]{2,1,0:T(8,128)(2,1)}, bf16[8,1024,256]{2,1,0:T(8,128)(2,1)}, f32[8,384,256]{2,1,0:T(8,128)}, f32[8,1,256]{2,1,0:T(1,128)}, f32[38...) custom-call(s32[1]{0:T(128)} %bitcast.refs_0_, ...), custom_call_target="tpu_custom_call" | custom-call | flops 12306087936 | bytes 25165824 | tf_op jit(solution)/shard_map/forward/pallas_call | solution.py:436
  41.1 1.8 collective-permute-start.4
  42.9 2.8 %collective-permute-done.4.refs_3_ = f32[32,512]{1,0:T(8,128)S(1)} collective-permute-done((f32[32,512]{1,0:T(8,128)}, f32[32,512]{1,0:T(8,128)S(1)}, u32[]{:S(2)}, u32[]{:S(2)}) %collective-permute-start.4) | collective-permute-done | bytes 65568 | tf_op jit(solution)/shard_map/ppermute | solution.py:1015
  48.0 16.6 %middle.1 = (f32[4,384]{1,0:T(4,128)}, f32[256,384]{1,0:T(8,128)}, f32[256,384]{1,0:T(8,128)}, f32[384,1792]{1,0:T(8,128)}, f32[384,1792]{1,0:T(8,128)}, /*index...) custom-call(s32[1]{0:T(128)} %bitcast.refs_0_, f32[32,512]{1,0:T(8,128)S(1)} %copy-done.5, ...), custom_call_target="tpu_custom_call" | custom-call | flops 8589934592 | bytes 29360128 | tf_op jit(solution)/shard_map/middle/pallas_call | solution.py:611
  66.7 3.1 %collective-permute-done.7.refs_1_ = f32[32,384]{1,0:T(8,128)S(1)} collective-permute-done((f32[32,384]{1,0:T(8,128)}, f32[32,384]{1,0:T(8,128)S(1)}, u32[]{:S(2)}, u32[]{:S(2)}) %collective-permute-start.7) | collective-permute-done | bytes 49184 | tf_op jit(solution)/shard_map/ppermute | solution.py:1015
  71.3 2.7 %class_finish.1 = (f32[4,384]{1,0:T(4,128)}, f32[136,384]{1,0:T(8,128)S(1)}) custom-call(f32[32,384]{1,0:T(8,128)S(1)} %copy-done.2, f32[32,384]{1,0:T(8,128)S(1)} %collective-permute-done.7.refs_1_, f32[32,384]{1,0:T(8,128)S(1)} %collective-permute-done.8.refs_2_, f32[32,384]{1,0:T(8,128)S(1)} %collective-permute-done.9.refs_3_, ...), custom_call_target="tpu_custom_call" | custom-call | flops 536870912 | bytes 3145728 | tf_op jit(solution)/shard_map/class_finish/pallas_call | solution.py:658
  74.0 1.8 add_bitcast_fusion
  79.4 2.6 %collective-permute-start.13 = (f32[1,34,384]{2,1,0:T(8,128)S(1)}, f32[1,34,384]{2,1,0:T(8,128)S(1)}, u32[]{:S(2)}, u32[]{:S(2)}) collective-permute-start(f32[1,34,384]{2,1,0:T(8,128)S(1)} %dynamic-slice_bitcast_fusion), channel_id=1, source_target_pairs={{0,16},{1,17},{2,18},{3,19},{4,20},{5,21},{6,22},{7,23},{8,24},{9,... | collective-permute-start | bytes 156680 | tf_op jit(solution)/shard_map/ppermute | solution.py:1068
  82.0 35.7 %backward.1 = (f32[2,256,384]{2,1,0:T(8,128)}, f32[2,256,384]{2,1,0:T(8,128)}, f32[384,640]{1,0:T(8,128)}, f32[384,640]{1,0:T(8,128)}) custom-call(s32[1]{0:T(128)} %bitcast.refs_0_, s32[1,4]{1,0:T(1,128)S(1)} %copy-done.6, f32[256,384]{1,0:T(8,128)} %tokens_ref, f32[256,384]{1,0:T(8,128)} %copy-done.1, f32[256,384]{1,0:T(8,128)} %copy-done.3, ...), custom_call_target="tpu_custom_call" | custom-call | flops 22951231488 | bytes 25165824 | tf_op jit(solution)/shard_map/backward/pallas_call | solution.py:835
  120.7 2.1 %add_bitcast_fusion.3 = (f32[2,48,640]{2,1,0:T(8,128)S(1)}, f32[2,48,640]{2,1,0:T(8,128)}, f32[2,48,640]{2,1,0:T(8,128)}) fusion(f32[2,2,2,48,640]{4,3,2,1,0:T(8,128)} %bitcast.13, u32[]{:T(128)S(6)} %convert_element_type.33, u32[]{:T(128)S(6)} %convert_element_type.31, f32[2,2,2,48,640]{4,3,2,1,0:T(8,128)S(1)} %bitcast.84, u32[]{:T(128)S(6)} %convert_element_type.30, ...), kind=kLoop, calls=%fused_computation.19 | loop fusion | flops 184320 | bytes 2211856 | tf_op jit(solution)/shard_map/add | solution.py:1173
  130.1 1.8 collective-permute-start.20
  131.9 3.8 %collective-permute-done.17 = f32[2,34,384]{2,1,0:T(8,128)} collective-permute-done((f32[2,34,384]{2,1,0:T(8,128)S(1)}, f32[2,34,384]{2,1,0:T(8,128)}, u32[]{:S(2)}, u32[]{:S(2)}) %collective-permute-start.17) | collective-permute-done | bytes 104480 | tf_op jit(solution)/shard_map/ppermute | solution.py:1068
  140.4 8.9 %collective-permute-done.21 = f32[2,48,640]{2,1,0:T(8,128)S(1)} collective-permute-done((f32[2,48,640]{2,1,0:T(8,128)}, f32[2,48,640]{2,1,0:T(8,128)S(1)}, u32[]{:S(2)}, u32[]{:S(2)}) %collective-permute-start.21) | collective-permute-done | bytes 245792 | tf_op jit(solution)/shard_map/ppermute | solution.py:1068
  149.3 2.6 %collective-permute-done.22 = f32[2,48,640]{2,1,0:T(8,128)S(1)} collective-permute-done((f32[2,48,640]{2,1,0:T(8,128)S(1)}, f32[2,48,640]{2,1,0:T(8,128)S(1)}, u32[]{:S(2)}, u32[]{:S(2)}) %collective-permute-start.22) | collective-permute-done | bytes 245792 | tf_op jit(solution)/shard_map/ppermute | solution.py:1068
  157.5 3.7 %stage.1 = (f32[2,3,48,1536]{3,2,1,0:T(8,128)S(1)}, f32[2,3,48,1536]{3,2,1,0:T(8,128)S(1)}, f32[2,3,48,1536]{3,2,1,0:T(8,128)S(1)}, f32[2,3,48,1536]{3,2,1,0:T(8,128)S(1)}) custom-call(s32[2]{0:T(128)S(1)} %pad_add_fusion.place_ref.refs_0_, f32[2,3,384,1536]{3,2,1,0:T(8,128)} %w_ref.1, f32[2,3,48,1536]{3,2,1,0:T(8,128)} %m1_ref.1, ...), custom_call_target="tpu_custom_call" | custom-call | flops 1 | bytes 1 | tf_op jit(solution)/shard_map/stage/pallas_call | solution.py:929
  161.1 3.0 %collective-permute-done.25 = f32[48,640]{1,0:T(8,128)S(1)} collective-permute-done((f32[48,640]{1,0:T(8,128)S(1)}, f32[48,640]{1,0:T(8,128)S(1)}, u32[]{:S(2)}, u32[]{:S(2)}) %collective-permute-start.25) | collective-permute-done | bytes 122912 | tf_op jit(solution)/shard_map/ppermute | solution.py:1068
  167.6 2.6 %collective-permute-done.27.refs_6_ = f32[48,640]{1,0:T(8,128)S(1)} collective-permute-done((f32[48,640]{1,0:T(8,128)S(1)}, f32[48,640]{1,0:T(8,128)S(1)}, u32[]{:S(2)}, u32[]{:S(2)}) %collective-permute-start.27) | collective-permute-done | bytes 122912 | tf_op jit(solution)/shard_map/ppermute | solution.py:1068
  175.1 2.1 %collective-permute-start.33 = (f32[8,128]{1,0:T(8,128)S(1)}, f32[8,128]{1,0:T(8,128)S(1)}, u32[]{:S(2)}, u32[]{:S(2)}) collective-permute-start(f32[8,128]{1,0:T(8,128)S(1)} %add_add_fusion.1), channel_id=1, source_target_pairs={{0,16},{1,17},{2,18},{3,19},{4,20},{5,21},{6,22},{7,23},{8,24},{9,... | collective-permute-start | bytes 12296 | tf_op jit(solution)/shard_map/ppermute | solution.py:1068
  177.3 2.2 %collective-permute-start.34 = (f32[8,128]{1,0:T(8,128)S(1)}, f32[8,128]{1,0:T(8,128)S(1)}, u32[]{:S(2)}, u32[]{:S(2)}) collective-permute-start(f32[8,128]{1,0:T(8,128)S(1)} %add_add_fusion.1), channel_id=1, source_target_pairs={{0,24},{1,25},{2,26},{3,27},{4,28},{5,29},{6,30},{7,31},{8,16},{9,... | collective-permute-start | bytes 12296 | tf_op jit(solution)/shard_map/ppermute | solution.py:1068
  179.5 2.2 %token_grad.1 = f32[256,384]{1,0:T(8,128)} custom-call(f32[256,384]{1,0:T(8,128)} %tokens_ref, f32[28,384]{1,0:T(8,128)} %refs_12_.3, f32[256,384]{1,0:T(8,128)S(1)} %get-tuple-element.302.own_ref, f32[256,384]{1,0:T(8,128)S(1)} %get-tuple-element.303.near_ref, f32[256,384]{1,0:T(8,128)S(1)} %collective-permute-done.24.far_ref, ...), custom_call_target="tpu_custom_call" | custom-call | flops 2097152 | bytes 2097152 | tf_op jit(solution)/shard_map/token_grad/pallas_call | solution.py:866
  182.7 6.0 %optimizer.1 = (f32[1,1]{1,0:T(1,128)}, f32[2,3,48,1536]{3,2,1,0:T(8,128)}, f32[2,3,48,1536]{3,2,1,0:T(8,128)}, f32[2,3,48,1536]{3,2,1,0:T(8,128)}, f32[2,3,48,1...) custom-call(s32[2]{0:T(128)S(1)} %pad_add_fusion.place_ref.refs_0_, ...), custom_call_target="tpu_custom_call" | custom-call | flops 8388608 | bytes 14680064 | tf_op jit(solution)/shard_map/optimizer/pallas_call | solution.py:1001
  (103 shorter events, 41.8 us)
Async XLA Ops:
  1.2 12.5 %collective-permute-start = (f32[256,384]{1,0:T(8,128)}, f32[256,384]{1,0:T(8,128)S(1)}, u32[]{:S(2)}, u32[]{:S(2)}) collective-permute-start(f32[256,384]{1,0:T(8,128)} %tokens_ref), channel_id=1, source_target_pairs={{0,2},{1,3},{2,0},{3,1},{4,6},{5,7},{6,4},{7,5},{8,10},{9,11},{10,... | collective-permute-start | bytes 1179656 | tf_op jit(solution)/shard_map/ppermute | solution.py:1015
  64.6 9.4 %collective-permute-start.6 = (f32[384,1792]{1,0:T(8,128)}, f32[384,1792]{1,0:T(8,128)}, u32[]{:S(2)}, u32[]{:S(2)}) collective-permute-start(f32[384,1792]{1,0:T(8,128)} %get-tuple-element.186), channel_id=1, source_target_pairs={{0,1},{1,0},{2,3},{3,2},{4,5},{5,4},{6,7},{7,6},{8,9},{9,8},{10,11... | collective-permute-start | bytes 8257544 | tf_op jit(solution)/shard_map/ppermute | solution.py:1068
  64.8 5.0 %collective-permute-start.7 = (f32[32,384]{1,0:T(8,128)}, f32[32,384]{1,0:T(8,128)S(1)}, u32[]{:S(2)}, u32[]{:S(2)}) collective-permute-start(f32[32,384]{1,0:T(8,128)} %get-tuple-element.187.refs_0_), channel_id=1, source_target_pairs={{0,1},{1,0},{2,3},{3,2},{4,5},{5,4},{6,7},{7,6},{8,9},{9,8},{10,11... | collective-permute-start | bytes 147464 | tf_op jit(solution)/shard_map/ppermute | solution.py:1015
  75.8 41.8 %collective-permute-start.10 = (f32[2,48,1792]{2,1,0:T(8,128)S(1)}, f32[2,48,1792]{2,1,0:T(8,128)}, u32[]{:S(2)}, u32[]{:S(2)}) collective-permute-start(f32[2,48,1792]{2,1,0:T(8,128)S(1)} %get-tuple-element.212), channel_id=1, source_target_pairs={{0,4},{1,5},{2,6},{3,7},{4,0},{5,1},{6,2},{7,3},{8,12},{9,13},{10,... | collective-permute-start | bytes 2064392 | tf_op jit(solution)/shard_map/ppermute | solution.py:1068
  77.3 40.3 %collective-permute-start.11 = (f32[2,48,1792]{2,1,0:T(8,128)S(1)}, f32[2,48,1792]{2,1,0:T(8,128)}, u32[]{:S(2)}, u32[]{:S(2)}) collective-permute-start(f32[2,48,1792]{2,1,0:T(8,128)S(1)} %get-tuple-element.213), channel_id=1, source_target_pairs={{0,8},{1,9},{2,10},{3,11},{4,12},{5,13},{6,14},{7,15},{8,0},{9,1},... | collective-permute-start | bytes 2064392 | tf_op jit(solution)/shard_map/ppermute | solution.py:1068
  79.0 38.7 %collective-permute-start.12 = (f32[2,48,1792]{2,1,0:T(8,128)S(1)}, f32[2,48,1792]{2,1,0:T(8,128)}, u32[]{:S(2)}, u32[]{:S(2)}) collective-permute-start(f32[2,48,1792]{2,1,0:T(8,128)S(1)} %get-tuple-element.214), channel_id=1, source_target_pairs={{0,12},{1,13},{2,14},{3,15},{4,8},{5,9},{6,10},{7,11},{8,4},{9,5},... | collective-permute-start | bytes 2064392 | tf_op jit(solution)/shard_map/ppermute | solution.py:1068
  79.4 38.3 %collective-permute-start.13 = (f32[1,34,384]{2,1,0:T(8,128)S(1)}, f32[1,34,384]{2,1,0:T(8,128)S(1)}, u32[]{:S(2)}, u32[]{:S(2)}) collective-permute-start(f32[1,34,384]{2,1,0:T(8,128)S(1)} %dynamic-slice_bitcast_fusion), channel_id=1, source_target_pairs={{0,16},{1,17},{2,18},{3,19},{4,20},{5,21},{6,22},{7,23},{8,24},{9,... | collective-permute-start | bytes 156680 | tf_op jit(solution)/shard_map/ppermute | solution.py:1068
  117.8 5.0 %collective-permute-start.15 = (f32[2,256,384]{2,1,0:T(8,128)}, f32[2,256,384]{2,1,0:T(8,128)}, u32[]{:S(2)}, u32[]{:S(2)}) collective-permute-start(f32[2,256,384]{2,1,0:T(8,128)} %get-tuple-element.225), channel_id=1, source_target_pairs={{0,1},{1,0},{2,3},{3,2},{4,5},{5,4},{6,7},{7,6},{8,9},{9,8},{10,11... | collective-permute-start | bytes 2359304 | tf_op jit(solution)/shard_map/ppermute | solution.py:1068
  124.0 27.9 %collective-permute-start.24 = (f32[256,384]{1,0:T(8,128)S(1)}, f32[256,384]{1,0:T(8,128)S(1)}, u32[]{:S(2)}, u32[]{:S(2)}) collective-permute-start(f32[256,384]{1,0:T(8,128)S(1)} %get-tuple-element.301), channel_id=1, source_target_pairs={{0,2},{1,3},{2,0},{3,1},{4,6},{5,7},{6,4},{7,5},{8,10},{9,11},{10,... | collective-permute-start | bytes 1179656 | tf_op jit(solution)/shard_map/ppermute | solution.py:1015
  124.9 5.1 %collective-permute-start.16 = (f32[2,34,384]{2,1,0:T(8,128)S(1)}, f32[2,34,384]{2,1,0:T(8,128)S(1)}, u32[]{:S(2)}, u32[]{:S(2)}) collective-permute-start(f32[2,34,384]{2,1,0:T(8,128)S(1)} %pad_maximum_fusion.3), channel_id=1, source_target_pairs={{0,4},{1,5},{2,6},{3,7},{4,0},{5,1},{6,2},{7,3},{8,12},{9,13},{10,... | collective-permute-start | bytes 313352 | tf_op jit(solution)/shard_map/ppermute | solution.py:1068
  126.6 9.1 %collective-permute-start.17 = (f32[2,34,384]{2,1,0:T(8,128)S(1)}, f32[2,34,384]{2,1,0:T(8,128)}, u32[]{:S(2)}, u32[]{:S(2)}) collective-permute-start(f32[2,34,384]{2,1,0:T(8,128)S(1)} %pad_maximum_fusion.3), channel_id=1, source_target_pairs={{0,8},{1,9},{2,10},{3,11},{4,12},{5,13},{6,14},{7,15},{8,0},{9,1},... | collective-permute-start | bytes 313352 | tf_op jit(solution)/shard_map/ppermute | solution.py:1068
  128.1 8.6 %collective-permute-start.18 = (f32[2,34,384]{2,1,0:T(8,128)S(1)}, f32[2,34,384]{2,1,0:T(8,128)}, u32[]{:S(2)}, u32[]{:S(2)}) collective-permute-start(f32[2,34,384]{2,1,0:T(8,128)S(1)} %pad_maximum_fusion.3), channel_id=1, source_target_pairs={{0,12},{1,13},{2,14},{3,15},{4,8},{5,9},{6,10},{7,11},{8,4},{9,5},... | collective-permute-start | bytes 313352 | tf_op jit(solution)/shard_map/ppermute | solution.py:1068
  128.5 23.4 %collective-permute-start.23 = (f32[48,1792]{1,0:T(8,128)S(1)}, f32[48,1792]{1,0:T(8,128)S(1)}, u32[]{:S(2)}, u32[]{:S(2)}) collective-permute-start(f32[48,1792]{1,0:T(8,128)S(1)} %bitcast_add_fusion.3), channel_id=1, source_target_pairs={{0,16},{1,17},{2,18},{3,19},{4,20},{5,21},{6,22},{7,23},{8,24},{9,... | collective-permute-start | bytes 1032200 | tf_op jit(solution)/shard_map/ppermute | solution.py:1068
  130.1 9.2 %collective-permute-start.20 = (f32[2,48,640]{2,1,0:T(8,128)}, f32[2,48,640]{2,1,0:T(8,128)S(1)}, u32[]{:S(2)}, u32[]{:S(2)}) collective-permute-start(f32[2,48,640]{2,1,0:T(8,128)} %get-tuple-element.231), channel_id=1, source_target_pairs={{0,4},{1,5},{2,6},{3,7},{4,0},{5,1},{6,2},{7,3},{8,12},{9,13},{10,... | collective-permute-start | bytes 737288 | tf_op jit(solution)/shard_map/ppermute | solution.py:1068
  135.7 13.6 %collective-permute-start.21 = (f32[2,48,640]{2,1,0:T(8,128)}, f32[2,48,640]{2,1,0:T(8,128)S(1)}, u32[]{:S(2)}, u32[]{:S(2)}) collective-permute-start(f32[2,48,640]{2,1,0:T(8,128)} %get-tuple-element.232), channel_id=1, source_target_pairs={{0,8},{1,9},{2,10},{3,11},{4,12},{5,13},{6,14},{7,15},{8,0},{9,1},... | collective-permute-start | bytes 737288 | tf_op jit(solution)/shard_map/ppermute | solution.py:1068
  136.7 15.2 %collective-permute-start.22 = (f32[2,48,640]{2,1,0:T(8,128)S(1)}, f32[2,48,640]{2,1,0:T(8,128)S(1)}, u32[]{:S(2)}, u32[]{:S(2)}) collective-permute-start(f32[2,48,640]{2,1,0:T(8,128)S(1)} %get-tuple-element.233), channel_id=1, source_target_pairs={{0,12},{1,13},{2,14},{3,15},{4,8},{5,9},{6,10},{7,11},{8,4},{9,5},... | collective-permute-start | bytes 737288 | tf_op jit(solution)/shard_map/ppermute | solution.py:1068
  139.2 15.2 %collective-permute-start.19 = (f32[8,34,384]{2,1,0:T(8,128)S(1)}, f32[8,34,384]{2,1,0:T(8,128)S(1)}, u32[]{:S(2)}, u32[]{:S(2)}) collective-permute-start(f32[8,34,384]{2,1,0:T(8,128)S(1)} %pad_maximum_fusion.2), channel_id=1, source_target_pairs={{0,2},{1,3},{2,0},{3,1},{4,6},{5,7},{6,4},{7,5},{8,10},{9,11},{10,... | collective-permute-start | bytes 1253384 | tf_op jit(solution)/shard_map/ppermute | solution.py:1068
  154.9 9.3 %collective-permute-start.25 = (f32[48,640]{1,0:T(8,128)S(1)}, f32[48,640]{1,0:T(8,128)S(1)}, u32[]{:S(2)}, u32[]{:S(2)}) collective-permute-start(f32[48,640]{1,0:T(8,128)S(1)} %bitcast_add_fusion.9), channel_id=1, source_target_pairs={{0,16},{1,17},{2,18},{3,19},{4,20},{5,21},{6,22},{7,23},{8,24},{9,... | collective-permute-start | bytes 368648 | tf_op jit(solution)/shard_map/ppermute | solution.py:1068
  155.3 12.2 %collective-permute-start.28 = (f32[48,1792]{1,0:T(8,128)S(1)}, f32[48,1792]{1,0:T(8,128)S(1)}, u32[]{:S(2)}, u32[]{:S(2)}) collective-permute-start(f32[48,1792]{1,0:T(8,128)S(1)} %fusion.1.refs_3_), channel_id=1, source_target_pairs={{0,2},{1,3},{2,0},{3,1},{4,6},{5,7},{6,4},{7,5},{8,10},{9,11},{10,... | collective-permute-start | bytes 1032200 | tf_op jit(solution)/shard_map/ppermute | solution.py:1068
  165.2 5.0 %collective-permute-start.27 = (f32[48,640]{1,0:T(8,128)S(1)}, f32[48,640]{1,0:T(8,128)S(1)}, u32[]{:S(2)}, u32[]{:S(2)}) collective-permute-start(f32[48,640]{1,0:T(8,128)S(1)} %fusion.2.refs_5_), channel_id=1, source_target_pairs={{0,2},{1,3},{2,0},{3,1},{4,6},{5,7},{6,4},{7,5},{8,10},{9,11},{10,... | collective-permute-start | bytes 368648 | tf_op jit(solution)/shard_map/ppermute | solution.py:1068
  172.4 10.3 %collective-permute-start.35 = (f32[48,1792]{1,0:T(8,128)S(1)}, f32[48,1792]{1,0:T(8,128)S(1)}, u32[]{:S(2)}, u32[]{:S(2)}) collective-permute-start(f32[48,1792]{1,0:T(8,128)S(1)} %get-tuple-element.271.refs_2_), channel_id=1, source_target_pairs={{0,1},{1,0},{2,3},{3,2},{4,5},{5,4},{6,7},{7,6},{8,9},{9,8},{10,11... | collective-permute-start | bytes 1032200 | tf_op jit(solution)/shard_map/ppermute | solution.py:1068
  175.1 6.6 %collective-permute-start.32 = (f32[8,128]{1,0:T(8,128)S(1)}, f32[8,128]{1,0:T(8,128)S(1)}, u32[]{:S(2)}, u32[]{:S(2)}) collective-permute-start(f32[8,128]{1,0:T(8,128)S(1)} %add_add_fusion.1), channel_id=1, source_target_pairs={{0,8},{1,9},{2,10},{3,11},{4,12},{5,13},{6,14},{7,15},{8,0},{9,1},... | collective-permute-start | bytes 12296 | tf_op jit(solution)/shard_map/ppermute | solution.py:1068
  175.1 6.6 %collective-permute-start.33 = (f32[8,128]{1,0:T(8,128)S(1)}, f32[8,128]{1,0:T(8,128)S(1)}, u32[]{:S(2)}, u32[]{:S(2)}) collective-permute-start(f32[8,128]{1,0:T(8,128)S(1)} %add_add_fusion.1), channel_id=1, source_target_pairs={{0,16},{1,17},{2,18},{3,19},{4,20},{5,21},{6,22},{7,23},{8,24},{9,... | collective-permute-start | bytes 12296 | tf_op jit(solution)/shard_map/ppermute | solution.py:1068
  177.3 5.4 %collective-permute-start.34 = (f32[8,128]{1,0:T(8,128)S(1)}, f32[8,128]{1,0:T(8,128)S(1)}, u32[]{:S(2)}, u32[]{:S(2)}) collective-permute-start(f32[8,128]{1,0:T(8,128)S(1)} %add_add_fusion.1), channel_id=1, source_target_pairs={{0,24},{1,25},{2,26},{3,27},{4,28},{5,29},{6,30},{7,31},{8,16},{9,... | collective-permute-start | bytes 12296 | tf_op jit(solution)/shard_map/ppermute | solution.py:1068
  (25 other events, 149.2 us)

commit v3 on v2

--- a/solution.py
+++ b/solution.py
@@ -469,24 +469,46 @@
     )(place, lengths, *operands)
 
 
+def class_stage_kernel(place_ref, mats_ref, last_out, up_out, down_out, first_out, arrived):
+    width = first_out.shape[1]
+    pairs = [(mats_ref.at[1, 0, :, pl.ds(width, width)], last_out), (mats_ref.at[1, 1], up_out),
+             (mats_ref.at[1, 2], down_out), (mats_ref.at[1, 0, :, pl.ds(0, width)], first_out)]
+    for copy in copy_in(pairs, arrived):
+        copy.wait()
+
+
+def class_stage(place, matrices):
+    rows, columns = matrices.shape[2:]
+    half, whole_matrix = (rows, columns // 2), (rows, columns)
+    return pl.pallas_call(
+        class_stage_kernel,
+        in_specs=[smem(), anywhere()],
+        out_specs=[pl.BlockSpec(memory_space=pltpu.VMEM)] * 4,
+        out_shape=[pltpu.VMEM(shape, F32) for shape in (half, whole_matrix, whole_matrix, half)],
+        scratch_shapes=[pltpu.SemaphoreType.DMA((4,))],
+        compiler_params=limit(8),
+        cost_estimate=pl.CostEstimate(flops=1, bytes_accessed=1, transcendentals=0),
+        name="class_stage",
+    )(place, *far_off(matrices))
+
+
 def middle_kernel(images, slots, *refs):
     place_ref = refs[0]
     parts = [ref[...] for ref in refs[1 : 1 + slots]]
     (
         vecs_ref, normed_c_ref, query_c_ref, value_c_ref, key_rows_ref, own_ref,
-        class_ref, cot_class_ref, cot_patch_ref, patch_ref, scores_ref,
+        class_ref, cot_class_ref, cot_patch_ref, patch_ref, scores_ref, wc0, wc1, wc2,
         attended_hbm, projected_hbm, mixed_hbm, hidden_hbm, slope_hbm, lowered_hbm, mats_ref,
         class_out_ref, d_attended_ref, d_mixed_ref, keep_ref, send_ref, partial_ref,
         factors_ref, vec_rows_ref, class_terms_ref,
-        wc0, wc1, wc2, ws0, ws1, ws2, attended_ref, projected_ref, mixed_ref, hidden_ref, slope_ref, lowered_ref,
+        ws0, ws1, ws2, attended_ref, projected_ref, mixed_ref, hidden_ref, slope_ref, lowered_ref,
         keep, send, arrived, stored,
     ) = refs[1 + slots :]
     width = class_ref.shape[1]
     heads = 8
     size = width // heads
     copies = copy_in(
-        [(mats_ref.at[1, 0, :, pl.ds(2 * width, 2 * width)], wc0), (mats_ref.at[1, 1], wc1), (mats_ref.at[1, 2], wc2),
-         (lowered_hbm, lowered_ref), (hidden_hbm, hidden_ref), (mats_ref.at[0, 2], ws2), (slope_hbm, slope_ref),
+        [(lowered_hbm, lowered_ref), (hidden_hbm, hidden_ref), (mats_ref.at[0, 2], ws2), (slope_hbm, slope_ref),
          (mixed_hbm, mixed_ref), (mats_ref.at[0, 1], ws1), (projected_hbm, projected_ref),
          (attended_hbm, attended_ref), (mats_ref.at[0, 0, :, pl.ds(3 * width, width)], ws0)], arrived)
     vecs = vecs_ref[...]
@@ -511,8 +533,6 @@
     normed_p = split(unit_p * vecs_c[0:1] + vecs_c[1:2])
     scores = scores_ref[...]
     probs = jnp.where(scores > 0.5 * MASKED, jnp.exp(scores - top) * (1.0 / total), 0.0)
-    for copy in copies[:3]:
-        copy.wait()
     w_v = split(wc0[:, :width])
     class_attended = fold_heads(mm3_tall(split(value_rows), w_v), mask) + vecs_c[3:4]
     w_out_c = wc0[:, width:]
@@ -523,6 +543,8 @@
     d_mixed_c, d_attended_c, d_projected_c, d_hidden_c, d_lowered_c, normed2_c, tail_rows_c = (
         tail_backward(dot_tall, cot_class_ref[...], kept_c, w_out_c, wc1[...], wc2[...], vecs_c)
     )
+    for copy in copies:
+        copy.wait()
     delta = head_sums(d_attended_c * class_attended, mask)
     cot_rows = mm3_tall(split(spread(d_attended_c, mask)), w_v, NT)
     cot_const = head_sums(d_attended_c * vecs_c[3:4], mask)
@@ -543,8 +565,6 @@
         [normed_c, class_attended, normed2_c, d_lowered_c, d_own * normed_rep, value_rows,
          jnp.zeros_like(query_c), query_c * size ** (-0.5), d_attended_c, d_projected_c,
          *chunks(d_hidden_c), *chunks(kept_c[2])], axis=0)
-    for copy in copies[3:]:
-        copy.wait()
     projected, mixed, hidden, lowered = projected_ref[...], mixed_ref[...], split(hidden_ref[...]), lowered_ref[...]
     unit, scale = norm_rows(mixed)
     normed = split(unit * vecs_s[6:7] + vecs_s[7:8])
@@ -592,36 +612,36 @@
         copy.wait()
 
 
-def middle(place, parts, vectors, prepared, class_tokens, cot_class, cot_patch, patch, scores, kept, matrices):
+def middle(
+    place, parts, vectors, prepared, class_tokens, cot_class, cot_patch, patch, scores, staged, kept, matrices
+):
     images, width = class_tokens.shape
     rows = cot_patch.shape[0]
     hidden = matrices.shape[3]
     pairs = parts[0].shape[0]
-    rest = [vectors, *prepared, class_tokens, cot_class, cot_patch, patch, scores, *kept, matrices]
-    operands = [*parts, *far_off(*rest)]
+    rest = [vectors, *prepared, class_tokens, cot_class, cot_patch, patch, scores]
+    operands = [*parts, *far_off(*rest), *staged, *far_off(*kept, matrices)]
     outs = [
         far_struct((images, width)), far_struct((rows, width)), far_struct((rows, width)),
         far_struct((width, hidden + 256)), far_struct((width, hidden + 256)), far_struct((pairs, width)),
         far_struct((16 * images + 2 * pairs, width)), far_struct((28, width)), far_struct((2 * images, width)),
     ]
-    in_specs = [whole(operand.shape) for operand in operands]
+    vmem = pl.BlockSpec(memory_space=pltpu.VMEM)
+    in_specs = [vmem] * len(operands)
     in_specs[-1 - len(kept) :] = [anywhere()] * (1 + len(kept))
-    out_specs = [whole(out.shape) for out in outs]
+    out_specs = [vmem] * len(outs)
     out_specs[3:5] = [anywhere()] * 2
     return pl.pallas_call(
         functools.partial(middle_kernel, images, len(parts)),
-        grid=(1,),
         in_specs=[smem()] + in_specs,
         out_specs=out_specs,
         out_shape=outs,
-        scratch_shapes=[pltpu.VMEM((width, 2 * width), F32)]
-        + [pltpu.VMEM((width, hidden), F32)] * 2
-        + [pltpu.VMEM((width, width), F32)]
+        scratch_shapes=[pltpu.VMEM((width, width), F32)]
         + [pltpu.VMEM((width, hidden), F32)] * 2
         + [pltpu.VMEM(value.shape, F32) for value in kept]
         + [pltpu.VMEM((width, hidden + 256), F32)] * 2
-        + [pltpu.SemaphoreType.DMA((12,)), pltpu.SemaphoreType.DMA((4,))],
-        compiler_params=limit(NEAR_MIB),
+        + [pltpu.SemaphoreType.DMA((9,)), pltpu.SemaphoreType.DMA((4,))],
+        compiler_params=limit(44),
         cost_estimate=pl.CostEstimate(flops=8 << 30, bytes_accessed=28 << 20, transcendentals=1 << 19),
         name="middle",
     )(place, *operands)
@@ -650,19 +670,17 @@
     factors_out_ref[count:, :] = jnp.concatenate(added, axis=0)
 
 
-def class_finish(partials, terms, class_tokens, vectors, matrices, factors):
-    operands = [*partials, *far_off(terms, class_tokens, vectors, matrices, factors)]
-    specs = [whole(operand.shape) for operand in operands]
-    specs[-2] = weight_block(1, 0, matrices.shape, 2 * class_tokens.shape[1])
+def class_finish(partials, terms, class_tokens, vectors, w_first, factors):
+    operands = [*partials, *far_off(terms, class_tokens, vectors), w_first, *far_off(factors)]
+    vmem = pl.BlockSpec(memory_space=pltpu.VMEM)
     outs = [struct(class_tokens.shape), struct((factors.shape[0] + 8, factors.shape[1]))]
     return pl.pallas_call(
         functools.partial(class_kernel, len(partials)),
-        grid=(1,),
-        in_specs=specs,
-        out_specs=[whole(out.shape) for out in outs],
+        in_specs=[vmem] * len(operands),
+        out_specs=[vmem] * len(outs),
         out_shape=outs,
-        compiler_params=limit(SMALL_MIB),
-        cost_estimate=pl.CostEstimate(flops=1 << 29, bytes_accessed=3 << 20, transcendentals=0),
+        compiler_params=limit(12),
+        cost_estimate=pl.CostEstimate(flops=1, bytes_accessed=1, transcendentals=0),
         name="class_finish",
     )(*operands)
 
@@ -1118,6 +1136,26 @@
         return sum_of(self.terms)
 
 
+def join_kernel(*refs):
+    out_ref, at = refs[-1], 0
+    for ref in refs[:-1]:
+        out_ref[at : at + ref.shape[0]] = ref[...]
+        at += ref.shape[0]
+
+
+def join(parts):
+    shape = (sum(part.shape[0] for part in parts),) + parts[0].shape[1:]
+    return pl.pallas_call(
+        join_kernel,
+        in_specs=[pl.BlockSpec(memory_space=pltpu.VMEM)] * len(parts),
+        out_specs=pl.BlockSpec(memory_space=pltpu.VMEM),
+        out_shape=struct(shape),
+        compiler_params=limit(SMALL_MIB),
+        cost_estimate=pl.CostEstimate(flops=1, bytes_accessed=1, transcendentals=0),
+        name="join",
+    )(*parts)
+
+
 class Gather:
     def __init__(self, value, places):
         self.places = places
@@ -1139,7 +1177,7 @@
     def set_received(self, values):
         group = self.groups.pop(0)
         if group[0][0] == "dp":
-            self.value = jnp.concatenate([self.value, *values], axis=0)
+            self.value = join([self.value, *values])
         else:
             self.value = jnp.concatenate(self.places.pair(self.value, values[0], group[0]), axis=1)
         self.others = []
@@ -1217,18 +1255,19 @@
         [query, k1, k2, v1, v2, kt1, kt2, vt1, vt2],
     )
     parts = [packed] + [swap(packed, "seq", seq_size, bit) for bit in range(1, seq_size)]
+    *staged, w_first = class_stage(tie(place, packed), matrices)
     (
         class_out, d_attended, d_mixed, early_keep, early_send, partial, factors, vec_rows, class_terms,
     ) = middle(
         place, parts, vectors, prepared, class_tokens, cot_class, cot_patch,
-        patch_out, scores, [attended, *kept], matrices,
+        patch_out, scores, staged, [attended, *kept], matrices,
     )
 
     core, chips, dp = ("seq", 1), bits_of("seq", seq_size, 2), bits_of("dp", dp_size)
     pairs = lambda steps: [tuple(steps[i : i + 2]) for i in range(0, len(steps), 2)]
     other = places.swap(early_send, [core])
     partials = [partial] + [swap(partial, "seq", seq_size, bit) for bit in range(1, seq_size)]
-    grad_class, factors = class_finish(partials, class_terms, class_tokens, vectors, matrices, factors)
+    grad_class, factors = class_finish(partials, class_terms, class_tokens, vectors, w_first, factors)
     gather = Gather(places.share(factors, factors.shape[0] // seq_size), places)
     other, gather.value = together(other, gather.value)
     early = Reduce(

time: 192 us -> 190 us (0.990)
  waiting for transfers between devices: 41.6 us -> 39.2 us
  Pallas kernels: 99.8 us -> 102 us
    ppermute x10, waiting for transfers between devices: 13.4 us -> 10.3 us  [swap(): lax.ppermute(value, axis, [(place, place ^ bit) for place in range(size)])]
    pallas_call x2 -> x5, Pallas kernels: 19.2 us -> 21 us  [the longest x1 15.7 us: middle(): pl.pallas_call(functools.partial(middle_kernel, images, len(parts)), in_s...]
  transfers between devices with their start and end apart: 37 -> 37, of which waited for: 19 -> 17; matrix products, arithmetic and copies ran while one was open for 5% -> 4% of each run, Pallas kernels for 27% -> 29%
where the time goes in v3:
time: 190 us; the launch traced here: 187 us
  Pallas kernels  102 us (54%)
  waiting for transfers between devices  39.2 us (21%)
  starting transfers between devices  31.8 us (17%)
  other arithmetic  10 us (5%)
  local copies, waits for them, and re-layouts  2.66 us (1%)
    pallas_call x1, Pallas kernels, backward(): pl.pallas_call(functools.partial(backward_kernel, slots, lengths.shape[1]...  35.7 us
    ppermute x27, waiting for transfers between devices, swap(): lax.ppermute(value, ('dp', 'seq'), [(place, place ^ flip) for place in ra...  29 us
    pallas_call x1, Pallas kernels, forward(): pl.pallas_call(functools.partial(forward_kernel, slots, lengths.shape[1],...  25.5 us
    ppermute x27, starting transfers between devices, swap(): lax.ppermute(value, ('dp', 'seq'), [(place, place ^ flip) for place in ra...  23.8 us
    pallas_call x1, Pallas kernels, middle(): pl.pallas_call(functools.partial(middle_kernel, images, len(parts)), in_s...  15.7 us
    ppermute x10, waiting for transfers between devices, swap(): lax.ppermute(value, axis, [(place, place ^ bit) for place in range(size)])  10.3 us
    add x8, other arithmetic, sum_of(): total = total + term  9.37 us
    ppermute x10, starting transfers between devices, swap(): lax.ppermute(value, axis, [(place, place ^ bit) for place in range(size)])  7.95 us
  transfers between devices with their start and end apart: 37, of which 17 were waited for; matrix products, arithmetic and copies ran while one was open for 4% of the time, Pallas kernels for 29%

profile of v3, /device:TPU:0, one launch (start us, length us, event | category | flops | bytes accessed | tf_op | source)
XLA Modules:
  0.0 186.6 jit_solution(2595367576081411000)
XLA Ops:
  1.2 2.6 %collective-permute-start = (f32[256,384]{1,0:T(8,128)}, f32[256,384]{1,0:T(8,128)S(1)}, u32[]{:S(2)}, u32[]{:S(2)}) collective-permute-start(f32[256,384]{1,0:T(8,128)} %tokens_ref), channel_id=1, source_target_pairs={{0,2},{1,3},{2,0},{3,1},{4,6},{5,7},{6,4},{7,5},{8,10},{9,11},{10,... | collective-permute-start | bytes 1179656 | tf_op jit(solution)/shard_map/ppermute | solution.py:1033
  3.8 6.4 %prepare.1 = (f32[4,384]{1,0:T(4,128)}, f32[4,384]{1,0:T(4,128)}, f32[4,384]{1,0:T(4,128)}, f32[32,384]{1,0:T(8,128)}, f32[32,128]{1,0:T(8,128)}, /*index=5*/f32...) custom-call(f32[256,384]{1,0:T(8,128)} %tokens_ref, ...), custom_call_target="tpu_custom_call" | custom-call | flops 4294967296 | bytes 8388608 | tf_op jit(solution)/shard_map/prepare/pallas_call | solution.py:273
  10.2 3.5 %collective-permute-done.refs_3_.refs_4_ = f32[256,384]{1,0:T(8,128)S(1)} collective-permute-done((f32[256,384]{1,0:T(8,128)}, f32[256,384]{1,0:T(8,128)S(1)}, u32[]{:S(2)}, u32[]{:S(2)}) %collective-permute-start) | collective-permute-done | bytes 393248 | tf_op jit(solution)/shard_map/ppermute | solution.py:1033
  13.7 1.7 collective-permute-done.2.refs_4_.refs_5_
  15.5 25.5 %forward.1 = (bf16[8,1024,256]{2,1,0:T(8,128)(2,1)}, bf16[8,1024,256]{2,1,0:T(8,128)(2,1)}, f32[8,384,256]{2,1,0:T(8,128)}, f32[8,1,256]{2,1,0:T(1,128)}, f32[38...) custom-call(s32[1]{0:T(128)} %bitcast.refs_0_.place_ref, ...), custom_call_target="tpu_custom_call" | custom-call | flops 12306087936 | bytes 25165824 | tf_op jit(solution)/shard_map/forward/pallas_call | solution.py:436
  41.1 1.8 collective-permute-start.4
  42.9 3.1 %class_stage.1 = (f32[384,768]{1,0:T(8,128)S(1)}, f32[384,1536]{1,0:T(8,128)S(1)}, f32[384,1536]{1,0:T(8,128)S(1)}, f32[384,768]{1,0:T(8,128)S(1)}) custom-call(s32[1]{0:T(128)} %bitcast.refs_0_.place_ref, f32[2,3,384,1536]{3,2,1,0:T(8,128)} %w_ref.1), custom_call_target="tpu_custom_call" | custom-call | flops 1 | bytes 1 | tf_op jit(solution)/shard_map/class_stage/pallas_call | solution.py:483
  47.2 15.7 %middle.1 = (f32[4,384]{1,0:T(4,128)}, f32[256,384]{1,0:T(8,128)}, f32[256,384]{1,0:T(8,128)}, f32[384,1792]{1,0:T(8,128)}, f32[384,1792]{1,0:T(8,128)}, /*index...) custom-call(s32[1]{0:T(128)} %bitcast.refs_0_.place_ref, f32[32,512]{1,0:T(8,128)S(1)} %copy-done.5, ...), custom_call_target="tpu_custom_call" | custom-call | flops 8589934592 | bytes 29360128 | tf_op jit(solution)/shard_map/middle/pallas_call | solution.py:634
  64.9 3.1 %collective-permute-done.7.refs_1_ = f32[32,384]{1,0:T(8,128)S(1)} collective-permute-done((f32[32,384]{1,0:T(8,128)}, f32[32,384]{1,0:T(8,128)S(1)}, u32[]{:S(2)}, u32[]{:S(2)}) %collective-permute-start.7) | collective-permute-done | bytes 49184 | tf_op jit(solution)/shard_map/ppermute | solution.py:1033
  69.6 2.2 %class_finish.1 = (f32[4,384]{1,0:T(4,128)}, f32[136,384]{1,0:T(8,128)S(1)}) custom-call(f32[32,384]{1,0:T(8,128)S(1)} %copy-done.2, f32[32,384]{1,0:T(8,128)S(1)} %collective-permute-done.7.refs_1_, f32[32,384]{1,0:T(8,128)S(1)} %collective-permute-done.8.refs_2_, f32[32,384]{1,0:T(8,128)S(1)} %collective-permute-done.9.refs_3_, ...), custom_call_target="tpu_custom_call" | custom-call | flops 1 | bytes 1 | tf_op jit(solution)/shard_map/class_finish/pallas_call | solution.py:677
  71.8 2.4 %add_bitcast_fusion = (f32[2,48,1792]{2,1,0:T(8,128)S(1)}, f32[2,48,1792]{2,1,0:T(8,128)S(1)}, f32[2,48,1792]{2,1,0:T(8,128)S(1)}) fusion(f32[2,2,2,48,1792]{4,3,2,1,0:T(8,128)} %bitcast.4, u32[]{:T(128)S(6)} %convert_element_type.33, u32[]{:T(128)S(6)} %convert_element_type.31, f32[2,2,2,48,1792]{4,3,2,1,0:T(8,128)} %bitcast.79, ...), kind=kLoop, calls=%fused_computation.4 | loop fusion | flops 516096 | bytes 6193168 | tf_op jit(solution)/shard_map/add | solution.py:1211
  77.7 2.6 %collective-permute-start.13 = (f32[1,34,384]{2,1,0:T(8,128)S(1)}, f32[1,34,384]{2,1,0:T(8,128)S(1)}, u32[]{:S(2)}, u32[]{:S(2)}) collective-permute-start(f32[1,34,384]{2,1,0:T(8,128)S(1)} %dynamic-slice_bitcast_fusion.refs_0_), channel_id=1, source_target_pairs={{0,16},{1,17},{2,18},{3,19},{4,20},{5,21},{6,22},{7,23},{8,24},{9,... | collective-permute-start | bytes 156680 | tf_op jit(solution)/shard_map/ppermute | solution.py:1086
  80.3 35.7 %backward.1 = (f32[2,256,384]{2,1,0:T(8,128)}, f32[2,256,384]{2,1,0:T(8,128)}, f32[384,640]{1,0:T(8,128)}, f32[384,640]{1,0:T(8,128)}) custom-call(s32[1]{0:T(128)} %bitcast.refs_0_.place_ref, s32[1,4]{1,0:T(1,128)S(1)} %copy-done.6, f32[256,384]{1,0:T(8,128)} %tokens_ref, f32[256,384]{1,0:T(8,128)} %copy-done.1, f32[256,384]{1,0:T(8,128)} %copy-done.3, ...), custom_call_target="tpu_custom_call" | custom-call | flops 22951231488 | bytes 25165824 | tf_op jit(solution)/shard_map/backward/pallas_call | solution.py:853
  117.6 2.3 %bitcast_add_fusion.3 = f32[48,1792]{1,0:T(8,128)} fusion(f32[2,48,1792]{2,1,0:T(8,128)} %copy-done.12, u32[]{:T(128)S(6)} %convert_element_type.35, f32[2,48,1792]{2,1,0:T(8,128)} %copy-done.11, f32[2,48,1792]{2,1,0:T(8,128)} %copy-done.10, f32[2,2,2,48,1792]{4,3,2,1,0:T(8,128)} %bitcast.4, u32[]{:T(128)S(6)} %optimization_barrier.259, ...), kind=kLoop, calls=%fused_computation.15 | loop fusion | flops 344064 | bytes 2064400 | tf_op jit(solution)/shard_map/add | solution.py:1211
  129.1 3.4 %collective-permute-done.17.refs_2_ = f32[2,34,384]{2,1,0:T(8,128)S(1)} collective-permute-done((f32[2,34,384]{2,1,0:T(8,128)S(1)}, f32[2,34,384]{2,1,0:T(8,128)S(1)}, u32[]{:S(2)}, u32[]{:S(2)}) %collective-permute-start.17) | collective-permute-done | bytes 104480 | tf_op jit(solution)/shard_map/ppermute | solution.py:1086
  137.7 9.0 %collective-permute-done.21 = f32[2,48,640]{2,1,0:T(8,128)} collective-permute-done((f32[2,48,640]{2,1,0:T(8,128)}, f32[2,48,640]{2,1,0:T(8,128)}, u32[]{:S(2)}, u32[]{:S(2)}) %collective-permute-start.21) | collective-permute-done | bytes 245792 | tf_op jit(solution)/shard_map/ppermute | solution.py:1086
  146.6 2.7 %collective-permute-done.22 = f32[2,48,640]{2,1,0:T(8,128)} collective-permute-done((f32[2,48,640]{2,1,0:T(8,128)}, f32[2,48,640]{2,1,0:T(8,128)}, u32[]{:S(2)}, u32[]{:S(2)}) %collective-permute-start.22) | collective-permute-done | bytes 245792 | tf_op jit(solution)/shard_map/ppermute | solution.py:1086
  155.1 3.7 %stage.1 = (f32[2,3,48,1536]{3,2,1,0:T(8,128)S(1)}, f32[2,3,48,1536]{3,2,1,0:T(8,128)S(1)}, f32[2,3,48,1536]{3,2,1,0:T(8,128)S(1)}, f32[2,3,48,1536]{3,2,1,0:T(8,128)S(1)}) custom-call(s32[2]{0:T(128)S(1)} %pad_add_fusion.place_ref.refs_0_, f32[2,3,384,1536]{3,2,1,0:T(8,128)} %w_ref.1, f32[2,3,48,1536]{3,2,1,0:T(8,128)} %m1_ref.1, ...), custom_call_target="tpu_custom_call" | custom-call | flops 1 | bytes 1 | tf_op jit(solution)/shard_map/stage/pallas_call | solution.py:947
  158.7 3.0 %collective-permute-done.25 = f32[48,640]{1,0:T(8,128)S(1)} collective-permute-done((f32[48,640]{1,0:T(8,128)S(1)}, f32[48,640]{1,0:T(8,128)S(1)}, u32[]{:S(2)}, u32[]{:S(2)}) %collective-permute-start.25) | collective-permute-done | bytes 122912 | tf_op jit(solution)/shard_map/ppermute | solution.py:1086
  165.1 2.7 %collective-permute-done.27.refs_6_ = f32[48,640]{1,0:T(8,128)S(1)} collective-permute-done((f32[48,640]{1,0:T(8,128)S(1)}, f32[48,640]{1,0:T(8,128)S(1)}, u32[]{:S(2)}, u32[]{:S(2)}) %collective-permute-start.27) | collective-permute-done | bytes 122912 | tf_op jit(solution)/shard_map/ppermute | solution.py:1086
  172.8 2.1 %collective-permute-start.33 = (f32[8,128]{1,0:T(8,128)S(1)}, f32[8,128]{1,0:T(8,128)S(1)}, u32[]{:S(2)}, u32[]{:S(2)}) collective-permute-start(f32[8,128]{1,0:T(8,128)S(1)} %add_add_fusion.1), channel_id=1, source_target_pairs={{0,16},{1,17},{2,18},{3,19},{4,20},{5,21},{6,22},{7,23},{8,24},{9,... | collective-permute-start | bytes 12296 | tf_op jit(solution)/shard_map/ppermute | solution.py:1086
  174.9 2.2 %collective-permute-start.34 = (f32[8,128]{1,0:T(8,128)S(1)}, f32[8,128]{1,0:T(8,128)S(1)}, u32[]{:S(2)}, u32[]{:S(2)}) collective-permute-start(f32[8,128]{1,0:T(8,128)S(1)} %add_add_fusion.1), channel_id=1, source_target_pairs={{0,24},{1,25},{2,26},{3,27},{4,28},{5,29},{6,30},{7,31},{8,16},{9,... | collective-permute-start | bytes 12296 | tf_op jit(solution)/shard_map/ppermute | solution.py:1086
  177.1 2.2 %token_grad.1 = f32[256,384]{1,0:T(8,128)} custom-call(f32[256,384]{1,0:T(8,128)} %tokens_ref, f32[28,384]{1,0:T(8,128)} %refs_12_.3, f32[256,384]{1,0:T(8,128)S(1)} %get-tuple-element.312.own_ref, f32[256,384]{1,0:T(8,128)S(1)} %get-tuple-element.313.near_ref, f32[256,384]{1,0:T(8,128)S(1)} %collective-permute-done.24.far_ref, ...), custom_call_target="tpu_custom_call" | custom-call | flops 2097152 | bytes 2097152 | tf_op jit(solution)/shard_map/token_grad/pallas_call | solution.py:884
  180.3 6.0 %optimizer.1 = (f32[1,1]{1,0:T(1,128)}, f32[2,3,48,1536]{3,2,1,0:T(8,128)}, f32[2,3,48,1536]{3,2,1,0:T(8,128)}, f32[2,3,48,1536]{3,2,1,0:T(8,128)}, f32[2,3,48,1...) custom-call(s32[2]{0:T(128)S(1)} %pad_add_fusion.place_ref.refs_0_, ...), custom_call_target="tpu_custom_call" | custom-call | flops 8388608 | bytes 14680064 | tf_op jit(solution)/shard_map/optimizer/pallas_call | solution.py:1019
  (106 shorter events, 40.0 us)
Async XLA Ops:
  1.2 12.5 %collective-permute-start = (f32[256,384]{1,0:T(8,128)}, f32[256,384]{1,0:T(8,128)S(1)}, u32[]{:S(2)}, u32[]{:S(2)}) collective-permute-start(f32[256,384]{1,0:T(8,128)} %tokens_ref), channel_id=1, source_target_pairs={{0,2},{1,3},{2,0},{3,1},{4,6},{5,7},{6,4},{7,5},{8,10},{9,11},{10,... | collective-permute-start | bytes 1179656 | tf_op jit(solution)/shard_map/ppermute | solution.py:1033
  41.0 5.0 %collective-permute-start.3 = (f32[32,512]{1,0:T(8,128)}, f32[32,512]{1,0:T(8,128)S(1)}, u32[]{:S(2)}, u32[]{:S(2)}) collective-permute-start(f32[32,512]{1,0:T(8,128)} %get-tuple-element.175.refs_1_), channel_id=1, source_target_pairs={{0,1},{1,0},{2,3},{3,2},{4,5},{5,4},{6,7},{7,6},{8,9},{9,8},{10,11... | collective-permute-start | bytes 196616 | tf_op jit(solution)/shard_map/ppermute | solution.py:1033
  62.9 8.9 %collective-permute-start.6 = (f32[384,1792]{1,0:T(8,128)}, f32[384,1792]{1,0:T(8,128)}, u32[]{:S(2)}, u32[]{:S(2)}) collective-permute-start(f32[384,1792]{1,0:T(8,128)} %get-tuple-element.195), channel_id=1, source_target_pairs={{0,1},{1,0},{2,3},{3,2},{4,5},{5,4},{6,7},{7,6},{8,9},{9,8},{10,11... | collective-permute-start | bytes 8257544 | tf_op jit(solution)/shard_map/ppermute | solution.py:1086
  63.0 5.0 %collective-permute-start.7 = (f32[32,384]{1,0:T(8,128)}, f32[32,384]{1,0:T(8,128)S(1)}, u32[]{:S(2)}, u32[]{:S(2)}) collective-permute-start(f32[32,384]{1,0:T(8,128)} %get-tuple-element.196.refs_0_), channel_id=1, source_target_pairs={{0,1},{1,0},{2,3},{3,2},{4,5},{5,4},{6,7},{7,6},{8,9},{9,8},{10,11... | collective-permute-start | bytes 147464 | tf_op jit(solution)/shard_map/ppermute | solution.py:1033
  74.2 41.9 %collective-permute-start.10 = (f32[2,48,1792]{2,1,0:T(8,128)S(1)}, f32[2,48,1792]{2,1,0:T(8,128)S(1)}, u32[]{:S(2)}, u32[]{:S(2)}) collective-permute-start(f32[2,48,1792]{2,1,0:T(8,128)S(1)} %get-tuple-element.222), channel_id=1, source_target_pairs={{0,4},{1,5},{2,6},{3,7},{4,0},{5,1},{6,2},{7,3},{8,12},{9,13},{10,... | collective-permute-start | bytes 2064392 | tf_op jit(solution)/shard_map/ppermute | solution.py:1086
  75.7 40.3 %collective-permute-start.11 = (f32[2,48,1792]{2,1,0:T(8,128)S(1)}, f32[2,48,1792]{2,1,0:T(8,128)S(1)}, u32[]{:S(2)}, u32[]{:S(2)}) collective-permute-start(f32[2,48,1792]{2,1,0:T(8,128)S(1)} %get-tuple-element.223), channel_id=1, source_target_pairs={{0,8},{1,9},{2,10},{3,11},{4,12},{5,13},{6,14},{7,15},{8,0},{9,1},... | collective-permute-start | bytes 2064392 | tf_op jit(solution)/shard_map/ppermute | solution.py:1086
  77.3 38.8 %collective-permute-start.12 = (f32[2,48,1792]{2,1,0:T(8,128)S(1)}, f32[2,48,1792]{2,1,0:T(8,128)S(1)}, u32[]{:S(2)}, u32[]{:S(2)}) collective-permute-start(f32[2,48,1792]{2,1,0:T(8,128)S(1)} %get-tuple-element.224), channel_id=1, source_target_pairs={{0,12},{1,13},{2,14},{3,15},{4,8},{5,9},{6,10},{7,11},{8,4},{9,5},... | collective-permute-start | bytes 2064392 | tf_op jit(solution)/shard_map/ppermute | solution.py:1086
  77.7 38.3 %collective-permute-start.13 = (f32[1,34,384]{2,1,0:T(8,128)S(1)}, f32[1,34,384]{2,1,0:T(8,128)S(1)}, u32[]{:S(2)}, u32[]{:S(2)}) collective-permute-start(f32[1,34,384]{2,1,0:T(8,128)S(1)} %dynamic-slice_bitcast_fusion.refs_0_), channel_id=1, source_target_pairs={{0,16},{1,17},{2,18},{3,19},{4,20},{5,21},{6,22},{7,23},{8,24},{9,... | collective-permute-start | bytes 156680 | tf_op jit(solution)/shard_map/ppermute | solution.py:1086
  121.2 28.1 %collective-permute-start.24 = (f32[256,384]{1,0:T(8,128)S(1)}, f32[256,384]{1,0:T(8,128)S(1)}, u32[]{:S(2)}, u32[]{:S(2)}) collective-permute-start(f32[256,384]{1,0:T(8,128)S(1)} %get-tuple-element.311), channel_id=1, source_target_pairs={{0,2},{1,3},{2,0},{3,1},{4,6},{5,7},{6,4},{7,5},{8,10},{9,11},{10,... | collective-permute-start | bytes 1179656 | tf_op jit(solution)/shard_map/ppermute | solution.py:1033
  122.3 5.2 %collective-permute-start.16 = (f32[2,34,384]{2,1,0:T(8,128)S(1)}, f32[2,34,384]{2,1,0:T(8,128)S(1)}, u32[]{:S(2)}, u32[]{:S(2)}) collective-permute-start(f32[2,34,384]{2,1,0:T(8,128)S(1)} %join.2.refs_0_), channel_id=1, source_target_pairs={{0,4},{1,5},{2,6},{3,7},{4,0},{5,1},{6,2},{7,3},{8,12},{9,13},{10,... | collective-permute-start | bytes 313352 | tf_op jit(solution)/shard_map/ppermute | solution.py:1086
  123.8 8.7 %collective-permute-start.17 = (f32[2,34,384]{2,1,0:T(8,128)S(1)}, f32[2,34,384]{2,1,0:T(8,128)S(1)}, u32[]{:S(2)}, u32[]{:S(2)}) collective-permute-start(f32[2,34,384]{2,1,0:T(8,128)S(1)} %join.2.refs_0_), channel_id=1, source_target_pairs={{0,8},{1,9},{2,10},{3,11},{4,12},{5,13},{6,14},{7,15},{8,0},{9,1},... | collective-permute-start | bytes 313352 | tf_op jit(solution)/shard_map/ppermute | solution.py:1086
  125.4 8.4 %collective-permute-start.18 = (f32[2,34,384]{2,1,0:T(8,128)S(1)}, f32[2,34,384]{2,1,0:T(8,128)S(1)}, u32[]{:S(2)}, u32[]{:S(2)}) collective-permute-start(f32[2,34,384]{2,1,0:T(8,128)S(1)} %join.2.refs_0_), channel_id=1, source_target_pairs={{0,12},{1,13},{2,14},{3,15},{4,8},{5,9},{6,10},{7,11},{8,4},{9,5},... | collective-permute-start | bytes 313352 | tf_op jit(solution)/shard_map/ppermute | solution.py:1086
  125.8 23.5 %collective-permute-start.23 = (f32[48,1792]{1,0:T(8,128)}, f32[48,1792]{1,0:T(8,128)}, u32[]{:S(2)}, u32[]{:S(2)}) collective-permute-start(f32[48,1792]{1,0:T(8,128)} %bitcast_add_fusion.3), channel_id=1, source_target_pairs={{0,16},{1,17},{2,18},{3,19},{4,20},{5,21},{6,22},{7,23},{8,24},{9,... | collective-permute-start | bytes 1032200 | tf_op jit(solution)/shard_map/ppermute | solution.py:1086
  127.5 9.1 %collective-permute-start.20 = (f32[2,48,640]{2,1,0:T(8,128)}, f32[2,48,640]{2,1,0:T(8,128)S(1)}, u32[]{:S(2)}, u32[]{:S(2)}) collective-permute-start(f32[2,48,640]{2,1,0:T(8,128)} %get-tuple-element.241), channel_id=1, source_target_pairs={{0,4},{1,5},{2,6},{3,7},{4,0},{5,1},{6,2},{7,3},{8,12},{9,13},{10,... | collective-permute-start | bytes 737288 | tf_op jit(solution)/shard_map/ppermute | solution.py:1086
  132.5 14.1 %collective-permute-start.21 = (f32[2,48,640]{2,1,0:T(8,128)}, f32[2,48,640]{2,1,0:T(8,128)}, u32[]{:S(2)}, u32[]{:S(2)}) collective-permute-start(f32[2,48,640]{2,1,0:T(8,128)} %get-tuple-element.242), channel_id=1, source_target_pairs={{0,8},{1,9},{2,10},{3,11},{4,12},{5,13},{6,14},{7,15},{8,0},{9,1},... | collective-permute-start | bytes 737288 | tf_op jit(solution)/shard_map/ppermute | solution.py:1086
  133.8 15.5 %collective-permute-start.22 = (f32[2,48,640]{2,1,0:T(8,128)}, f32[2,48,640]{2,1,0:T(8,128)}, u32[]{:S(2)}, u32[]{:S(2)}) collective-permute-start(f32[2,48,640]{2,1,0:T(8,128)} %get-tuple-element.243), channel_id=1, source_target_pairs={{0,12},{1,13},{2,14},{3,15},{4,8},{5,9},{6,10},{7,11},{8,4},{9,5},... | collective-permute-start | bytes 737288 | tf_op jit(solution)/shard_map/ppermute | solution.py:1086
  136.6 15.4 %collective-permute-start.19 = (f32[8,34,384]{2,1,0:T(8,128)S(1)}, f32[8,34,384]{2,1,0:T(8,128)S(1)}, u32[]{:S(2)}, u32[]{:S(2)}) collective-permute-start(f32[8,34,384]{2,1,0:T(8,128)S(1)} %join.3), channel_id=1, source_target_pairs={{0,2},{1,3},{2,0},{3,1},{4,6},{5,7},{6,4},{7,5},{8,10},{9,11},{10,... | collective-permute-start | bytes 1253384 | tf_op jit(solution)/shard_map/ppermute | solution.py:1086
  152.5 9.3 %collective-permute-start.25 = (f32[48,640]{1,0:T(8,128)S(1)}, f32[48,640]{1,0:T(8,128)S(1)}, u32[]{:S(2)}, u32[]{:S(2)}) collective-permute-start(f32[48,640]{1,0:T(8,128)S(1)} %bitcast_add_fusion.9), channel_id=1, source_target_pairs={{0,16},{1,17},{2,18},{3,19},{4,20},{5,21},{6,22},{7,23},{8,24},{9,... | collective-permute-start | bytes 368648 | tf_op jit(solution)/shard_map/ppermute | solution.py:1086
  152.8 12.3 %collective-permute-start.28 = (f32[48,1792]{1,0:T(8,128)S(1)}, f32[48,1792]{1,0:T(8,128)S(1)}, u32[]{:S(2)}, u32[]{:S(2)}) collective-permute-start(f32[48,1792]{1,0:T(8,128)S(1)} %fusion.1.refs_3_), channel_id=1, source_target_pairs={{0,2},{1,3},{2,0},{3,1},{4,6},{5,7},{6,4},{7,5},{8,10},{9,11},{10,... | collective-permute-start | bytes 1032200 | tf_op jit(solution)/shard_map/ppermute | solution.py:1086
  162.8 5.0 %collective-permute-start.27 = (f32[48,640]{1,0:T(8,128)S(1)}, f32[48,640]{1,0:T(8,128)S(1)}, u32[]{:S(2)}, u32[]{:S(2)}) collective-permute-start(f32[48,640]{1,0:T(8,128)S(1)} %fusion.2.refs_5_), channel_id=1, source_target_pairs={{0,2},{1,3},{2,0},{3,1},{4,6},{5,7},{6,4},{7,5},{8,10},{9,11},{10,... | collective-permute-start | bytes 368648 | tf_op jit(solution)/shard_map/ppermute | solution.py:1086
  170.0 10.3 %collective-permute-start.35 = (f32[48,1792]{1,0:T(8,128)S(1)}, f32[48,1792]{1,0:T(8,128)S(1)}, u32[]{:S(2)}, u32[]{:S(2)}) collective-permute-start(f32[48,1792]{1,0:T(8,128)S(1)} %get-tuple-element.281.refs_2_), channel_id=1, source_target_pairs={{0,1},{1,0},{2,3},{3,2},{4,5},{5,4},{6,7},{7,6},{8,9},{9,8},{10,11... | collective-permute-start | bytes 1032200 | tf_op jit(solution)/shard_map/ppermute | solution.py:1086
  172.7 6.6 %collective-permute-start.32 = (f32[8,128]{1,0:T(8,128)S(1)}, f32[8,128]{1,0:T(8,128)S(1)}, u32[]{:S(2)}, u32[]{:S(2)}) collective-permute-start(f32[8,128]{1,0:T(8,128)S(1)} %add_add_fusion.1), channel_id=1, source_target_pairs={{0,8},{1,9},{2,10},{3,11},{4,12},{5,13},{6,14},{7,15},{8,0},{9,1},... | collective-permute-start | bytes 12296 | tf_op jit(solution)/shard_map/ppermute | solution.py:1086
  172.8 6.6 %collective-permute-start.33 = (f32[8,128]{1,0:T(8,128)S(1)}, f32[8,128]{1,0:T(8,128)S(1)}, u32[]{:S(2)}, u32[]{:S(2)}) collective-permute-start(f32[8,128]{1,0:T(8,128)S(1)} %add_add_fusion.1), channel_id=1, source_target_pairs={{0,16},{1,17},{2,18},{3,19},{4,20},{5,21},{6,22},{7,23},{8,24},{9,... | collective-permute-start | bytes 12296 | tf_op jit(solution)/shard_map/ppermute | solution.py:1086
  174.9 5.4 %collective-permute-start.34 = (f32[8,128]{1,0:T(8,128)S(1)}, f32[8,128]{1,0:T(8,128)S(1)}, u32[]{:S(2)}, u32[]{:S(2)}) collective-permute-start(f32[8,128]{1,0:T(8,128)S(1)} %add_add_fusion.1), channel_id=1, source_target_pairs={{0,24},{1,25},{2,26},{3,27},{4,28},{5,29},{6,30},{7,31},{8,16},{9,... | collective-permute-start | bytes 12296 | tf_op jit(solution)/shard_map/ppermute | solution.py:1086
  (26 other events, 151.4 us)

commit v4 on v3

--- a/solution.py
+++ b/solution.py
@@ -671,7 +671,8 @@
 
 
 def class_finish(partials, terms, class_tokens, vectors, w_first, factors):
-    operands = [*partials, *far_off(terms, class_tokens, vectors), w_first, *far_off(factors)]
+    operands = [*far_off(partials[0]), *partials[1:], *far_off(terms, class_tokens, vectors), w_first]
+    operands += far_off(factors)
     vmem = pl.BlockSpec(memory_space=pltpu.VMEM)
     outs = [struct(class_tokens.shape), struct((factors.shape[0] + 8, factors.shape[1]))]
     return pl.pallas_call(
@@ -865,7 +866,7 @@
             pltpu.VMEM((slots, rows, width), F32),
             pltpu.SemaphoreType.DMA((1 + slots,)),
         ],
-        compiler_params=limit(NEAR_MIB if total <= 1024 else KERNEL_MIB),
+        compiler_params=limit(46 if total <= 1024 else KERNEL_MIB),
         cost_estimate=pl.CostEstimate(
             flops=6 * (4 * heads + 6) * total * rows * width, bytes_accessed=24 << 20, transcendentals=0
         ),

time: 190 us -> 189 us (level)
  no operation moved by 1% of the time
where the time goes in v4:
time: 189 us; the launch traced here: 186 us
  Pallas kernels  102 us (54%)
  waiting for transfers between devices  39.2 us (21%)
  starting transfers between devices  31.8 us (17%)
  other arithmetic  10 us (5%)
    pallas_call x1, Pallas kernels, backward(): pl.pallas_call(functools.partial(backward_kernel, slots, lengths.shape[1]...  35.7 us
    ppermute x27, waiting for transfers between devices, swap(): lax.ppermute(value, ('dp', 'seq'), [(place, place ^ flip) for place in ra...  29 us
    pallas_call x1, Pallas kernels, forward(): pl.pallas_call(functools.partial(forward_kernel, slots, lengths.shape[1],...  25.5 us
    ppermute x27, starting transfers between devices, swap(): lax.ppermute(value, ('dp', 'seq'), [(place, place ^ flip) for place in ra...  23.8 us
    pallas_call x1, Pallas kernels, middle(): pl.pallas_call(functools.partial(middle_kernel, images, len(parts)), in_s...  15.7 us
    ppermute x10, waiting for transfers between devices, swap(): lax.ppermute(value, axis, [(place, place ^ bit) for place in range(size)])  10.3 us
    add x8, other arithmetic, sum_of(): total = total + term  9.36 us
    ppermute x10, starting transfers between devices, swap(): lax.ppermute(value, axis, [(place, place ^ bit) for place in range(size)])  7.95 us
  transfers between devices with their start and end apart: 37, of which 17 were waited for; matrix products, arithmetic and copies ran while one was open for 4% of the time, Pallas kernels for 29%

profile of v4, /device:TPU:0, one launch (start us, length us, event | category | flops | bytes accessed | tf_op | source)
XLA Modules:
  0.0 185.8 jit_solution(4315537229448003531)
XLA Ops:
  1.2 2.6 %collective-permute-start = (f32[256,384]{1,0:T(8,128)}, f32[256,384]{1,0:T(8,128)S(1)}, u32[]{:S(2)}, u32[]{:S(2)}) collective-permute-start(f32[256,384]{1,0:T(8,128)} %tokens_ref), channel_id=1, source_target_pairs={{0,2},{1,3},{2,0},{3,1},{4,6},{5,7},{6,4},{7,5},{8,10},{9,11},{10,... | collective-permute-start | bytes 1179656 | tf_op jit(solution)/shard_map/ppermute | solution.py:1034
  3.8 6.4 %prepare.1 = (f32[4,384]{1,0:T(4,128)}, f32[4,384]{1,0:T(4,128)}, f32[4,384]{1,0:T(4,128)}, f32[32,384]{1,0:T(8,128)}, f32[32,128]{1,0:T(8,128)}, /*index=5*/f32...) custom-call(f32[256,384]{1,0:T(8,128)} %tokens_ref, ...), custom_call_target="tpu_custom_call" | custom-call | flops 4294967296 | bytes 8388608 | tf_op jit(solution)/shard_map/prepare/pallas_call | solution.py:273
  10.2 3.5 %collective-permute-done.refs_3_.refs_4_ = f32[256,384]{1,0:T(8,128)S(1)} collective-permute-done((f32[256,384]{1,0:T(8,128)}, f32[256,384]{1,0:T(8,128)S(1)}, u32[]{:S(2)}, u32[]{:S(2)}) %collective-permute-start) | collective-permute-done | bytes 393248 | tf_op jit(solution)/shard_map/ppermute | solution.py:1034
  13.7 1.7 collective-permute-done.2.refs_4_.refs_5_
  15.5 25.5 %forward.1 = (bf16[8,1024,256]{2,1,0:T(8,128)(2,1)}, bf16[8,1024,256]{2,1,0:T(8,128)(2,1)}, f32[8,384,256]{2,1,0:T(8,128)}, f32[8,1,256]{2,1,0:T(1,128)}, f32[38...) custom-call(s32[1]{0:T(128)} %bitcast.refs_0_.place_ref, ...), custom_call_target="tpu_custom_call" | custom-call | flops 12306087936 | bytes 25165824 | tf_op jit(solution)/shard_map/forward/pallas_call | solution.py:436
  41.1 1.8 collective-permute-start.4
  42.9 3.1 %class_stage.1 = (f32[384,768]{1,0:T(8,128)S(1)}, f32[384,1536]{1,0:T(8,128)S(1)}, f32[384,1536]{1,0:T(8,128)S(1)}, f32[384,768]{1,0:T(8,128)S(1)}) custom-call(s32[1]{0:T(128)} %bitcast.refs_0_.place_ref, f32[2,3,384,1536]{3,2,1,0:T(8,128)} %w_ref.1), custom_call_target="tpu_custom_call" | custom-call | flops 1 | bytes 1 | tf_op jit(solution)/shard_map/class_stage/pallas_call | solution.py:483
  47.2 15.7 %middle.1 = (f32[4,384]{1,0:T(4,128)}, f32[256,384]{1,0:T(8,128)}, f32[256,384]{1,0:T(8,128)}, f32[384,1792]{1,0:T(8,128)}, f32[384,1792]{1,0:T(8,128)}, /*index...) custom-call(s32[1]{0:T(128)} %bitcast.refs_0_.place_ref, f32[32,512]{1,0:T(8,128)S(1)} %copy-done.4, ...), custom_call_target="tpu_custom_call" | custom-call | flops 8589934592 | bytes 29360128 | tf_op jit(solution)/shard_map/middle/pallas_call | solution.py:634
  65.0 3.1 %collective-permute-done.7.refs_1_ = f32[32,384]{1,0:T(8,128)S(1)} collective-permute-done((f32[32,384]{1,0:T(8,128)}, f32[32,384]{1,0:T(8,128)S(1)}, u32[]{:S(2)}, u32[]{:S(2)}) %collective-permute-start.7) | collective-permute-done | bytes 49184 | tf_op jit(solution)/shard_map/ppermute | solution.py:1034
  68.8 2.2 %class_finish.1 = (f32[4,384]{1,0:T(4,128)}, f32[136,384]{1,0:T(8,128)S(1)}) custom-call(f32[32,384]{1,0:T(8,128)} %get-tuple-element.196.refs_0_, f32[32,384]{1,0:T(8,128)S(1)} %collective-permute-done.7.refs_1_, f32[32,384]{1,0:T(8,128)S(1)} %collective-permute-done.8.refs_2_, f32[32,384]{1,0:T(8,128)S(1)} %collective-permute-done.9.refs_3_, ...), custom_call_target="tpu_custom_call" | custom-call | flops 1 | bytes 1 | tf_op jit(solution)/shard_map/class_finish/pallas_call | solution.py:678
  71.1 2.4 %add_bitcast_fusion = (f32[2,48,1792]{2,1,0:T(8,128)S(1)}, f32[2,48,1792]{2,1,0:T(8,128)S(1)}, f32[2,48,1792]{2,1,0:T(8,128)S(1)}) fusion(f32[2,2,2,48,1792]{4,3,2,1,0:T(8,128)} %bitcast.4, u32[]{:T(128)S(6)} %convert_element_type.33, u32[]{:T(128)S(6)} %convert_element_type.31, f32[2,2,2,48,1792]{4,3,2,1,0:T(8,128)} %bitcast.79, ...), kind=kLoop, calls=%fused_computation.4 | loop fusion | flops 516096 | bytes 6193168 | tf_op jit(solution)/shard_map/add | solution.py:1212
  77.0 2.6 %collective-permute-start.13 = (f32[1,34,384]{2,1,0:T(8,128)S(1)}, f32[1,34,384]{2,1,0:T(8,128)S(1)}, u32[]{:S(2)}, u32[]{:S(2)}) collective-permute-start(f32[1,34,384]{2,1,0:T(8,128)S(1)} %dynamic-slice_bitcast_fusion.refs_0_), channel_id=1, source_target_pairs={{0,16},{1,17},{2,18},{3,19},{4,20},{5,21},{6,22},{7,23},{8,24},{9,... | collective-permute-start | bytes 156680 | tf_op jit(solution)/shard_map/ppermute | solution.py:1087
  79.6 35.7 %backward.1 = (f32[2,256,384]{2,1,0:T(8,128)}, f32[2,256,384]{2,1,0:T(8,128)}, f32[384,640]{1,0:T(8,128)}, f32[384,640]{1,0:T(8,128)}) custom-call(s32[1]{0:T(128)} %bitcast.refs_0_.place_ref, s32[1,4]{1,0:T(1,128)S(1)} %copy-done.5, f32[256,384]{1,0:T(8,128)} %tokens_ref, f32[256,384]{1,0:T(8,128)} %copy-done.1, f32[256,384]{1,0:T(8,128)} %copy-done.2, ...), custom_call_target="tpu_custom_call" | custom-call | flops 22951231488 | bytes 25165824 | tf_op jit(solution)/shard_map/backward/pallas_call | solution.py:854
  116.9 2.3 %bitcast_add_fusion.3 = f32[48,1792]{1,0:T(8,128)} fusion(f32[2,48,1792]{2,1,0:T(8,128)} %copy-done.11, u32[]{:T(128)S(6)} %convert_element_type.35, f32[2,48,1792]{2,1,0:T(8,128)} %copy-done.10, f32[2,48,1792]{2,1,0:T(8,128)} %copy-done.9, f32[2,2,2,48,1792]{4,3,2,1,0:T(8,128)} %bitcast.4, u32[]{:T(128)S(6)} %optimization_barrier.259, ...), kind=kLoop, calls=%fused_computation.15 | loop fusion | flops 344064 | bytes 2064400 | tf_op jit(solution)/shard_map/add | solution.py:1212
  128.4 3.4 %collective-permute-done.17.refs_2_ = f32[2,34,384]{2,1,0:T(8,128)S(1)} collective-permute-done((f32[2,34,384]{2,1,0:T(8,128)S(1)}, f32[2,34,384]{2,1,0:T(8,128)S(1)}, u32[]{:S(2)}, u32[]{:S(2)}) %collective-permute-start.17) | collective-permute-done | bytes 104480 | tf_op jit(solution)/shard_map/ppermute | solution.py:1087
  136.9 9.0 %collective-permute-done.21 = f32[2,48,640]{2,1,0:T(8,128)} collective-permute-done((f32[2,48,640]{2,1,0:T(8,128)}, f32[2,48,640]{2,1,0:T(8,128)}, u32[]{:S(2)}, u32[]{:S(2)}) %collective-permute-start.21) | collective-permute-done | bytes 245792 | tf_op jit(solution)/shard_map/ppermute | solution.py:1087
  145.9 2.7 %collective-permute-done.22 = f32[2,48,640]{2,1,0:T(8,128)} collective-permute-done((f32[2,48,640]{2,1,0:T(8,128)}, f32[2,48,640]{2,1,0:T(8,128)}, u32[]{:S(2)}, u32[]{:S(2)}) %collective-permute-start.22) | collective-permute-done | bytes 245792 | tf_op jit(solution)/shard_map/ppermute | solution.py:1087
  154.3 3.7 %stage.1 = (f32[2,3,48,1536]{3,2,1,0:T(8,128)S(1)}, f32[2,3,48,1536]{3,2,1,0:T(8,128)S(1)}, f32[2,3,48,1536]{3,2,1,0:T(8,128)S(1)}, f32[2,3,48,1536]{3,2,1,0:T(8,128)S(1)}) custom-call(s32[2]{0:T(128)S(1)} %pad_add_fusion.place_ref.refs_0_, f32[2,3,384,1536]{3,2,1,0:T(8,128)} %w_ref.1, f32[2,3,48,1536]{3,2,1,0:T(8,128)} %m1_ref.1, ...), custom_call_target="tpu_custom_call" | custom-call | flops 1 | bytes 1 | tf_op jit(solution)/shard_map/stage/pallas_call | solution.py:948
  158.0 3.0 %collective-permute-done.25 = f32[48,640]{1,0:T(8,128)S(1)} collective-permute-done((f32[48,640]{1,0:T(8,128)S(1)}, f32[48,640]{1,0:T(8,128)S(1)}, u32[]{:S(2)}, u32[]{:S(2)}) %collective-permute-start.25) | collective-permute-done | bytes 122912 | tf_op jit(solution)/shard_map/ppermute | solution.py:1087
  164.4 2.7 %collective-permute-done.27.refs_6_ = f32[48,640]{1,0:T(8,128)S(1)} collective-permute-done((f32[48,640]{1,0:T(8,128)S(1)}, f32[48,640]{1,0:T(8,128)S(1)}, u32[]{:S(2)}, u32[]{:S(2)}) %collective-permute-start.27) | collective-permute-done | bytes 122912 | tf_op jit(solution)/shard_map/ppermute | solution.py:1087
  172.0 2.1 %collective-permute-start.33 = (f32[8,128]{1,0:T(8,128)S(1)}, f32[8,128]{1,0:T(8,128)S(1)}, u32[]{:S(2)}, u32[]{:S(2)}) collective-permute-start(f32[8,128]{1,0:T(8,128)S(1)} %add_add_fusion.1), channel_id=1, source_target_pairs={{0,16},{1,17},{2,18},{3,19},{4,20},{5,21},{6,22},{7,23},{8,24},{9,... | collective-permute-start | bytes 12296 | tf_op jit(solution)/shard_map/ppermute | solution.py:1087
  174.2 2.2 %collective-permute-start.34 = (f32[8,128]{1,0:T(8,128)S(1)}, f32[8,128]{1,0:T(8,128)S(1)}, u32[]{:S(2)}, u32[]{:S(2)}) collective-permute-start(f32[8,128]{1,0:T(8,128)S(1)} %add_add_fusion.1), channel_id=1, source_target_pairs={{0,24},{1,25},{2,26},{3,27},{4,28},{5,29},{6,30},{7,31},{8,16},{9,... | collective-permute-start | bytes 12296 | tf_op jit(solution)/shard_map/ppermute | solution.py:1087
  176.4 2.2 %token_grad.1 = f32[256,384]{1,0:T(8,128)} custom-call(f32[256,384]{1,0:T(8,128)} %tokens_ref, f32[28,384]{1,0:T(8,128)} %refs_12_.3, f32[256,384]{1,0:T(8,128)S(1)} %get-tuple-element.312.own_ref, f32[256,384]{1,0:T(8,128)S(1)} %get-tuple-element.313.near_ref, f32[256,384]{1,0:T(8,128)S(1)} %collective-permute-done.24.far_ref, ...), custom_call_target="tpu_custom_call" | custom-call | flops 2097152 | bytes 2097152 | tf_op jit(solution)/shard_map/token_grad/pallas_call | solution.py:885
  179.6 6.0 %optimizer.1 = (f32[1,1]{1,0:T(1,128)}, f32[2,3,48,1536]{3,2,1,0:T(8,128)}, f32[2,3,48,1536]{3,2,1,0:T(8,128)}, f32[2,3,48,1536]{3,2,1,0:T(8,128)}, f32[2,3,48,1...) custom-call(s32[2]{0:T(128)S(1)} %pad_add_fusion.place_ref.refs_0_, ...), custom_call_target="tpu_custom_call" | custom-call | flops 8388608 | bytes 14680064 | tf_op jit(solution)/shard_map/optimizer/pallas_call | solution.py:1020
  (104 shorter events, 39.2 us)
Async XLA Ops:
  1.2 12.5 %collective-permute-start = (f32[256,384]{1,0:T(8,128)}, f32[256,384]{1,0:T(8,128)S(1)}, u32[]{:S(2)}, u32[]{:S(2)}) collective-permute-start(f32[256,384]{1,0:T(8,128)} %tokens_ref), channel_id=1, source_target_pairs={{0,2},{1,3},{2,0},{3,1},{4,6},{5,7},{6,4},{7,5},{8,10},{9,11},{10,... | collective-permute-start | bytes 1179656 | tf_op jit(solution)/shard_map/ppermute | solution.py:1034
  41.0 5.0 %collective-permute-start.3 = (f32[32,512]{1,0:T(8,128)}, f32[32,512]{1,0:T(8,128)S(1)}, u32[]{:S(2)}, u32[]{:S(2)}) collective-permute-start(f32[32,512]{1,0:T(8,128)} %get-tuple-element.175.refs_1_), channel_id=1, source_target_pairs={{0,1},{1,0},{2,3},{3,2},{4,5},{5,4},{6,7},{7,6},{8,9},{9,8},{10,11... | collective-permute-start | bytes 196616 | tf_op jit(solution)/shard_map/ppermute | solution.py:1034
  62.9 8.1 %collective-permute-start.6 = (f32[384,1792]{1,0:T(8,128)}, f32[384,1792]{1,0:T(8,128)}, u32[]{:S(2)}, u32[]{:S(2)}) collective-permute-start(f32[384,1792]{1,0:T(8,128)} %get-tuple-element.195), channel_id=1, source_target_pairs={{0,1},{1,0},{2,3},{3,2},{4,5},{5,4},{6,7},{7,6},{8,9},{9,8},{10,11... | collective-permute-start | bytes 8257544 | tf_op jit(solution)/shard_map/ppermute | solution.py:1087
  63.1 5.0 %collective-permute-start.7 = (f32[32,384]{1,0:T(8,128)}, f32[32,384]{1,0:T(8,128)S(1)}, u32[]{:S(2)}, u32[]{:S(2)}) collective-permute-start(f32[32,384]{1,0:T(8,128)} %get-tuple-element.196.refs_0_), channel_id=1, source_target_pairs={{0,1},{1,0},{2,3},{3,2},{4,5},{5,4},{6,7},{7,6},{8,9},{9,8},{10,11... | collective-permute-start | bytes 147464 | tf_op jit(solution)/shard_map/ppermute | solution.py:1034
  73.5 41.9 %collective-permute-start.10 = (f32[2,48,1792]{2,1,0:T(8,128)S(1)}, f32[2,48,1792]{2,1,0:T(8,128)S(1)}, u32[]{:S(2)}, u32[]{:S(2)}) collective-permute-start(f32[2,48,1792]{2,1,0:T(8,128)S(1)} %get-tuple-element.222), channel_id=1, source_target_pairs={{0,4},{1,5},{2,6},{3,7},{4,0},{5,1},{6,2},{7,3},{8,12},{9,13},{10,... | collective-permute-start | bytes 2064392 | tf_op jit(solution)/shard_map/ppermute | solution.py:1087
  75.0 40.3 %collective-permute-start.11 = (f32[2,48,1792]{2,1,0:T(8,128)S(1)}, f32[2,48,1792]{2,1,0:T(8,128)S(1)}, u32[]{:S(2)}, u32[]{:S(2)}) collective-permute-start(f32[2,48,1792]{2,1,0:T(8,128)S(1)} %get-tuple-element.223), channel_id=1, source_target_pairs={{0,8},{1,9},{2,10},{3,11},{4,12},{5,13},{6,14},{7,15},{8,0},{9,1},... | collective-permute-start | bytes 2064392 | tf_op jit(solution)/shard_map/ppermute | solution.py:1087
  76.6 38.8 %collective-permute-start.12 = (f32[2,48,1792]{2,1,0:T(8,128)S(1)}, f32[2,48,1792]{2,1,0:T(8,128)S(1)}, u32[]{:S(2)}, u32[]{:S(2)}) collective-permute-start(f32[2,48,1792]{2,1,0:T(8,128)S(1)} %get-tuple-element.224), channel_id=1, source_target_pairs={{0,12},{1,13},{2,14},{3,15},{4,8},{5,9},{6,10},{7,11},{8,4},{9,5},... | collective-permute-start | bytes 2064392 | tf_op jit(solution)/shard_map/ppermute | solution.py:1087
  77.0 38.3 %collective-permute-start.13 = (f32[1,34,384]{2,1,0:T(8,128)S(1)}, f32[1,34,384]{2,1,0:T(8,128)S(1)}, u32[]{:S(2)}, u32[]{:S(2)}) collective-permute-start(f32[1,34,384]{2,1,0:T(8,128)S(1)} %dynamic-slice_bitcast_fusion.refs_0_), channel_id=1, source_target_pairs={{0,16},{1,17},{2,18},{3,19},{4,20},{5,21},{6,22},{7,23},{8,24},{9,... | collective-permute-start | bytes 156680 | tf_op jit(solution)/shard_map/ppermute | solution.py:1087
  120.5 28.1 %collective-permute-start.24 = (f32[256,384]{1,0:T(8,128)S(1)}, f32[256,384]{1,0:T(8,128)S(1)}, u32[]{:S(2)}, u32[]{:S(2)}) collective-permute-start(f32[256,384]{1,0:T(8,128)S(1)} %get-tuple-element.311), channel_id=1, source_target_pairs={{0,2},{1,3},{2,0},{3,1},{4,6},{5,7},{6,4},{7,5},{8,10},{9,11},{10,... | collective-permute-start | bytes 1179656 | tf_op jit(solution)/shard_map/ppermute | solution.py:1034
  121.5 5.2 %collective-permute-start.16 = (f32[2,34,384]{2,1,0:T(8,128)S(1)}, f32[2,34,384]{2,1,0:T(8,128)S(1)}, u32[]{:S(2)}, u32[]{:S(2)}) collective-permute-start(f32[2,34,384]{2,1,0:T(8,128)S(1)} %join.2.refs_0_), channel_id=1, source_target_pairs={{0,4},{1,5},{2,6},{3,7},{4,0},{5,1},{6,2},{7,3},{8,12},{9,13},{10,... | collective-permute-start | bytes 313352 | tf_op jit(solution)/shard_map/ppermute | solution.py:1087
  123.1 8.7 %collective-permute-start.17 = (f32[2,34,384]{2,1,0:T(8,128)S(1)}, f32[2,34,384]{2,1,0:T(8,128)S(1)}, u32[]{:S(2)}, u32[]{:S(2)}) collective-permute-start(f32[2,34,384]{2,1,0:T(8,128)S(1)} %join.2.refs_0_), channel_id=1, source_target_pairs={{0,8},{1,9},{2,10},{3,11},{4,12},{5,13},{6,14},{7,15},{8,0},{9,1},... | collective-permute-start | bytes 313352 | tf_op jit(solution)/shard_map/ppermute | solution.py:1087
  124.7 8.4 %collective-permute-start.18 = (f32[2,34,384]{2,1,0:T(8,128)S(1)}, f32[2,34,384]{2,1,0:T(8,128)S(1)}, u32[]{:S(2)}, u32[]{:S(2)}) collective-permute-start(f32[2,34,384]{2,1,0:T(8,128)S(1)} %join.2.refs_0_), channel_id=1, source_target_pairs={{0,12},{1,13},{2,14},{3,15},{4,8},{5,9},{6,10},{7,11},{8,4},{9,5},... | collective-permute-start | bytes 313352 | tf_op jit(solution)/shard_map/ppermute | solution.py:1087
  125.1 23.5 %collective-permute-start.23 = (f32[48,1792]{1,0:T(8,128)}, f32[48,1792]{1,0:T(8,128)}, u32[]{:S(2)}, u32[]{:S(2)}) collective-permute-start(f32[48,1792]{1,0:T(8,128)} %bitcast_add_fusion.3), channel_id=1, source_target_pairs={{0,16},{1,17},{2,18},{3,19},{4,20},{5,21},{6,22},{7,23},{8,24},{9,... | collective-permute-start | bytes 1032200 | tf_op jit(solution)/shard_map/ppermute | solution.py:1087
  126.8 9.1 %collective-permute-start.20 = (f32[2,48,640]{2,1,0:T(8,128)}, f32[2,48,640]{2,1,0:T(8,128)S(1)}, u32[]{:S(2)}, u32[]{:S(2)}) collective-permute-start(f32[2,48,640]{2,1,0:T(8,128)} %get-tuple-element.241), channel_id=1, source_target_pairs={{0,4},{1,5},{2,6},{3,7},{4,0},{5,1},{6,2},{7,3},{8,12},{9,13},{10,... | collective-permute-start | bytes 737288 | tf_op jit(solution)/shard_map/ppermute | solution.py:1087
  131.8 14.1 %collective-permute-start.21 = (f32[2,48,640]{2,1,0:T(8,128)}, f32[2,48,640]{2,1,0:T(8,128)}, u32[]{:S(2)}, u32[]{:S(2)}) collective-permute-start(f32[2,48,640]{2,1,0:T(8,128)} %get-tuple-element.242), channel_id=1, source_target_pairs={{0,8},{1,9},{2,10},{3,11},{4,12},{5,13},{6,14},{7,15},{8,0},{9,1},... | collective-permute-start | bytes 737288 | tf_op jit(solution)/shard_map/ppermute | solution.py:1087
  133.1 15.5 %collective-permute-start.22 = (f32[2,48,640]{2,1,0:T(8,128)}, f32[2,48,640]{2,1,0:T(8,128)}, u32[]{:S(2)}, u32[]{:S(2)}) collective-permute-start(f32[2,48,640]{2,1,0:T(8,128)} %get-tuple-element.243), channel_id=1, source_target_pairs={{0,12},{1,13},{2,14},{3,15},{4,8},{5,9},{6,10},{7,11},{8,4},{9,5},... | collective-permute-start | bytes 737288 | tf_op jit(solution)/shard_map/ppermute | solution.py:1087
  135.8 15.4 %collective-permute-start.19 = (f32[8,34,384]{2,1,0:T(8,128)S(1)}, f32[8,34,384]{2,1,0:T(8,128)S(1)}, u32[]{:S(2)}, u32[]{:S(2)}) collective-permute-start(f32[8,34,384]{2,1,0:T(8,128)S(1)} %join.3), channel_id=1, source_target_pairs={{0,2},{1,3},{2,0},{3,1},{4,6},{5,7},{6,4},{7,5},{8,10},{9,11},{10,... | collective-permute-start | bytes 1253384 | tf_op jit(solution)/shard_map/ppermute | solution.py:1087
  151.8 9.3 %collective-permute-start.25 = (f32[48,640]{1,0:T(8,128)S(1)}, f32[48,640]{1,0:T(8,128)S(1)}, u32[]{:S(2)}, u32[]{:S(2)}) collective-permute-start(f32[48,640]{1,0:T(8,128)S(1)} %bitcast_add_fusion.9), channel_id=1, source_target_pairs={{0,16},{1,17},{2,18},{3,19},{4,20},{5,21},{6,22},{7,23},{8,24},{9,... | collective-permute-start | bytes 368648 | tf_op jit(solution)/shard_map/ppermute | solution.py:1087
  152.1 12.3 %collective-permute-start.28 = (f32[48,1792]{1,0:T(8,128)S(1)}, f32[48,1792]{1,0:T(8,128)S(1)}, u32[]{:S(2)}, u32[]{:S(2)}) collective-permute-start(f32[48,1792]{1,0:T(8,128)S(1)} %fusion.1.refs_3_), channel_id=1, source_target_pairs={{0,2},{1,3},{2,0},{3,1},{4,6},{5,7},{6,4},{7,5},{8,10},{9,11},{10,... | collective-permute-start | bytes 1032200 | tf_op jit(solution)/shard_map/ppermute | solution.py:1087
  162.1 5.0 %collective-permute-start.27 = (f32[48,640]{1,0:T(8,128)S(1)}, f32[48,640]{1,0:T(8,128)S(1)}, u32[]{:S(2)}, u32[]{:S(2)}) collective-permute-start(f32[48,640]{1,0:T(8,128)S(1)} %fusion.2.refs_5_), channel_id=1, source_target_pairs={{0,2},{1,3},{2,0},{3,1},{4,6},{5,7},{6,4},{7,5},{8,10},{9,11},{10,... | collective-permute-start | bytes 368648 | tf_op jit(solution)/shard_map/ppermute | solution.py:1087
  169.3 10.3 %collective-permute-start.35 = (f32[48,1792]{1,0:T(8,128)S(1)}, f32[48,1792]{1,0:T(8,128)S(1)}, u32[]{:S(2)}, u32[]{:S(2)}) collective-permute-start(f32[48,1792]{1,0:T(8,128)S(1)} %get-tuple-element.281.refs_2_), channel_id=1, source_target_pairs={{0,1},{1,0},{2,3},{3,2},{4,5},{5,4},{6,7},{7,6},{8,9},{9,8},{10,11... | collective-permute-start | bytes 1032200 | tf_op jit(solution)/shard_map/ppermute | solution.py:1087
  172.0 6.6 %collective-permute-start.32 = (f32[8,128]{1,0:T(8,128)S(1)}, f32[8,128]{1,0:T(8,128)S(1)}, u32[]{:S(2)}, u32[]{:S(2)}) collective-permute-start(f32[8,128]{1,0:T(8,128)S(1)} %add_add_fusion.1), channel_id=1, source_target_pairs={{0,8},{1,9},{2,10},{3,11},{4,12},{5,13},{6,14},{7,15},{8,0},{9,1},... | collective-permute-start | bytes 12296 | tf_op jit(solution)/shard_map/ppermute | solution.py:1087
  172.0 6.6 %collective-permute-start.33 = (f32[8,128]{1,0:T(8,128)S(1)}, f32[8,128]{1,0:T(8,128)S(1)}, u32[]{:S(2)}, u32[]{:S(2)}) collective-permute-start(f32[8,128]{1,0:T(8,128)S(1)} %add_add_fusion.1), channel_id=1, source_target_pairs={{0,16},{1,17},{2,18},{3,19},{4,20},{5,21},{6,22},{7,23},{8,24},{9,... | collective-permute-start | bytes 12296 | tf_op jit(solution)/shard_map/ppermute | solution.py:1087
  174.2 5.4 %collective-permute-start.34 = (f32[8,128]{1,0:T(8,128)S(1)}, f32[8,128]{1,0:T(8,128)S(1)}, u32[]{:S(2)}, u32[]{:S(2)}) collective-permute-start(f32[8,128]{1,0:T(8,128)S(1)} %add_add_fusion.1), channel_id=1, source_target_pairs={{0,24},{1,25},{2,26},{3,27},{4,28},{5,29},{6,30},{7,31},{8,16},{9,... | collective-permute-start | bytes 12296 | tf_op jit(solution)/shard_map/ppermute | solution.py:1087
  (25 other events, 150.6 us)

commit v5 on v4

--- a/solution.py
+++ b/solution.py
@@ -1326,7 +1326,7 @@
     last = [[term.reshape(row_share, -1) for term in stream.terms] for stream in (early, late)]
     squares, early, late = squares_of(dp_size, place, added, class_squares, *last)
     far, squares = together(far, squares)
-    for group in pairs([core] + dp):
+    for group in pairs(dp + [core]):
         squares = sum_of([squares] + [places.swap(squares, steps) for steps in subsets(group)])
     grad_tokens = token_grad(tokens, vectors, own[0], near, far, d_mixed)
     grads = []

time: 189 us -> 189 us (level)
  transfers between devices with their start and end apart: 37 -> 37, of which waited for: 17 -> 18; matrix products, arithmetic and copies ran while one was open for 4% -> 4% of each run, Pallas kernels for 29% -> 29%
where the time goes in v5:
time: 189 us; the launch traced here: 186 us
  Pallas kernels  102 us (54%)
  waiting for transfers between devices  39.2 us (21%)
  starting transfers between devices  31.7 us (17%)
  other arithmetic  10 us (5%)
    pallas_call x1, Pallas kernels, backward(): pl.pallas_call(functools.partial(backward_kernel, slots, lengths.shape[1]...  35.7 us
    ppermute x27, waiting for transfers between devices, swap(): lax.ppermute(value, ('dp', 'seq'), [(place, place ^ flip) for place in ra...  29 us
    pallas_call x1, Pallas kernels, forward(): pl.pallas_call(functools.partial(forward_kernel, slots, lengths.shape[1],...  25.5 us
    ppermute x27, starting transfers between devices, swap(): lax.ppermute(value, ('dp', 'seq'), [(place, place ^ flip) for place in ra...  23.8 us
    pallas_call x1, Pallas kernels, middle(): pl.pallas_call(functools.partial(middle_kernel, images, len(parts)), in_s...  15.7 us
    ppermute x10, waiting for transfers between devices, swap(): lax.ppermute(value, axis, [(place, place ^ bit) for place in range(size)])  10.3 us
    add x8, other arithmetic, sum_of(): total = total + term  9.36 us
    ppermute x10, starting transfers between devices, swap(): lax.ppermute(value, axis, [(place, place ^ bit) for place in range(size)])  7.95 us
  transfers between devices with their start and end apart: 37, of which 18 were waited for; matrix products, arithmetic and copies ran while one was open for 4% of the time, Pallas kernels for 29%

profile of v5, /device:TPU:0, one launch (start us, length us, event | category | flops | bytes accessed | tf_op | source)
XLA Modules:
  0.0 185.8 jit_solution(17750395324434179324)
XLA Ops:
  1.2 2.6 %collective-permute-start = (f32[256,384]{1,0:T(8,128)}, f32[256,384]{1,0:T(8,128)S(1)}, u32[]{:S(2)}, u32[]{:S(2)}) collective-permute-start(f32[256,384]{1,0:T(8,128)} %tokens_ref), channel_id=1, source_target_pairs={{0,2},{1,3},{2,0},{3,1},{4,6},{5,7},{6,4},{7,5},{8,10},{9,11},{10,... | collective-permute-start | bytes 1179656 | tf_op jit(solution)/shard_map/ppermute | solution.py:1034
  3.8 6.4 %prepare.1 = (f32[4,384]{1,0:T(4,128)}, f32[4,384]{1,0:T(4,128)}, f32[4,384]{1,0:T(4,128)}, f32[32,384]{1,0:T(8,128)}, f32[32,128]{1,0:T(8,128)}, /*index=5*/f32...) custom-call(f32[256,384]{1,0:T(8,128)} %tokens_ref, ...), custom_call_target="tpu_custom_call" | custom-call | flops 4294967296 | bytes 8388608 | tf_op jit(solution)/shard_map/prepare/pallas_call | solution.py:273
  10.2 3.5 %collective-permute-done.refs_3_.refs_4_ = f32[256,384]{1,0:T(8,128)S(1)} collective-permute-done((f32[256,384]{1,0:T(8,128)}, f32[256,384]{1,0:T(8,128)S(1)}, u32[]{:S(2)}, u32[]{:S(2)}) %collective-permute-start) | collective-permute-done | bytes 393248 | tf_op jit(solution)/shard_map/ppermute | solution.py:1034
  13.7 1.7 collective-permute-done.2.refs_4_.refs_5_
  15.5 25.5 %forward.1 = (bf16[8,1024,256]{2,1,0:T(8,128)(2,1)}, bf16[8,1024,256]{2,1,0:T(8,128)(2,1)}, f32[8,384,256]{2,1,0:T(8,128)}, f32[8,1,256]{2,1,0:T(1,128)}, f32[38...) custom-call(s32[1]{0:T(128)} %bitcast.refs_0_.place_ref, ...), custom_call_target="tpu_custom_call" | custom-call | flops 12306087936 | bytes 25165824 | tf_op jit(solution)/shard_map/forward/pallas_call | solution.py:436
  41.1 1.8 collective-permute-start.4
  42.9 3.1 %class_stage.1 = (f32[384,768]{1,0:T(8,128)S(1)}, f32[384,1536]{1,0:T(8,128)S(1)}, f32[384,1536]{1,0:T(8,128)S(1)}, f32[384,768]{1,0:T(8,128)S(1)}) custom-call(s32[1]{0:T(128)} %bitcast.refs_0_.place_ref, f32[2,3,384,1536]{3,2,1,0:T(8,128)} %w_ref.1), custom_call_target="tpu_custom_call" | custom-call | flops 1 | bytes 1 | tf_op jit(solution)/shard_map/class_stage/pallas_call | solution.py:483
  47.2 15.7 %middle.1 = (f32[4,384]{1,0:T(4,128)}, f32[256,384]{1,0:T(8,128)}, f32[256,384]{1,0:T(8,128)}, f32[384,1792]{1,0:T(8,128)}, f32[384,1792]{1,0:T(8,128)}, /*index...) custom-call(s32[1]{0:T(128)} %bitcast.refs_0_.place_ref, f32[32,512]{1,0:T(8,128)S(1)} %copy-done.4, ...), custom_call_target="tpu_custom_call" | custom-call | flops 8589934592 | bytes 29360128 | tf_op jit(solution)/shard_map/middle/pallas_call | solution.py:634
  65.0 3.1 %collective-permute-done.7.refs_1_ = f32[32,384]{1,0:T(8,128)S(1)} collective-permute-done((f32[32,384]{1,0:T(8,128)}, f32[32,384]{1,0:T(8,128)S(1)}, u32[]{:S(2)}, u32[]{:S(2)}) %collective-permute-start.7) | collective-permute-done | bytes 49184 | tf_op jit(solution)/shard_map/ppermute | solution.py:1034
  68.8 2.2 %class_finish.1 = (f32[4,384]{1,0:T(4,128)}, f32[136,384]{1,0:T(8,128)S(1)}) custom-call(f32[32,384]{1,0:T(8,128)} %get-tuple-element.196.refs_0_, f32[32,384]{1,0:T(8,128)S(1)} %collective-permute-done.7.refs_1_, f32[32,384]{1,0:T(8,128)S(1)} %collective-permute-done.8.refs_2_, f32[32,384]{1,0:T(8,128)S(1)} %collective-permute-done.9.refs_3_, ...), custom_call_target="tpu_custom_call" | custom-call | flops 1 | bytes 1 | tf_op jit(solution)/shard_map/class_finish/pallas_call | solution.py:678
  71.1 2.4 %add_bitcast_fusion = (f32[2,48,1792]{2,1,0:T(8,128)S(1)}, f32[2,48,1792]{2,1,0:T(8,128)S(1)}, f32[2,48,1792]{2,1,0:T(8,128)S(1)}) fusion(f32[2,2,2,48,1792]{4,3,2,1,0:T(8,128)} %bitcast.4, u32[]{:T(128)S(6)} %convert_element_type.33, u32[]{:T(128)S(6)} %convert_element_type.31, f32[2,2,2,48,1792]{4,3,2,1,0:T(8,128)} %bitcast.79, ...), kind=kLoop, calls=%fused_computation.4 | loop fusion | flops 516096 | bytes 6193168 | tf_op jit(solution)/shard_map/add | solution.py:1212
  77.0 2.6 %collective-permute-start.13 = (f32[1,34,384]{2,1,0:T(8,128)S(1)}, f32[1,34,384]{2,1,0:T(8,128)S(1)}, u32[]{:S(2)}, u32[]{:S(2)}) collective-permute-start(f32[1,34,384]{2,1,0:T(8,128)S(1)} %dynamic-slice_bitcast_fusion.refs_0_), channel_id=1, source_target_pairs={{0,16},{1,17},{2,18},{3,19},{4,20},{5,21},{6,22},{7,23},{8,24},{9,... | collective-permute-start | bytes 156680 | tf_op jit(solution)/shard_map/ppermute | solution.py:1087
  79.6 35.7 %backward.1 = (f32[2,256,384]{2,1,0:T(8,128)}, f32[2,256,384]{2,1,0:T(8,128)}, f32[384,640]{1,0:T(8,128)}, f32[384,640]{1,0:T(8,128)}) custom-call(s32[1]{0:T(128)} %bitcast.refs_0_.place_ref, s32[1,4]{1,0:T(1,128)S(1)} %copy-done.5, f32[256,384]{1,0:T(8,128)} %tokens_ref, f32[256,384]{1,0:T(8,128)} %copy-done.1, f32[256,384]{1,0:T(8,128)} %copy-done.2, ...), custom_call_target="tpu_custom_call" | custom-call | flops 22951231488 | bytes 25165824 | tf_op jit(solution)/shard_map/backward/pallas_call | solution.py:854
  116.9 2.3 %bitcast_add_fusion.3 = f32[48,1792]{1,0:T(8,128)} fusion(f32[2,48,1792]{2,1,0:T(8,128)} %copy-done.11, u32[]{:T(128)S(6)} %convert_element_type.35, f32[2,48,1792]{2,1,0:T(8,128)} %copy-done.10, f32[2,48,1792]{2,1,0:T(8,128)} %copy-done.9, f32[2,2,2,48,1792]{4,3,2,1,0:T(8,128)} %bitcast.4, u32[]{:T(128)S(6)} %optimization_barrier.259, ...), kind=kLoop, calls=%fused_computation.15 | loop fusion | flops 344064 | bytes 2064400 | tf_op jit(solution)/shard_map/add | solution.py:1212
  128.4 3.4 %collective-permute-done.17.refs_2_ = f32[2,34,384]{2,1,0:T(8,128)S(1)} collective-permute-done((f32[2,34,384]{2,1,0:T(8,128)S(1)}, f32[2,34,384]{2,1,0:T(8,128)S(1)}, u32[]{:S(2)}, u32[]{:S(2)}) %collective-permute-start.17) | collective-permute-done | bytes 104480 | tf_op jit(solution)/shard_map/ppermute | solution.py:1087
  136.9 9.0 %collective-permute-done.21 = f32[2,48,640]{2,1,0:T(8,128)} collective-permute-done((f32[2,48,640]{2,1,0:T(8,128)}, f32[2,48,640]{2,1,0:T(8,128)}, u32[]{:S(2)}, u32[]{:S(2)}) %collective-permute-start.21) | collective-permute-done | bytes 245792 | tf_op jit(solution)/shard_map/ppermute | solution.py:1087
  145.9 2.7 %collective-permute-done.22 = f32[2,48,640]{2,1,0:T(8,128)} collective-permute-done((f32[2,48,640]{2,1,0:T(8,128)}, f32[2,48,640]{2,1,0:T(8,128)}, u32[]{:S(2)}, u32[]{:S(2)}) %collective-permute-start.22) | collective-permute-done | bytes 245792 | tf_op jit(solution)/shard_map/ppermute | solution.py:1087
  154.3 3.7 %stage.1 = (f32[2,3,48,1536]{3,2,1,0:T(8,128)S(1)}, f32[2,3,48,1536]{3,2,1,0:T(8,128)S(1)}, f32[2,3,48,1536]{3,2,1,0:T(8,128)S(1)}, f32[2,3,48,1536]{3,2,1,0:T(8,128)S(1)}) custom-call(s32[2]{0:T(128)S(1)} %pad_add_fusion.place_ref.refs_0_, f32[2,3,384,1536]{3,2,1,0:T(8,128)} %w_ref.1, f32[2,3,48,1536]{3,2,1,0:T(8,128)} %m1_ref.1, ...), custom_call_target="tpu_custom_call" | custom-call | flops 1 | bytes 1 | tf_op jit(solution)/shard_map/stage/pallas_call | solution.py:948
  158.0 3.0 %collective-permute-done.25 = f32[48,640]{1,0:T(8,128)S(1)} collective-permute-done((f32[48,640]{1,0:T(8,128)S(1)}, f32[48,640]{1,0:T(8,128)S(1)}, u32[]{:S(2)}, u32[]{:S(2)}) %collective-permute-start.25) | collective-permute-done | bytes 122912 | tf_op jit(solution)/shard_map/ppermute | solution.py:1087
  164.4 2.7 %collective-permute-done.27.refs_6_ = f32[48,640]{1,0:T(8,128)S(1)} collective-permute-done((f32[48,640]{1,0:T(8,128)S(1)}, f32[48,640]{1,0:T(8,128)S(1)}, u32[]{:S(2)}, u32[]{:S(2)}) %collective-permute-start.27) | collective-permute-done | bytes 122912 | tf_op jit(solution)/shard_map/ppermute | solution.py:1087
  168.9 2.0 %collective-permute-start.31 = (f32[8,128]{1,0:T(8,128)S(1)}, f32[8,128]{1,0:T(8,128)S(1)}, u32[]{:S(2)}, u32[]{:S(2)}) collective-permute-start(f32[8,128]{1,0:T(8,128)S(1)} %get-tuple-element.280), channel_id=1, source_target_pairs={{0,12},{1,13},{2,14},{3,15},{4,8},{5,9},{6,10},{7,11},{8,4},{9,5},... | collective-permute-start | bytes 12296 | tf_op jit(solution)/shard_map/ppermute | solution.py:1087
  173.4 2.1 %collective-permute-start.32 = (f32[8,128]{1,0:T(8,128)S(1)}, f32[8,128]{1,0:T(8,128)S(1)}, u32[]{:S(2)}, u32[]{:S(2)}) collective-permute-start(f32[8,128]{1,0:T(8,128)S(1)} %add_add_fusion.1), channel_id=1, source_target_pairs={{0,16},{1,17},{2,18},{3,19},{4,20},{5,21},{6,22},{7,23},{8,24},{9,... | collective-permute-start | bytes 12296 | tf_op jit(solution)/shard_map/ppermute | solution.py:1087
  176.5 2.2 %token_grad.1 = f32[256,384]{1,0:T(8,128)} custom-call(f32[256,384]{1,0:T(8,128)} %tokens_ref, f32[28,384]{1,0:T(8,128)} %refs_12_.3, f32[256,384]{1,0:T(8,128)S(1)} %get-tuple-element.312.own_ref, f32[256,384]{1,0:T(8,128)S(1)} %get-tuple-element.313.near_ref, f32[256,384]{1,0:T(8,128)S(1)} %collective-permute-done.24.far_ref, ...), custom_call_target="tpu_custom_call" | custom-call | flops 2097152 | bytes 2097152 | tf_op jit(solution)/shard_map/token_grad/pallas_call | solution.py:885
  179.5 6.0 %optimizer.1 = (f32[1,1]{1,0:T(1,128)}, f32[2,3,48,1536]{3,2,1,0:T(8,128)}, f32[2,3,48,1536]{3,2,1,0:T(8,128)}, f32[2,3,48,1536]{3,2,1,0:T(8,128)}, f32[2,3,48,1...) custom-call(s32[2]{0:T(128)S(1)} %pad_add_fusion.place_ref.refs_0_, ...), custom_call_target="tpu_custom_call" | custom-call | flops 8388608 | bytes 14680064 | tf_op jit(solution)/shard_map/optimizer/pallas_call | solution.py:1020
  (104 shorter events, 39.3 us)
Async XLA Ops:
  1.2 12.5 %collective-permute-start = (f32[256,384]{1,0:T(8,128)}, f32[256,384]{1,0:T(8,128)S(1)}, u32[]{:S(2)}, u32[]{:S(2)}) collective-permute-start(f32[256,384]{1,0:T(8,128)} %tokens_ref), channel_id=1, source_target_pairs={{0,2},{1,3},{2,0},{3,1},{4,6},{5,7},{6,4},{7,5},{8,10},{9,11},{10,... | collective-permute-start | bytes 1179656 | tf_op jit(solution)/shard_map/ppermute | solution.py:1034
  41.0 5.0 %collective-permute-start.3 = (f32[32,512]{1,0:T(8,128)}, f32[32,512]{1,0:T(8,128)S(1)}, u32[]{:S(2)}, u32[]{:S(2)}) collective-permute-start(f32[32,512]{1,0:T(8,128)} %get-tuple-element.175.refs_1_), channel_id=1, source_target_pairs={{0,1},{1,0},{2,3},{3,2},{4,5},{5,4},{6,7},{7,6},{8,9},{9,8},{10,11... | collective-permute-start | bytes 196616 | tf_op jit(solution)/shard_map/ppermute | solution.py:1034
  41.1 4.9 %collective-permute-start.4 = (f32[32,512]{1,0:T(8,128)}, f32[32,512]{1,0:T(8,128)S(1)}, u32[]{:S(2)}, u32[]{:S(2)}) collective-permute-start(f32[32,512]{1,0:T(8,128)} %get-tuple-element.175.refs_1_), channel_id=1, source_target_pairs={{0,2},{1,3},{2,0},{3,1},{4,6},{5,7},{6,4},{7,5},{8,10},{9,11},{10,... | collective-permute-start | bytes 196616 | tf_op jit(solution)/shard_map/ppermute | solution.py:1034
  62.9 8.1 %collective-permute-start.6 = (f32[384,1792]{1,0:T(8,128)}, f32[384,1792]{1,0:T(8,128)}, u32[]{:S(2)}, u32[]{:S(2)}) collective-permute-start(f32[384,1792]{1,0:T(8,128)} %get-tuple-element.195), channel_id=1, source_target_pairs={{0,1},{1,0},{2,3},{3,2},{4,5},{5,4},{6,7},{7,6},{8,9},{9,8},{10,11... | collective-permute-start | bytes 8257544 | tf_op jit(solution)/shard_map/ppermute | solution.py:1087
  63.1 5.0 %collective-permute-start.7 = (f32[32,384]{1,0:T(8,128)}, f32[32,384]{1,0:T(8,128)S(1)}, u32[]{:S(2)}, u32[]{:S(2)}) collective-permute-start(f32[32,384]{1,0:T(8,128)} %get-tuple-element.196.refs_0_), channel_id=1, source_target_pairs={{0,1},{1,0},{2,3},{3,2},{4,5},{5,4},{6,7},{7,6},{8,9},{9,8},{10,11... | collective-permute-start | bytes 147464 | tf_op jit(solution)/shard_map/ppermute | solution.py:1034
  63.5 4.6 %collective-permute-start.8 = (f32[32,384]{1,0:T(8,128)}, f32[32,384]{1,0:T(8,128)S(1)}, u32[]{:S(2)}, u32[]{:S(2)}) collective-permute-start(f32[32,384]{1,0:T(8,128)} %get-tuple-element.196.refs_0_), channel_id=1, source_target_pairs={{0,2},{1,3},{2,0},{3,1},{4,6},{5,7},{6,4},{7,5},{8,10},{9,11},{10,... | collective-permute-start | bytes 147464 | tf_op jit(solution)/shard_map/ppermute | solution.py:1034
  73.5 41.9 %collective-permute-start.10 = (f32[2,48,1792]{2,1,0:T(8,128)S(1)}, f32[2,48,1792]{2,1,0:T(8,128)S(1)}, u32[]{:S(2)}, u32[]{:S(2)}) collective-permute-start(f32[2,48,1792]{2,1,0:T(8,128)S(1)} %get-tuple-element.222), channel_id=1, source_target_pairs={{0,4},{1,5},{2,6},{3,7},{4,0},{5,1},{6,2},{7,3},{8,12},{9,13},{10,... | collective-permute-start | bytes 2064392 | tf_op jit(solution)/shard_map/ppermute | solution.py:1087
  75.0 40.3 %collective-permute-start.11 = (f32[2,48,1792]{2,1,0:T(8,128)S(1)}, f32[2,48,1792]{2,1,0:T(8,128)S(1)}, u32[]{:S(2)}, u32[]{:S(2)}) collective-permute-start(f32[2,48,1792]{2,1,0:T(8,128)S(1)} %get-tuple-element.223), channel_id=1, source_target_pairs={{0,8},{1,9},{2,10},{3,11},{4,12},{5,13},{6,14},{7,15},{8,0},{9,1},... | collective-permute-start | bytes 2064392 | tf_op jit(solution)/shard_map/ppermute | solution.py:1087
  76.6 38.8 %collective-permute-start.12 = (f32[2,48,1792]{2,1,0:T(8,128)S(1)}, f32[2,48,1792]{2,1,0:T(8,128)S(1)}, u32[]{:S(2)}, u32[]{:S(2)}) collective-permute-start(f32[2,48,1792]{2,1,0:T(8,128)S(1)} %get-tuple-element.224), channel_id=1, source_target_pairs={{0,12},{1,13},{2,14},{3,15},{4,8},{5,9},{6,10},{7,11},{8,4},{9,5},... | collective-permute-start | bytes 2064392 | tf_op jit(solution)/shard_map/ppermute | solution.py:1087
  77.0 38.3 %collective-permute-start.13 = (f32[1,34,384]{2,1,0:T(8,128)S(1)}, f32[1,34,384]{2,1,0:T(8,128)S(1)}, u32[]{:S(2)}, u32[]{:S(2)}) collective-permute-start(f32[1,34,384]{2,1,0:T(8,128)S(1)} %dynamic-slice_bitcast_fusion.refs_0_), channel_id=1, source_target_pairs={{0,16},{1,17},{2,18},{3,19},{4,20},{5,21},{6,22},{7,23},{8,24},{9,... | collective-permute-start | bytes 156680 | tf_op jit(solution)/shard_map/ppermute | solution.py:1087
  120.5 28.1 %collective-permute-start.24 = (f32[256,384]{1,0:T(8,128)S(1)}, f32[256,384]{1,0:T(8,128)S(1)}, u32[]{:S(2)}, u32[]{:S(2)}) collective-permute-start(f32[256,384]{1,0:T(8,128)S(1)} %get-tuple-element.311), channel_id=1, source_target_pairs={{0,2},{1,3},{2,0},{3,1},{4,6},{5,7},{6,4},{7,5},{8,10},{9,11},{10,... | collective-permute-start | bytes 1179656 | tf_op jit(solution)/shard_map/ppermute | solution.py:1034
  121.5 5.2 %collective-permute-start.16 = (f32[2,34,384]{2,1,0:T(8,128)S(1)}, f32[2,34,384]{2,1,0:T(8,128)S(1)}, u32[]{:S(2)}, u32[]{:S(2)}) collective-permute-start(f32[2,34,384]{2,1,0:T(8,128)S(1)} %join.2.refs_0_), channel_id=1, source_target_pairs={{0,4},{1,5},{2,6},{3,7},{4,0},{5,1},{6,2},{7,3},{8,12},{9,13},{10,... | collective-permute-start | bytes 313352 | tf_op jit(solution)/shard_map/ppermute | solution.py:1087
  123.1 8.7 %collective-permute-start.17 = (f32[2,34,384]{2,1,0:T(8,128)S(1)}, f32[2,34,384]{2,1,0:T(8,128)S(1)}, u32[]{:S(2)}, u32[]{:S(2)}) collective-permute-start(f32[2,34,384]{2,1,0:T(8,128)S(1)} %join.2.refs_0_), channel_id=1, source_target_pairs={{0,8},{1,9},{2,10},{3,11},{4,12},{5,13},{6,14},{7,15},{8,0},{9,1},... | collective-permute-start | bytes 313352 | tf_op jit(solution)/shard_map/ppermute | solution.py:1087
  124.7 8.4 %collective-permute-start.18 = (f32[2,34,384]{2,1,0:T(8,128)S(1)}, f32[2,34,384]{2,1,0:T(8,128)S(1)}, u32[]{:S(2)}, u32[]{:S(2)}) collective-permute-start(f32[2,34,384]{2,1,0:T(8,128)S(1)} %join.2.refs_0_), channel_id=1, source_target_pairs={{0,12},{1,13},{2,14},{3,15},{4,8},{5,9},{6,10},{7,11},{8,4},{9,5},... | collective-permute-start | bytes 313352 | tf_op jit(solution)/shard_map/ppermute | solution.py:1087
  125.1 23.5 %collective-permute-start.23 = (f32[48,1792]{1,0:T(8,128)}, f32[48,1792]{1,0:T(8,128)}, u32[]{:S(2)}, u32[]{:S(2)}) collective-permute-start(f32[48,1792]{1,0:T(8,128)} %bitcast_add_fusion.3), channel_id=1, source_target_pairs={{0,16},{1,17},{2,18},{3,19},{4,20},{5,21},{6,22},{7,23},{8,24},{9,... | collective-permute-start | bytes 1032200 | tf_op jit(solution)/shard_map/ppermute | solution.py:1087
  126.8 9.1 %collective-permute-start.20 = (f32[2,48,640]{2,1,0:T(8,128)}, f32[2,48,640]{2,1,0:T(8,128)S(1)}, u32[]{:S(2)}, u32[]{:S(2)}) collective-permute-start(f32[2,48,640]{2,1,0:T(8,128)} %get-tuple-element.241), channel_id=1, source_target_pairs={{0,4},{1,5},{2,6},{3,7},{4,0},{5,1},{6,2},{7,3},{8,12},{9,13},{10,... | collective-permute-start | bytes 737288 | tf_op jit(solution)/shard_map/ppermute | solution.py:1087
  131.8 14.1 %collective-permute-start.21 = (f32[2,48,640]{2,1,0:T(8,128)}, f32[2,48,640]{2,1,0:T(8,128)}, u32[]{:S(2)}, u32[]{:S(2)}) collective-permute-start(f32[2,48,640]{2,1,0:T(8,128)} %get-tuple-element.242), channel_id=1, source_target_pairs={{0,8},{1,9},{2,10},{3,11},{4,12},{5,13},{6,14},{7,15},{8,0},{9,1},... | collective-permute-start | bytes 737288 | tf_op jit(solution)/shard_map/ppermute | solution.py:1087
  133.1 15.5 %collective-permute-start.22 = (f32[2,48,640]{2,1,0:T(8,128)}, f32[2,48,640]{2,1,0:T(8,128)}, u32[]{:S(2)}, u32[]{:S(2)}) collective-permute-start(f32[2,48,640]{2,1,0:T(8,128)} %get-tuple-element.243), channel_id=1, source_target_pairs={{0,12},{1,13},{2,14},{3,15},{4,8},{5,9},{6,10},{7,11},{8,4},{9,5},... | collective-permute-start | bytes 737288 | tf_op jit(solution)/shard_map/ppermute | solution.py:1087
  135.8 15.4 %collective-permute-start.19 = (f32[8,34,384]{2,1,0:T(8,128)S(1)}, f32[8,34,384]{2,1,0:T(8,128)S(1)}, u32[]{:S(2)}, u32[]{:S(2)}) collective-permute-start(f32[8,34,384]{2,1,0:T(8,128)S(1)} %join.3), channel_id=1, source_target_pairs={{0,2},{1,3},{2,0},{3,1},{4,6},{5,7},{6,4},{7,5},{8,10},{9,11},{10,... | collective-permute-start | bytes 1253384 | tf_op jit(solution)/shard_map/ppermute | solution.py:1087
  151.8 9.3 %collective-permute-start.25 = (f32[48,640]{1,0:T(8,128)S(1)}, f32[48,640]{1,0:T(8,128)S(1)}, u32[]{:S(2)}, u32[]{:S(2)}) collective-permute-start(f32[48,640]{1,0:T(8,128)S(1)} %bitcast_add_fusion.9), channel_id=1, source_target_pairs={{0,16},{1,17},{2,18},{3,19},{4,20},{5,21},{6,22},{7,23},{8,24},{9,... | collective-permute-start | bytes 368648 | tf_op jit(solution)/shard_map/ppermute | solution.py:1087
  152.1 12.3 %collective-permute-start.28 = (f32[48,1792]{1,0:T(8,128)S(1)}, f32[48,1792]{1,0:T(8,128)S(1)}, u32[]{:S(2)}, u32[]{:S(2)}) collective-permute-start(f32[48,1792]{1,0:T(8,128)S(1)} %fusion.1.refs_3_), channel_id=1, source_target_pairs={{0,2},{1,3},{2,0},{3,1},{4,6},{5,7},{6,4},{7,5},{8,10},{9,11},{10,... | collective-permute-start | bytes 1032200 | tf_op jit(solution)/shard_map/ppermute | solution.py:1087
  162.1 5.0 %collective-permute-start.27 = (f32[48,640]{1,0:T(8,128)S(1)}, f32[48,640]{1,0:T(8,128)S(1)}, u32[]{:S(2)}, u32[]{:S(2)}) collective-permute-start(f32[48,640]{1,0:T(8,128)S(1)} %fusion.2.refs_5_), channel_id=1, source_target_pairs={{0,2},{1,3},{2,0},{3,1},{4,6},{5,7},{6,4},{7,5},{8,10},{9,11},{10,... | collective-permute-start | bytes 368648 | tf_op jit(solution)/shard_map/ppermute | solution.py:1087
  170.9 8.6 %collective-permute-start.35 = (f32[48,1792]{1,0:T(8,128)S(1)}, f32[48,1792]{1,0:T(8,128)S(1)}, u32[]{:S(2)}, u32[]{:S(2)}) collective-permute-start(f32[48,1792]{1,0:T(8,128)S(1)} %get-tuple-element.281.refs_2_), channel_id=1, source_target_pairs={{0,1},{1,0},{2,3},{3,2},{4,5},{5,4},{6,7},{7,6},{8,9},{9,8},{10,11... | collective-permute-start | bytes 1032200 | tf_op jit(solution)/shard_map/ppermute | solution.py:1087
  173.4 5.2 %collective-permute-start.32 = (f32[8,128]{1,0:T(8,128)S(1)}, f32[8,128]{1,0:T(8,128)S(1)}, u32[]{:S(2)}, u32[]{:S(2)}) collective-permute-start(f32[8,128]{1,0:T(8,128)S(1)} %add_add_fusion.1), channel_id=1, source_target_pairs={{0,16},{1,17},{2,18},{3,19},{4,20},{5,21},{6,22},{7,23},{8,24},{9,... | collective-permute-start | bytes 12296 | tf_op jit(solution)/shard_map/ppermute | solution.py:1087
  (25 other events, 150.8 us)
